TPU v7x, 256 devices: a whole 4x4x8 slice. The times are simulated.
256 devices in a mesh: attn: 8 (over z), expert: 32 (over y, x, core).
Axes of the slice: x: 4, y: 4, z: 8, core: 2. Of those that a mesh axis runs over, the one named last changes fastest.
Arguments:
- tokens: bfloat16 [512, 7168], P(('attn', 'expert')), may hold values from -6 to 6
- expert_ids: int32 [512, 8], P(('attn', 'expert')), may hold values from 0 to 31, all different within a row; in each aligned block of 64 rows (0 to 63, 64 to 127, ...) at most 24 rows name the same one
- replica: int32 [512, 8], P(('attn', 'expert')), may hold values from 0 to 1
- route_weight: float32 [512, 8], P(('attn', 'expert')), may hold values from 0.05 to 0.5
- spare_plan: int32 [32], replicated, may hold values from 0 to 31, each once
- w_in: bfloat16 [32, 2, 7168, 1024], P('expert', None, None, 'attn'), may hold values from -0.0625 to 0.0625
- w_down: bfloat16 [32, 1024, 7168], P('expert', 'attn'), may hold values from -0.1875 to 0.1875
Outputs:
- layer_output: bfloat16 [512, 7168], P(('attn', 'expert'))
- slot_load: int32 [32, 2], P('expert')
Inputs may be any that keep to these rules, and one draw needn't show every extreme that they name: `expert_ids`: each row names 8 different experts; among the rows of one index of attn no expert is named by more than 24 rows, and one is named by exactly 24. `replica`: 0 names the expert's own index of expert, 1 the index whose spare slot holds it. `spare_plan`: each expert appears once.
All inputs are finite; a program needn't handle non-finite values.
Results may differ from a plain program's by a relative error of at most 0.023.
Values may be sent and summed in bfloat16 or wider, within the bound.
No kernel may reach another device: no remote copies, remote signals or barrier semaphores. Data moves between devices by JAX's collectives and lax.ppermute only.
A program may use at most 128 MiB of HBM per device.

v0:
```python
import jax
import jax.numpy as jnp
from jax import lax
from jax.sharding import PartitionSpec as P


def body(tokens, expert_ids, replica, route_weight, spare_plan, w_in, w_down):
    row_count = tokens.shape[0]
    top_count = expert_ids.shape[1]
    groups = lax.axis_size("expert")
    my_expert = lax.axis_index("expert")
    most = min(row_count * top_count * 3 // 2, row_count * groups)
    labels = jnp.arange(groups, dtype=jnp.int32)
    named = expert_ids[..., None] == labels
    by_owner = jnp.sum(named & (replica == 0)[..., None], axis=(0, 1), dtype=jnp.int32)
    by_copy = jnp.sum(named & (replica == 1)[..., None], axis=(0, 1), dtype=jnp.int32)
    spare_match = (spare_plan[:, None] == labels[None, :]).astype(jnp.int32)
    by_spare = jnp.sum(spare_match * by_copy[None, :], 1)
    local_counts = jnp.stack([by_owner, by_spare], 1)
    totals = lax.psum(local_counts, ("attn", "expert"))
    slot_load = lax.dynamic_slice_in_dim(totals, my_expert, 1, 0)
    slot_total = 2
    host_of = jnp.sum(labels[:, None] * spare_match, 0)
    target_dev = jnp.where(replica == 0, expert_ids, jnp.take(host_of, expert_ids))
    target = replica * groups + target_dev
    spread_in, spread_down = (
        lax.all_to_all(w_in, "expert", split_axis=2, concat_axis=0, tiled=True),
        lax.all_to_all(w_down, "expert", split_axis=2, concat_axis=0, tiled=True),
    )
    picked_in = jnp.take(spread_in, spare_plan, axis=0)
    picked_down = jnp.take(spread_down, spare_plan, axis=0)
    spare_in, spare_down = (
        lax.all_to_all(picked_in, "expert", split_axis=0, concat_axis=2, tiled=True),
        lax.all_to_all(picked_down, "expert", split_axis=0, concat_axis=2, tiled=True),
    )
    in_weights = [w_in[0], spare_in[0]]
    down_weights = [w_down[0], spare_down[0]]
    slot_span = slot_total * groups
    slot_labels = jnp.arange(slot_span, dtype=jnp.int32)
    most_labels = jnp.arange(most, dtype=jnp.int32)
    slot_hits = (target[:, :, None] == slot_labels[None, None, :]).astype(jnp.float32)
    slot_coef = jnp.sum(slot_hits * route_weight[:, :, None], 1)
    group_tokens = lax.all_gather(tokens, "expert", axis=0, tiled=True)
    group_coef = lax.all_gather(slot_coef, "expert", axis=0, tiled=True)
    group_total = group_tokens.shape[0]
    own_coef = lax.dynamic_slice_in_dim(
        group_coef.reshape(group_total, slot_total, groups), my_expert, 1, 2
    )[:, :, 0]
    group_hits = (own_coef > 0.0).astype(jnp.int32)
    group_rank = jnp.cumsum(group_hits, 0) - group_hits
    compact_map = (
        (group_hits.T[:, None, :] == 1) & (group_rank.T[:, None, :] == most_labels[None, :, None])
    ).astype(jnp.bfloat16)
    packed = jnp.einsum(
        "smj,jd->msd", compact_map, group_tokens, preferred_element_type=jnp.float32
    ).astype(jnp.bfloat16)
    block_rows = lax.all_gather(packed, "attn", axis=0, tiled=True)
    results = []
    for slot_idx in range(slot_total):
        slot_rows = block_rows[:, slot_idx, :]
        gate_part = jnp.dot(slot_rows, in_weights[slot_idx][0], preferred_element_type=jnp.float32)
        up_part = jnp.dot(slot_rows, in_weights[slot_idx][1], preferred_element_type=jnp.float32)
        results.append((jax.nn.silu(gate_part) * up_part).astype(jnp.bfloat16))
    hidden = jnp.stack(results, 1)
    results = []
    for slot_idx in range(slot_total):
        results.append(
            jnp.dot(
                hidden[:, slot_idx, :], down_weights[slot_idx], preferred_element_type=jnp.float32
            )
        )
    summed = lax.psum_scatter(
        jnp.stack(results, 1).astype(jnp.bfloat16), "attn", scatter_dimension=0, tiled=True
    )
    unpacked = jnp.einsum("smj,msd->jsd", compact_map, summed, preferred_element_type=jnp.float32)
    weighted_term = jnp.sum(own_coef[:, :, None] * unpacked, 1)
    layer_output = lax.psum_scatter(
        weighted_term.astype(jnp.bfloat16), "expert", scatter_dimension=0, tiled=True
    )
    return (layer_output, slot_load)


def solution(mesh):
    placed = (
        P(("attn", "expert"), None),
        P(("attn", "expert"), None),
        P(("attn", "expert"), None),
        P(("attn", "expert"), None),
        P(),
        P("expert", None, None, "attn"),
        P("expert", "attn", None),
    )
    return jax.shard_map(
        body,
        mesh=mesh,
        in_specs=placed,
        out_specs=(P(("attn", "expert"), None), P("expert", None)),
        check_vma=False,
    )
```

profile of v0, /device:TPU:64, one launch (start us, length us, event | category | flops | bytes accessed | tf_op | source)
XLA Modules:
  0.0 445.2 jit_solution(2259124646840259376)
XLA Ops:
  7.2 0.0 all-gather.4.cloned.1.call-start
  7.2 0.7 broadcast_compare_fusion
  7.9 0.7 compare_select_fusion
  8.6 0.1 reshape.40
  8.7 0.8 convert_reduce_fusion.1
  9.4 0.8 select_reduce_fusion
  10.3 0.7 gather_fusion
  11.0 0.1 reshape.39
  11.0 0.7 fusion.48
  11.8 0.8 select_reduce_fusion.2
  12.5 24.5 %all-gather = f32[32,2,64]{2,1,0:T(2,128)S(1)} all-gather(f32[1,2,64]{2,1,0:T(2,128)S(1)} %bitcast.102), channel_id=1, replica_groups=mesh['attn'=8,'expert'=32] {'expert'}, dimensions={0}, use_global_device_ids=true | all-gather | bytes 16896 | tf_op jit(solution)/shard_map/all_gather | solution.py:44
  37.0 0.1 reshape.37
  37.1 0.1 constant_dynamic-slice_fusion.2
  37.2 0.1 copy.50
  37.3 24.3 %all-gather.1 = bf16[32,2,7168]{2,1,0:T(2,128)(2,1)S(1)} all-gather(bf16[1,2,7168]{2,1,0:T(2,128)(2,1)} %bitcast.99), channel_id=1, replica_groups=mesh['attn'=8,'expert'=32] {'expert'}, dimensions={0}, use_global_device_ids=true | all-gather | bytes 946176 | tf_op jit(solution)/shard_map/all_gather | solution.py:43
  61.6 0.3 reshape.71
  61.9 0.1 copy.51
  62.0 0.1 reduce_window_sum.11
  62.1 0.1 copy.53
  62.2 0.1 copy.52
  62.3 1.2 fusion.3
  63.5 0.0 all-gather.4.cloned.1.call-update
  63.5 9.1 %copy.54 = bf16[1,2,7168,128]{3,1,0,2:T(2,128)(2,1)} copy(bf16[1,2,7168,128]{3,2,1,0:T(8,128)(2,1)} %param.12) | data formatting | bytes 7340032 | tf_op args[5]
  72.6 5.0 %all-to-all-start = ((bf16[1,2,7168,128]{3,1,0,2:T(2,128)(2,1)}), bf16[1,2,7168,128]{3,1,0,2:T(2,128)(2,1)}, u32[]{:S(2)}, u32[]{:S(2)}) async-start(bf16[1,2,7168,128]{3,1,0,2:T(2,128)(2,1)} %copy.54), calls=%async_computation | async-start | bytes 7340032 | tf_op jit(solution)/shard_map/all_to_all | solution.py:27
  77.6 0.0 copy-done.1
  77.6 6.1 %copy.57 = bf16[1,128,7168]{1,0,2:T(2,128)(2,1)} copy(bf16[1,128,7168]{2,1,0:T(8,128)(2,1)S(1)} %copy-done.1) | data formatting | bytes 3670016 | tf_op args[6]
  83.7 0.5 broadcast.76
  84.2 39.7 %reduce = bf16[7168,128]{1,0:T(8,128)(2,1)S(1)} reduce(bf16[7168,1,128]{2,1,0:T(2,128)(2,1)} %bitcast.94, bf16[]{:T(256)} %broadcast.76), dimensions={1}, to_apply=%bitcast.85.reduce_sub_computation | reduce | bytes 3670018
  124.0 1.5 reshape.76
  125.5 0.0 all-to-all-done
  125.5 7.6 %all-to-all-start.2 = ((bf16[32,2,14336]{2,1,0:T(2,128)(2,1)}), bf16[32,2,14336]{2,1,0:T(2,128)(2,1)S(1)}, u32[]{:S(2)}, u32[]{:S(2)}) async-start(bf16[32,2,14336]{2,1,0:T(2,128)(2,1)} %reshape.76), calls=%async_computation.2 | async-start | bytes 3670016 | tf_op jit(solution)/shard_map/all_to_all | solution.py:28
  133.2 4.7 %copy.71 = bf16[1,2,32,224,128]{4,3,1,2,0:T(8,128)(2,1)} copy(bf16[1,2,32,224,128]{4,1,3,2,0:T(2,128)(2,1)} %bitcast.12) | data formatting | bytes 7340032 | tf_op jit(solution)/shard_map/all_to_all | solution.py:27
  137.9 4.8 %gather_fusion.1 = bf16[32,2,224,128]{3,2,1,0:T(8,128)(2,1)} fusion(bf16[32,2,224,128]{3,2,1,0:T(8,128)(2,1)} %bitcast.93, s32[1024]{0:T(1024)S(1)} %pad_clamp_fusion), kind=kCustom, calls=%fused_computation.1 | custom fusion | bytes 7340160 | tf_op jit(solution)/shard_map/jit(_take)/gather | solution.py:30
  142.7 4.2 broadcast_select_fusion
  147.0 12.9 %all-to-all-done.2 = bf16[32,2,14336]{2,1,0:T(2,128)(2,1)S(1)} async-done(((bf16[32,2,14336]{2,1,0:T(2,128)(2,1)}), bf16[32,2,14336]{2,1,0:T(2,128)(2,1)S(1)}, u32[]{:S(2)}, u32[]{:S(2)}) %all-to-all-start.2) | async-done | bytes 1835040 | tf_op jit(solution)/shard_map/all_to_all | solution.py:28
  159.9 4.9 %all-to-all-start.1 = ((bf16[32,2,224,128]{3,2,1,0:T(8,128)(2,1)}), bf16[32,2,224,128]{3,2,1,0:T(8,128)(2,1)}, u32[]{:S(2)}, u32[]{:S(2)}) async-start(bf16[32,2,224,128]{3,2,1,0:T(8,128)(2,1)} %broadcast_select_fusion), calls=%async_computation.1 | async-start | bytes 7340032 | tf_op jit(solution)/shard_map/all_to_all | solution.py:33
  164.7 6.5 %reshape.77 = bf16[7168,1,128]{2,1,0:T(2,128)(2,1)} reshape(bf16[32,2,14336]{2,1,0:T(2,128)(2,1)S(1)} %all-to-all-done.2) | data formatting | bytes 3670016
  171.2 3.5 copy.63
  174.8 2.4 gather_fusion.2
  177.2 1.5 broadcast_select_fusion.1
  178.6 33.8 %all-to-all-done.1 = bf16[32,2,224,128]{3,2,1,0:T(8,128)(2,1)} async-done(((bf16[32,2,224,128]{3,2,1,0:T(8,128)(2,1)}), bf16[32,2,224,128]{3,2,1,0:T(8,128)(2,1)}, u32[]{:S(2)}, u32[]{:S(2)}) %all-to-all-start.1) | async-done | bytes 3670048 | tf_op jit(solution)/shard_map/all_to_all | solution.py:33
  212.4 4.7 %all-to-all-start.3 = ((bf16[32,128,224]{1,2,0:T(8,128)(2,1)}), bf16[32,128,224]{1,2,0:T(8,128)(2,1)}, u32[]{:S(2)}, u32[]{:S(2)}) async-start(bf16[32,128,224]{1,2,0:T(8,128)(2,1)} %broadcast_select_fusion.1), calls=%async_computation.3 | async-start | bytes 3670016 | tf_op jit(solution)/shard_map/all_to_all | solution.py:34
  217.1 0.0 reduce-scatter.4.cloned.1.call-start
  217.2 3.5 fusion.51
  220.7 2.8 fusion.7
  223.5 0.1 copy-done
  223.6 2.7 fusion.5
  226.3 4.6 %fusion.1 = bf16[192,1,7168]{2,0,1:T(8,128)(2,1)S(1)} fusion(bf16[1,128,7168]{2,1,0:T(8,128)(2,1)} %param.13, bf16[1,2,7168,128]{3,2,1,0:T(8,128)(2,1)} %param.12, bf16[192,2,7168]{2,0,1:T(8,128)(2,1)} %all-gather.4.cloned.1.call-done, f32[192,128]{1,0:T(8,128)S(1)} %fusion.5), kind=kOutput, calls=%fused_computation.7 | convolution fusion | flops 706166784 | bytes 9273344 | tf_op jit(solution)/shard_map/dot_general | solution.py:68
  230.8 13.2 %all-to-all-done.3 = bf16[32,128,224]{1,2,0:T(8,128)(2,1)} async-done(((bf16[32,128,224]{1,2,0:T(8,128)(2,1)}), bf16[32,128,224]{1,2,0:T(8,128)(2,1)}, u32[]{:S(2)}, u32[]{:S(2)}) %all-to-all-start.3) | async-done | bytes 1835040 | tf_op jit(solution)/shard_map/all_to_all | solution.py:34
  244.0 6.1 %fusion.2 = bf16[192,1,7168]{2,0,1:T(8,128)(2,1)} fusion(bf16[128,7168]{0,1:T(8,128)(2,1)} %bitcast.24, bf16[7168,128]{1,0:T(8,128)(2,1)} %bitcast.97, bf16[192,2,7168]{2,0,1:T(8,128)(2,1)} %all-gather.4.cloned.1.call-done, f32[192,128]{1,0:T(8,128)S(1)} %fusion.7), kind=kOutput, calls=%fused_computation.8 | convolution fusion | flops 706166784 | bytes 9273344 | tf_op jit(solution)/shard_map/dot_general | solution.py:68
  250.1 2.3 maximum_bitcast_fusion
  252.4 2.9 copy.65
  255.3 0.0 reduce-scatter.4.cloned.1.call-update
  255.3 0.0 copy-start.3
  255.3 0.0 all-reduce.3.cloned.1.call-start
  255.3 63.9 %reduce-scatter.4.cloned.1.call-done = bf16[24,14336]{1,0:T(8,128)(2,1)} async-done(((bf16[192,14336]{1,0:T(8,128)(2,1)}), bf16[24,14336]{1,0:T(8,128)(2,1)}) %reduce-scatter.4.cloned.1.call-update) | async-done | bytes 688144
  319.2 3.0 fusion.13
  322.2 0.0 all-reduce.3.cloned.1.call-update
  322.2 76.4 %psum.7 = s32[32,2]{0,1:T(2,128)S(1)} all-reduce(s32[32,2]{0,1:T(2,128)S(1)} %pad_add_fusion), channel_id=1, replica_groups=mesh['attn'=8,'expert'=32] {'attn','expert'}, use_global_device_ids=true, to_apply=%region_9.10 | all-reduce | flops 64 | bytes 512 | tf_op jit(solution)/shard_map/psum | solution.py:20
  398.6 0.1 constant_dynamic-slice_fusion.1
  398.7 0.6 copy.58
  399.3 0.6 dynamic-slice
  400.5 36.6 %all-reduce.3.cloned.1.call-done = bf16[64,7168]{1,0:T(8,128)(2,1)} async-done(((bf16[64,7168]{1,0:T(8,128)(2,1)}), bf16[64,7168]{1,0:T(8,128)(2,1)}) %all-reduce.3.cloned.1.call-update) | async-done | bytes 917520
  437.1 1.5 constant_dynamic-slice_fusion
  (13 shorter events, 0.1 us)
Async XLA Ops:
  7.2 213.6 %all-gather.4.cloned.1.call-start = ((), (), s32[]{:S(2)}) async-start(), calls=%async_computation.5 | async-start | bytes 6193152 | tf_op jit(solution)/shard_map/all_gather | solution.py:57
  72.6 5.0 %copy-start.1 = (bf16[1,128,7168]{2,1,0:T(8,128)(2,1)S(1)}, bf16[1,128,7168]{2,1,0:T(8,128)(2,1)}, u32[]{:S(2)}) copy-start(bf16[1,128,7168]{2,1,0:T(8,128)(2,1)} %param.13) | copy-start | bytes 5505028
  72.6 52.8 %all-to-all-start = ((bf16[1,2,7168,128]{3,1,0,2:T(2,128)(2,1)}), bf16[1,2,7168,128]{3,1,0,2:T(2,128)(2,1)}, u32[]{:S(2)}, u32[]{:S(2)}) async-start(bf16[1,2,7168,128]{3,1,0,2:T(2,128)(2,1)} %copy.54), calls=%async_computation | async-start | bytes 7340032 | tf_op jit(solution)/shard_map/all_to_all | solution.py:27
  125.5 7.6 %copy-start.2 = (s32[32]{0:T(128)S(1)}, s32[32]{0:T(128)}, u32[]{:S(2)}) copy-start(s32[32]{0:T(128)} %param.11) | copy-start | bytes 388
  125.5 34.4 %all-to-all-start.2 = ((bf16[32,2,14336]{2,1,0:T(2,128)(2,1)}), bf16[32,2,14336]{2,1,0:T(2,128)(2,1)S(1)}, u32[]{:S(2)}, u32[]{:S(2)}) async-start(bf16[32,2,14336]{2,1,0:T(2,128)(2,1)} %reshape.76), calls=%async_computation.2 | async-start | bytes 3670016 | tf_op jit(solution)/shard_map/all_to_all | solution.py:28
  159.9 52.5 %all-to-all-start.1 = ((bf16[32,2,224,128]{3,2,1,0:T(8,128)(2,1)}), bf16[32,2,224,128]{3,2,1,0:T(8,128)(2,1)}, u32[]{:S(2)}, u32[]{:S(2)}) async-start(bf16[32,2,224,128]{3,2,1,0:T(8,128)(2,1)} %broadcast_select_fusion), calls=%async_computation.1 | async-start | bytes 7340032 | tf_op jit(solution)/shard_map/all_to_all | solution.py:33
  212.4 31.6 %all-to-all-start.3 = ((bf16[32,128,224]{1,2,0:T(8,128)(2,1)}), bf16[32,128,224]{1,2,0:T(8,128)(2,1)}, u32[]{:S(2)}, u32[]{:S(2)}) async-start(bf16[32,128,224]{1,2,0:T(8,128)(2,1)} %broadcast_select_fusion.1), calls=%async_computation.3 | async-start | bytes 3670016 | tf_op jit(solution)/shard_map/all_to_all | solution.py:34
  217.1 102.1 %reduce-scatter.4.cloned.1.call-start = ((), (), s32[]{:S(2)}) async-start(), calls=%async_computation.6 | async-start | bytes 6193152
  220.7 2.9 copy-start
  255.3 144.0 %copy-start.3 = (u32[256]{0:T(256)S(1)}, u32[256]{0:T(256)}, u32[]{:S(2)}) copy-start(u32[256]{0:T(256)} %constant.73) | copy-start | bytes 3076
  255.3 181.8 %all-reduce.3.cloned.1.call-start = ((), (), s32[]{:S(2)}) async-start(), calls=%async_computation.7 | async-start | bytes 1835008
Sparse Core Ops, SparseCore 0:
  63.6 64.5 all-gather.3
  255.4 63.7 reduce-scatter.3
  322.5 114.5 all-reduce.2
where the time goes:
time: 448 us; the launch traced here: 445 us
  waiting for transfers between devices  160 us (36%)
  blocking collectives  125 us (28%)
  other arithmetic  52.4 us (12%)
  local copies, waits for them, and re-layouts  50.2 us (11%)
  starting transfers between devices  22.3 us (5%)
  matrix products  20.3 us (5%)
  between operations  14.6 us (3%)
    unnamed x5, waiting for transfers between devices  100 us
    psum x1, blocking collectives, body(): totals = lax.psum(local_counts, ('attn', 'expert'))  76.4 us
    unnamed x2, other arithmetic  42 us
    all_to_all x1, waiting for transfers between devices, body(): lax.all_to_all(picked_in, 'expert', split_axis=0, concat_axis=2, tiled=True)  33.8 us
    unnamed x19, local copies, waits for them, and re-layouts  33.2 us
    all_gather x1, blocking collectives, body(): group_coef = lax.all_gather(slot_coef, 'expert', axis=0, tiled=True)  24.5 us
    all_gather x1, blocking collectives, body(): group_tokens = lax.all_gather(tokens, 'expert', axis=0, tiled=True)  24.3 us
    all_to_all x1, waiting for transfers between devices, body(): lax.all_to_all(picked_down, 'expert', split_axis=0, concat_axis=2, tiled=...  13.2 us
  transfers between devices with their start and end apart: 7, of which 5 were waited for; matrix products, arithmetic and copies ran while one was open for 22% of the time, Pallas kernels for 0%

commit v1 on v0

v1 whole, which is shorter than its diff:
```python
import jax
import jax.numpy as jnp
from jax import lax
from jax.sharding import PartitionSpec as P

F32, BF16 = jnp.float32, jnp.bfloat16
MOST = 24
META = 128


def ring_shift(value, step, count):
    return lax.ppermute(value, "attn", [(i, (i + step) % count) for i in range(count)])


def core_swap(value, groups):
    return lax.ppermute(value, "expert", [(i, i ^ 1) for i in range(groups)])


def gather_ring(chunks, count):
    half = count // 2
    right = [[c] for c in chunks]
    left = [[c] for c in chunks]
    for step in range(half):
        for r, l in zip(right, left):
            r.append(ring_shift(r[-1], 1, count))
            if step < half - 1:
                l.append(ring_shift(l[-1], count - 1, count))
    return [r + l[1:] for r, l in zip(right, left)]


def reduce_ring(chunks, count):
    half = count // 2
    right = [f(half).astype(BF16) for f in chunks]
    left = [f(count - half + 1).astype(BF16) for f in chunks]
    for step in range(half - 1, 0, -1):
        for c, f in enumerate(chunks):
            right[c] = (ring_shift(right[c], 1, count).astype(F32) + f(step)).astype(BF16)
            if step > 1:
                left[c] = (
                    ring_shift(left[c], count - 1, count).astype(F32) + f(count - step + 1)
                ).astype(BF16)
    return [
        (
            f(0)
            + ring_shift(right[c], 1, count).astype(F32)
            + ring_shift(left[c], count - 1, count).astype(F32)
        ).astype(BF16)
        for c, f in enumerate(chunks)
    ]


def body(tokens, expert_ids, replica, route_weight, spare_plan, w_in, w_down):
    rows, width = tokens.shape
    top = expert_ids.shape[1]
    count = lax.axis_size("attn")
    groups = lax.axis_size("expert")
    me = lax.axis_index("expert")
    peers = groups // 2
    same_core = [[core + 2 * j for j in range(peers)] for core in range(2)]

    high = route_weight.astype(BF16)
    rest = route_weight - high.astype(F32)
    middle = rest.astype(BF16)
    low = (rest - middle.astype(F32)).astype(BF16)
    meta = [expert_ids.astype(BF16), replica.astype(BF16), high, middle, low]
    pad = jnp.zeros((rows, META - 5 * top), BF16)
    sent = jnp.concatenate([tokens] + meta + [pad], 1)

    spread = jnp.broadcast_to(sent[None], (peers, rows, width + META))
    near = lax.all_to_all(spread, "expert", 0, 0, axis_index_groups=same_core, tiled=True)
    near = near.reshape(peers * rows, width + META)
    far = core_swap(near, groups)
    group_rows = jnp.concatenate([near, far], 0)
    total = group_rows.shape[0]

    info = group_rows[:, width : width + 5 * top].astype(F32).reshape(total, 5, top)
    ids, copies = info[:, 0], info[:, 1]
    weights = info[:, 2] + info[:, 3] + info[:, 4]
    named = ids == me.astype(F32)
    spare = lax.dynamic_index_in_dim(spare_plan, me, 0, keepdims=False).astype(F32)
    counts = jnp.stack(
        [
            jnp.sum((named & (copies == 0.0)).astype(F32)),
            jnp.sum(((ids == spare) & (copies == 1.0)).astype(F32)),
        ]
    )
    hit = jnp.sum(named.astype(F32), 1)
    coef = jnp.sum(jnp.where(named, weights, 0.0), 1)
    place = jnp.arange(total, dtype=jnp.int32)
    before = (place[:, None] > place[None, :]).astype(F32)
    rank = jnp.sum(before * hit[None, :], 1)
    slot = jnp.arange(MOST, dtype=jnp.int32).astype(F32)
    chosen = jnp.where((hit[None, :] > 0.0) & (rank[None, :] == slot[:, None]), 1.0, 0.0)
    packed = jnp.dot(chosen.astype(BF16), group_rows[:, :width], preferred_element_type=F32)
    packed = packed.astype(BF16)
    half = width // 2
    tail = jnp.broadcast_to(jnp.pad(counts, (0, META - 2))[None], (MOST, META)).astype(BF16)
    parts = [jnp.concatenate([packed[:, :half], tail], 1), packed[:, half:]]
    first, second = gather_ring(parts, count)

    load = sum(b[0, half : half + 2].astype(F32) for b in first)
    slot_load = load.astype(jnp.int32)[None]

    first_rows = jnp.concatenate([b[:, :half] for b in first], 0)
    second_rows = jnp.concatenate(second, 0)

    def up(which):
        w = w_in[0, which]
        return jnp.dot(first_rows, w[:half], preferred_element_type=F32) + jnp.dot(
            second_rows, w[half:], preferred_element_type=F32
        )

    hidden = (jax.nn.silu(up(0)) * up(1)).astype(BF16)
    place_of = {0: 0}
    for s in range(1, count // 2 + 1):
        place_of[count - s] = s
    for s in range(1, count // 2):
        place_of[s] = count // 2 + s
    down = [
        jnp.dot(hidden, w_down[0][:, :half], preferred_element_type=F32),
        jnp.dot(hidden, w_down[0][:, half:], preferred_element_type=F32),
    ]

    def block(c):
        return lambda s: down[c][place_of[s] * MOST : (place_of[s] + 1) * MOST]

    summed = jnp.concatenate(reduce_ring([block(0), block(1)], count), 1)

    mix = chosen.T * coef[:, None]
    mix_high = mix.astype(BF16)
    mix_low = (mix - mix_high.astype(F32)).astype(BF16)
    share = jnp.dot(mix_high, summed, preferred_element_type=F32) + jnp.dot(
        mix_low, summed, preferred_element_type=F32
    )
    near_count = peers * rows
    other = core_swap(share[near_count:].astype(BF16), groups)
    pair = (share[:near_count] + other.astype(F32)).astype(BF16)
    back = lax.all_to_all(
        pair.reshape(peers, rows, width), "expert", 0, 0, axis_index_groups=same_core, tiled=True
    )
    layer_output = jnp.sum(back.astype(F32), 0).astype(BF16)
    return layer_output, slot_load


def solution(mesh):
    placed = (
        P(("attn", "expert"), None),
        P(("attn", "expert"), None),
        P(("attn", "expert"), None),
        P(("attn", "expert"), None),
        P(),
        P("expert", None, None, "attn"),
        P("expert", "attn", None),
    )
    return jax.shard_map(
        body,
        mesh=mesh,
        in_specs=placed,
        out_specs=(P(("attn", "expert"), None), P("expert", None)),
        check_vma=False,
    )
```

time: 448 us -> 129 us (0.29)
  waiting for transfers between devices: 160 us -> 38 us
  blocking collectives: 125 us -> 17.7 us
  other arithmetic: 52.4 us -> 8.47 us
  local copies, waits for them, and re-layouts: 50.2 us -> 7.36 us
  starting transfers between devices: 22.3 us -> 48.9 us
  matrix products: 20.3 us -> 5.08 us
  between operations: 14.6 us -> 1.63 us
    unnamed x5 -> x0, waiting for transfers between devices: 100 us -> none
    psum x1 -> x0, blocking collectives: 76.4 us -> none  [body(): totals = lax.psum(local_counts, ('attn', 'expert'))]
    all_to_all x4 -> x1, waiting for transfers between devices: 59.8 us -> 9.6 us  [body(): lax.all_to_all(pair.reshape(peers, rows, width), 'expert', 0, 0, axis_ind...]
    all_gather x2 -> x0, blocking collectives: 48.7 us -> none  [the longest x1 24.5 us: body(): group_coef = lax.all_gather(slot_coef, 'expert', axis=0, tiled=True)]
    ppermute x0 -> x30, starting transfers between devices: none -> 45.3 us  [the longest x28 45.2 us: ring_shift(): lax.ppermute(value, 'attn', [(i, (i + step) % count) for i in range(count)])]
    unnamed x2 -> x0, other arithmetic: 42 us -> none
    unnamed x19 -> x20, local copies, waits for them, and re-layouts: 33.2 us -> 1.13 us
    ppermute x0 -> x30, waiting for transfers between devices: none -> 28.4 us  [the longest x28 26.6 us: ring_shift(): lax.ppermute(value, 'attn', [(i, (i + step) % count) for i in range(count)])]
  transfers between devices with their start and end apart: 7 -> 31, of which waited for: 5 -> 22; matrix products, arithmetic and copies ran while one was open for 22% -> 5% of each run, Pallas kernels for 0% -> 0%
where the time goes in v1:
time: 129 us; the launch traced here: 127 us
  starting transfers between devices  48.9 us (38%)
  waiting for transfers between devices  38 us (29%)
  blocking collectives  17.7 us (14%)
  other arithmetic  8.47 us (7%)
  local copies, waits for them, and re-layouts  7.36 us (6%)
  matrix products  5.08 us (4%)
  between operations  1.63 us (1%)
    ppermute x28, starting transfers between devices, ring_shift(): lax.ppermute(value, 'attn', [(i, (i + step) % count) for i in range(count)])  45.2 us
    ppermute x28, waiting for transfers between devices, ring_shift(): lax.ppermute(value, 'attn', [(i, (i + step) % count) for i in range(count)])  26.6 us
    all_to_all x1, blocking collectives, body(): lax.all_to_all(spread, 'expert', 0, 0, axis_index_groups=same_core, tiled...  17.7 us
    all_to_all x1, waiting for transfers between devices, body(): lax.all_to_all(pair.reshape(peers, rows, width), 'expert', 0, 0, axis_ind...  9.6 us
    all_to_all x1, starting transfers between devices, body(): lax.all_to_all(pair.reshape(peers, rows, width), 'expert', 0, 0, axis_ind...  3.56 us
  transfers between devices with their start and end apart: 31, of which 22 were waited for; matrix products, arithmetic and copies ran while one was open for 5% of the time, Pallas kernels for 0%

profile of v1, /device:TPU:64, one launch (start us, length us, event | category | flops | bytes accessed | tf_op | source)
XLA Modules:
  0.0 127.2 jit_solution(1294356489089628525)
XLA Ops:
  0.6 0.7 convert_element_type.205
  1.3 0.7 convert_element_type.206
  2.0 0.8 subtract_convert_fusion.2
  2.8 0.8 concatenate.18
  3.9 17.7 %all_to_all.10 = bf16[16,2,7296]{2,1,0:T(2,128)(2,1)S(1)} all-to-all(bf16[16,2,7296]{2,1,0:T(2,128)(2,1)S(1)} %broadcast_in_dim.40), channel_id=1, replica_groups={{0,2,4,6,8,10,12,14,16,18,20,22,24,26,28,30},{1,3,5,7,9,11,13,15,17,19,..., dimensions={0} | all-to-all | bytes 933888 | tf_op jit(solution)/shard_map/all_to_all | solution.py:70
  21.9 0.6 dynamic_slice.4
  23.1 1.4 %copy.14 = bf16[32,7296]{0,1:T(8,128)(2,1)S(1)} copy(bf16[32,7296]{1,0:T(8,128)(2,1)S(1)} %reshape.54) | data formatting | bytes 933888 | tf_op jit(solution)/shard_map/reshape | solution.py:71
  24.5 1.8 %copy.15 = bf16[32,7296]{0,1:T(8,128)(2,1)} copy(bf16[32,7296]{1,0:T(8,128)(2,1)S(1)} %collective-permute-done) | data formatting | bytes 933888 | tf_op jit(solution)/shard_map/ppermute | solution.py:16
  26.4 0.9 fusion.46
  27.3 0.6 fusion.53
  28.1 1.1 convolution_convert_fusion
  29.4 1.9 %collective-permute-start.8 = (bf16[24,3584]{1,0:T(8,128)(2,1)S(1)}, bf16[24,3584]{1,0:T(8,128)(2,1)S(1)}, u32[]{:S(2)}, u32[]{:S(2)}) collective-permute-start(bf16[24,3584]{1,0:T(8,128)(2,1)S(1)} %get-tuple-element.21), channel_id=1, source_target_pairs={{0,32},{32,64},{64,96},{96,128},{128,160},{160,192},{192,224},{224... | collective-permute-start | bytes 516104 | tf_op jit(solution)/shard_map/ppermute | solution.py:12
  31.3 1.3 pad_maximum_fusion.6
  32.8 3.1 %collective-permute-start.1 = (bf16[24,3712]{1,0:T(8,128)(2,1)S(1)}, bf16[24,3712]{1,0:T(8,128)(2,1)S(1)}, u32[]{:S(2)}, u32[]{:S(2)}) collective-permute-start(bf16[24,3712]{1,0:T(8,128)(2,1)S(1)} %pad_maximum_fusion.5), channel_id=1, source_target_pairs={{0,32},{32,64},{64,96},{96,128},{128,160},{160,192},{192,224},{224... | collective-permute-start | bytes 534536 | tf_op jit(solution)/shard_map/ppermute | solution.py:12
  36.2 0.5 collective-permute-start.13
  36.8 2.6 %collective-permute-start.9 = (bf16[24,3584]{1,0:T(8,128)(2,1)S(1)}, bf16[24,3584]{1,0:T(8,128)(2,1)S(1)}, u32[]{:S(2)}, u32[]{:S(2)}) collective-permute-start(bf16[24,3584]{1,0:T(8,128)(2,1)S(1)} %collective-permute-done.8), channel_id=1, source_target_pairs={{0,32},{32,64},{64,96},{96,128},{128,160},{160,192},{192,224},{224... | collective-permute-start | bytes 516104 | tf_op jit(solution)/shard_map/ppermute | solution.py:12
  39.4 1.7 %collective-permute-done.5 = bf16[24,3712]{1,0:T(8,128)(2,1)S(1)} collective-permute-done((bf16[24,3712]{1,0:T(8,128)(2,1)S(1)}, bf16[24,3712]{1,0:T(8,128)(2,1)S(1)}, u32[]{:S(2)}, u32[]{:S(2)}) %collective-permute-start.5) | collective-permute-done | bytes 178208 | tf_op jit(solution)/shard_map/ppermute | solution.py:12
  41.1 0.5 collective-permute-start.6
  42.0 2.3 %collective-permute-start.2 = (bf16[24,3712]{1,0:T(8,128)(2,1)S(1)}, bf16[24,3712]{1,0:T(8,128)(2,1)S(1)}, u32[]{:S(2)}, u32[]{:S(2)}) collective-permute-start(bf16[24,3712]{1,0:T(8,128)(2,1)S(1)} %collective-permute-done.1), channel_id=1, source_target_pairs={{0,32},{32,64},{64,96},{96,128},{128,160},{160,192},{192,224},{224... | collective-permute-start | bytes 534536 | tf_op jit(solution)/shard_map/ppermute | solution.py:12
  44.3 0.5 collective-permute-done.13
  44.8 0.5 collective-permute-start.14
  45.7 2.1 %collective-permute-start.10 = (bf16[24,3584]{1,0:T(8,128)(2,1)S(1)}, bf16[24,3584]{1,0:T(8,128)(2,1)S(1)}, u32[]{:S(2)}, u32[]{:S(2)}) collective-permute-start(bf16[24,3584]{1,0:T(8,128)(2,1)S(1)} %collective-permute-done.9), channel_id=1, source_target_pairs={{0,32},{32,64},{64,96},{96,128},{128,160},{160,192},{192,224},{224... | collective-permute-start | bytes 516104 | tf_op jit(solution)/shard_map/ppermute | solution.py:12
  47.8 0.8 collective-permute-done.6
  48.6 0.8 collective-permute-start.7
  49.4 2.2 %collective-permute-start.3 = (bf16[24,3712]{1,0:T(8,128)(2,1)S(1)}, bf16[24,3712]{1,0:T(8,128)(2,1)S(1)}, u32[]{:S(2)}, u32[]{:S(2)}) collective-permute-start(bf16[24,3712]{1,0:T(8,128)(2,1)S(1)} %collective-permute-done.2), channel_id=1, source_target_pairs={{0,32},{32,64},{64,96},{96,128},{128,160},{160,192},{192,224},{224... | collective-permute-start | bytes 534536 | tf_op jit(solution)/shard_map/ppermute | solution.py:12
  51.6 2.3 %collective-permute-done.10 = bf16[24,3584]{1,0:T(8,128)(2,1)S(1)} collective-permute-done((bf16[24,3584]{1,0:T(8,128)(2,1)S(1)}, bf16[24,3584]{1,0:T(8,128)(2,1)S(1)}, u32[]{:S(2)}, u32[]{:S(2)}) %collective-permute-start.10) | collective-permute-done | bytes 172064 | tf_op jit(solution)/shard_map/ppermute | solution.py:12
  53.9 1.8 %collective-permute-start.11 = (bf16[24,3584]{1,0:T(8,128)(2,1)S(1)}, bf16[24,3584]{1,0:T(8,128)(2,1)S(1)}, u32[]{:S(2)}, u32[]{:S(2)}) collective-permute-start(bf16[24,3584]{1,0:T(8,128)(2,1)S(1)} %collective-permute-done.10), channel_id=1, source_target_pairs={{0,32},{32,64},{64,96},{96,128},{128,160},{160,192},{192,224},{224... | collective-permute-start | bytes 516104 | tf_op jit(solution)/shard_map/ppermute | solution.py:12
  55.7 2.0 %collective-permute-done.3 = bf16[24,3712]{1,0:T(8,128)(2,1)S(1)} collective-permute-done((bf16[24,3712]{1,0:T(8,128)(2,1)S(1)}, bf16[24,3712]{1,0:T(8,128)(2,1)S(1)}, u32[]{:S(2)}, u32[]{:S(2)}) %collective-permute-start.3) | collective-permute-done | bytes 178208 | tf_op jit(solution)/shard_map/ppermute | solution.py:12
  57.7 1.9 %collective-permute-start.4 = (bf16[24,3712]{1,0:T(8,128)(2,1)S(1)}, bf16[24,3712]{1,0:T(8,128)(2,1)S(1)}, u32[]{:S(2)}, u32[]{:S(2)}) collective-permute-start(bf16[24,3712]{1,0:T(8,128)(2,1)S(1)} %collective-permute-done.3), channel_id=1, source_target_pairs={{0,32},{32,64},{64,96},{96,128},{128,160},{160,192},{192,224},{224... | collective-permute-start | bytes 534536 | tf_op jit(solution)/shard_map/ppermute | solution.py:12
  59.6 2.5 %collective-permute-done.11 = bf16[24,3584]{1,0:T(8,128)(2,1)S(1)} collective-permute-done((bf16[24,3584]{1,0:T(8,128)(2,1)S(1)}, bf16[24,3584]{1,0:T(8,128)(2,1)S(1)}, u32[]{:S(2)}, u32[]{:S(2)}) %collective-permute-start.11) | collective-permute-done | bytes 172064 | tf_op jit(solution)/shard_map/ppermute | solution.py:12
  62.2 0.5 fusion.6
  62.7 0.5 fusion.9
  63.2 1.2 collective-permute-done.4
  64.5 0.5 convolution_add_fusion.2
  65.0 0.5 multiply_convert_fusion
  65.5 1.0 copy-done.1
  66.5 0.5 fusion.75
  67.0 0.5 fusion.76
  67.6 1.9 %collective-permute-start.22 = (bf16[24,3584]{1,0:T(8,128)(2,1)S(1)}, bf16[24,3584]{1,0:T(8,128)(2,1)S(1)}, u32[]{:S(2)}, u32[]{:S(2)}) collective-permute-start(bf16[24,3584]{1,0:T(8,128)(2,1)S(1)} %get-tuple-element.16), channel_id=1, source_target_pairs={{0,32},{32,64},{64,96},{96,128},{128,160},{160,192},{192,224},{224... | collective-permute-start | bytes 516104 | tf_op jit(solution)/shard_map/ppermute | solution.py:12
  69.5 1.5 %collective-permute-start.26 = (bf16[24,3584]{1,0:T(8,128)(2,1)S(1)}, bf16[24,3584]{1,0:T(8,128)(2,1)S(1)}, u32[]{:S(2)}, u32[]{:S(2)}) collective-permute-start(bf16[24,3584]{1,0:T(8,128)(2,1)S(1)} %get-tuple-element.17), channel_id=1, source_target_pairs={{0,224},{32,0},{64,32},{96,64},{128,96},{160,128},{192,160},{224,1... | collective-permute-start | bytes 516104 | tf_op jit(solution)/shard_map/ppermute | solution.py:12
  71.0 2.3 %collective-permute-start.15 = (bf16[24,3584]{1,0:T(8,128)(2,1)S(1)}, bf16[24,3584]{1,0:T(8,128)(2,1)S(1)}, u32[]{:S(2)}, u32[]{:S(2)}) collective-permute-start(bf16[24,3584]{1,0:T(8,128)(2,1)S(1)} %get-tuple-element.14), channel_id=1, source_target_pairs={{0,32},{32,64},{64,96},{96,128},{128,160},{160,192},{192,224},{224... | collective-permute-start | bytes 516104 | tf_op jit(solution)/shard_map/ppermute | solution.py:12
  73.3 1.1 collective-permute-start.19
  74.4 1.7 %collective-permute-done.22 = bf16[24,3584]{1,0:T(8,128)(2,1)S(1)} collective-permute-done((bf16[24,3584]{1,0:T(8,128)(2,1)S(1)}, bf16[24,3584]{1,0:T(8,128)(2,1)S(1)}, u32[]{:S(2)}, u32[]{:S(2)}) %collective-permute-start.22) | collective-permute-done | bytes 172064 | tf_op jit(solution)/shard_map/ppermute | solution.py:12
  76.1 1.9 %collective-permute-start.23 = (bf16[24,3584]{1,0:T(8,128)(2,1)S(1)}, bf16[24,3584]{1,0:T(8,128)(2,1)S(1)}, u32[]{:S(2)}, u32[]{:S(2)}) collective-permute-start(bf16[24,3584]{1,0:T(8,128)(2,1)S(1)} %fusion.20), channel_id=1, source_target_pairs={{0,32},{32,64},{64,96},{96,128},{128,160},{160,192},{192,224},{224... | collective-permute-start | bytes 516104 | tf_op jit(solution)/shard_map/ppermute | solution.py:12
  78.1 1.7 %collective-permute-done.15 = bf16[24,3584]{1,0:T(8,128)(2,1)S(1)} collective-permute-done((bf16[24,3584]{1,0:T(8,128)(2,1)S(1)}, bf16[24,3584]{1,0:T(8,128)(2,1)S(1)}, u32[]{:S(2)}, u32[]{:S(2)}) %collective-permute-start.15) | collective-permute-done | bytes 172064 | tf_op jit(solution)/shard_map/ppermute | solution.py:12
  79.8 2.0 %collective-permute-start.16 = (bf16[24,3584]{1,0:T(8,128)(2,1)S(1)}, bf16[24,3584]{1,0:T(8,128)(2,1)S(1)}, u32[]{:S(2)}, u32[]{:S(2)}) collective-permute-start(bf16[24,3584]{1,0:T(8,128)(2,1)S(1)} %fusion.27), channel_id=1, source_target_pairs={{0,32},{32,64},{64,96},{96,128},{128,160},{160,192},{192,224},{224... | collective-permute-start | bytes 516104 | tf_op jit(solution)/shard_map/ppermute | solution.py:12
  81.9 1.5 %collective-permute-done.23 = bf16[24,3584]{1,0:T(8,128)(2,1)S(1)} collective-permute-done((bf16[24,3584]{1,0:T(8,128)(2,1)S(1)}, bf16[24,3584]{1,0:T(8,128)(2,1)S(1)}, u32[]{:S(2)}, u32[]{:S(2)}) %collective-permute-start.23) | collective-permute-done | bytes 172064 | tf_op jit(solution)/shard_map/ppermute | solution.py:12
  83.5 1.7 %collective-permute-start.24 = (bf16[24,3584]{1,0:T(8,128)(2,1)S(1)}, bf16[24,3584]{1,0:T(8,128)(2,1)S(1)}, u32[]{:S(2)}, u32[]{:S(2)}) collective-permute-start(bf16[24,3584]{1,0:T(8,128)(2,1)S(1)} %get-tuple-element.12), channel_id=1, source_target_pairs={{0,32},{32,64},{64,96},{96,128},{128,160},{160,192},{192,224},{224... | collective-permute-start | bytes 516104 | tf_op jit(solution)/shard_map/ppermute | solution.py:12
  85.2 1.4 %collective-permute-start.27 = (bf16[24,3584]{1,0:T(8,128)(2,1)S(1)}, bf16[24,3584]{1,0:T(8,128)(2,1)S(1)}, u32[]{:S(2)}, u32[]{:S(2)}) collective-permute-start(bf16[24,3584]{1,0:T(8,128)(2,1)S(1)} %get-tuple-element.13), channel_id=1, source_target_pairs={{0,224},{32,0},{64,32},{96,64},{128,96},{160,128},{192,160},{224,1... | collective-permute-start | bytes 516104 | tf_op jit(solution)/shard_map/ppermute | solution.py:12
  86.7 1.5 %collective-permute-done.16 = bf16[24,3584]{1,0:T(8,128)(2,1)S(1)} collective-permute-done((bf16[24,3584]{1,0:T(8,128)(2,1)S(1)}, bf16[24,3584]{1,0:T(8,128)(2,1)S(1)}, u32[]{:S(2)}, u32[]{:S(2)}) %collective-permute-start.16) | collective-permute-done | bytes 172064 | tf_op jit(solution)/shard_map/ppermute | solution.py:12
  88.2 1.4 %collective-permute-start.17 = (bf16[24,3584]{1,0:T(8,128)(2,1)S(1)}, bf16[24,3584]{1,0:T(8,128)(2,1)S(1)}, u32[]{:S(2)}, u32[]{:S(2)}) collective-permute-start(bf16[24,3584]{1,0:T(8,128)(2,1)S(1)} %get-tuple-element.8), channel_id=1, source_target_pairs={{0,32},{32,64},{64,96},{96,128},{128,160},{160,192},{192,224},{224... | collective-permute-start | bytes 516104 | tf_op jit(solution)/shard_map/ppermute | solution.py:12
  89.7 1.8 %collective-permute-start.20 = (bf16[24,3584]{1,0:T(8,128)(2,1)S(1)}, bf16[24,3584]{1,0:T(8,128)(2,1)S(1)}, u32[]{:S(2)}, u32[]{:S(2)}) collective-permute-start(bf16[24,3584]{1,0:T(8,128)(2,1)S(1)} %get-tuple-element.9), channel_id=1, source_target_pairs={{0,224},{32,0},{64,32},{96,64},{128,96},{160,128},{192,160},{224,1... | collective-permute-start | bytes 516104 | tf_op jit(solution)/shard_map/ppermute | solution.py:12
  91.6 0.8 collective-permute-done.27
  92.5 4.2 %collective-permute-start.25 = (bf16[24,3584]{1,0:T(8,128)(2,1)S(1)}, bf16[24,3584]{1,0:T(8,128)(2,1)S(1)}, u32[]{:S(2)}, u32[]{:S(2)}) collective-permute-start(bf16[24,3584]{1,0:T(8,128)(2,1)S(1)} %get-tuple-element.10), channel_id=1, source_target_pairs={{0,32},{32,64},{64,96},{96,128},{128,160},{160,192},{192,224},{224... | collective-permute-start | bytes 516104 | tf_op jit(solution)/shard_map/ppermute | solution.py:12
  96.6 1.8 %collective-permute-done.20 = bf16[24,3584]{1,0:T(8,128)(2,1)S(1)} collective-permute-done((bf16[24,3584]{1,0:T(8,128)(2,1)S(1)}, bf16[24,3584]{1,0:T(8,128)(2,1)S(1)}, u32[]{:S(2)}, u32[]{:S(2)}) %collective-permute-start.20) | collective-permute-done | bytes 172064 | tf_op jit(solution)/shard_map/ppermute | solution.py:12
  98.6 3.2 %collective-permute-start.18 = (bf16[24,3584]{1,0:T(8,128)(2,1)S(1)}, bf16[24,3584]{1,0:T(8,128)(2,1)S(1)}, u32[]{:S(2)}, u32[]{:S(2)}) collective-permute-start(bf16[24,3584]{1,0:T(8,128)(2,1)S(1)} %get-tuple-element.6), channel_id=1, source_target_pairs={{0,32},{32,64},{64,96},{96,128},{128,160},{160,192},{192,224},{224... | collective-permute-start | bytes 516104 | tf_op jit(solution)/shard_map/ppermute | solution.py:12
  102.1 2.6 %collective-permute-done.18 = bf16[24,3584]{1,0:T(8,128)(2,1)S(1)} collective-permute-done((bf16[24,3584]{1,0:T(8,128)(2,1)S(1)}, bf16[24,3584]{1,0:T(8,128)(2,1)S(1)}, u32[]{:S(2)}, u32[]{:S(2)}) %collective-permute-start.18) | collective-permute-done | bytes 172064 | tf_op jit(solution)/shard_map/ppermute | solution.py:12
  104.7 2.5 %collective-permute-done.21 = bf16[24,3584]{1,0:T(8,128)(2,1)S(1)} collective-permute-done((bf16[24,3584]{1,0:T(8,128)(2,1)S(1)}, bf16[24,3584]{1,0:T(8,128)(2,1)S(1)}, u32[]{:S(2)}, u32[]{:S(2)}) %collective-permute-start.21) | collective-permute-done | bytes 172064 | tf_op jit(solution)/shard_map/ppermute | solution.py:12
  108.4 1.8 %collective-permute-done.29 = bf16[32,7168]{1,0:T(8,128)(2,1)S(1)} collective-permute-done((bf16[32,7168]{1,0:T(8,128)(2,1)S(1)}, bf16[32,7168]{1,0:T(8,128)(2,1)S(1)}, u32[]{:S(2)}, u32[]{:S(2)}) %collective-permute-start.29) | collective-permute-done | bytes 458784 | tf_op jit(solution)/shard_map/ppermute | solution.py:16
  110.3 0.9 reshape.57
  111.2 3.6 %all-to-all-start.1 = ((bf16[16,2,7168]{2,1,0:T(2,128)(2,1)}), bf16[16,2,7168]{2,1,0:T(2,128)(2,1)S(1)}, u32[]{:S(2)}, u32[]{:S(2)}) async-start(bf16[16,2,7168]{2,1,0:T(2,128)(2,1)} %reshape.57), calls=%async_computation.1 | async-start | bytes 917504 | tf_op jit(solution)/shard_map/all_to_all | solution.py:138
  114.8 1.8 %fusion.56 = s32[1,2]{1,0:T(1,128)} fusion(bf16[24,3712]{1,0:T(8,128)(2,1)S(1)} %collective-permute-done.7, bf16[24,3712]{1,0:T(8,128)(2,1)S(1)} %collective-permute-done.6, bf16[24,3712]{1,0:T(8,128)(2,1)S(1)} %collective-permute-done.5, bf16[24,3712]{1,0:T(8,128)(2,1)S(1)} %collective-permute-done.4, bf16[24,3712]{1,0:T(8,128)(2,1)S(1)} %collective-permute-done.3, ...), kind=kLoop, calls=%fused_computation.110 | loop fusion | flops 40 | bytes 40 | tf_op jit(solution)/shard_map/convert_element_type | solution.py:102
  116.5 9.6 %all-to-all-done.1 = bf16[16,2,7168]{2,1,0:T(2,128)(2,1)S(1)} async-done(((bf16[16,2,7168]{2,1,0:T(2,128)(2,1)}), bf16[16,2,7168]{2,1,0:T(2,128)(2,1)S(1)}, u32[]{:S(2)}, u32[]{:S(2)}) %all-to-all-start.1) | async-done | bytes 458784 | tf_op jit(solution)/shard_map/all_to_all | solution.py:138
  126.2 1.0 reduce_sum.62
  (64 shorter events, 4.3 us)
Async XLA Ops:
  0.6 21.2 %copy-start.3 = (s32[32]{0:T(128)S(1)}, s32[32]{0:T(128)}, u32[]{:S(2)}) copy-start(s32[32]{0:T(128)} %param.11) | copy-start | bytes 388
  21.8 2.8 %collective-permute-start = (bf16[32,7296]{1,0:T(8,128)(2,1)S(1)}, bf16[32,7296]{1,0:T(8,128)(2,1)S(1)}, u32[]{:S(2)}, u32[]{:S(2)}) collective-permute-start(bf16[32,7296]{1,0:T(8,128)(2,1)S(1)} %reshape.54), channel_id=1, source_target_pairs={{0,1},{1,0},{2,3},{3,2},{4,5},{5,4},{6,7},{7,6},{8,9},{9,8},{10,11... | collective-permute-start | bytes 1400840 | tf_op jit(solution)/shard_map/ppermute | solution.py:16
  26.4 1.7 %copy-start = (bf16[32,7296]{0,1:T(8,128)(2,1)S(1)}, bf16[32,7296]{0,1:T(8,128)(2,1)}, u32[]{:S(2)}) copy-start(bf16[32,7296]{0,1:T(8,128)(2,1)} %copy.15) | copy-start | bytes 1400836
  29.2 7.0 %collective-permute-start.12 = (bf16[24,3584]{1,0:T(8,128)(2,1)S(1)}, bf16[24,3584]{1,0:T(8,128)(2,1)S(1)}, u32[]{:S(2)}, u32[]{:S(2)}) collective-permute-start(bf16[24,3584]{1,0:T(8,128)(2,1)S(1)} %get-tuple-element.21), channel_id=1, source_target_pairs={{0,224},{32,0},{64,32},{96,64},{128,96},{160,128},{192,160},{224,1... | collective-permute-start | bytes 516104 | tf_op jit(solution)/shard_map/ppermute | solution.py:12
  29.4 7.4 %collective-permute-start.8 = (bf16[24,3584]{1,0:T(8,128)(2,1)S(1)}, bf16[24,3584]{1,0:T(8,128)(2,1)S(1)}, u32[]{:S(2)}, u32[]{:S(2)}) collective-permute-start(bf16[24,3584]{1,0:T(8,128)(2,1)S(1)} %get-tuple-element.21), channel_id=1, source_target_pairs={{0,32},{32,64},{64,96},{96,128},{128,160},{160,192},{192,224},{224... | collective-permute-start | bytes 516104 | tf_op jit(solution)/shard_map/ppermute | solution.py:12
  32.6 29.6 %copy-start.2 = (bf16[1,2,7168,128]{3,2,1,0:T(8,128)(2,1)S(1)}, bf16[1,2,7168,128]{3,2,1,0:T(8,128)(2,1)}, u32[]{:S(2)}) copy-start(bf16[1,2,7168,128]{3,2,1,0:T(8,128)(2,1)} %param.12) | copy-start | bytes 11010052
  32.6 8.5 %collective-permute-start.5 = (bf16[24,3712]{1,0:T(8,128)(2,1)S(1)}, bf16[24,3712]{1,0:T(8,128)(2,1)S(1)}, u32[]{:S(2)}, u32[]{:S(2)}) collective-permute-start(bf16[24,3712]{1,0:T(8,128)(2,1)S(1)} %pad_maximum_fusion.5), channel_id=1, source_target_pairs={{0,224},{32,0},{64,32},{96,64},{128,96},{160,128},{192,160},{224,1... | collective-permute-start | bytes 534536 | tf_op jit(solution)/shard_map/ppermute | solution.py:12
  32.8 9.2 %collective-permute-start.1 = (bf16[24,3712]{1,0:T(8,128)(2,1)S(1)}, bf16[24,3712]{1,0:T(8,128)(2,1)S(1)}, u32[]{:S(2)}, u32[]{:S(2)}) collective-permute-start(bf16[24,3712]{1,0:T(8,128)(2,1)S(1)} %pad_maximum_fusion.5), channel_id=1, source_target_pairs={{0,32},{32,64},{64,96},{96,128},{128,160},{160,192},{192,224},{224... | collective-permute-start | bytes 534536 | tf_op jit(solution)/shard_map/ppermute | solution.py:12
  36.2 8.6 %collective-permute-start.13 = (bf16[24,3584]{1,0:T(8,128)(2,1)S(1)}, bf16[24,3584]{1,0:T(8,128)(2,1)S(1)}, u32[]{:S(2)}, u32[]{:S(2)}) collective-permute-start(bf16[24,3584]{1,0:T(8,128)(2,1)S(1)} %collective-permute-done.12), channel_id=1, source_target_pairs={{0,224},{32,0},{64,32},{96,64},{128,96},{160,128},{192,160},{224,1... | collective-permute-start | bytes 516104 | tf_op jit(solution)/shard_map/ppermute | solution.py:12
  36.8 8.9 %collective-permute-start.9 = (bf16[24,3584]{1,0:T(8,128)(2,1)S(1)}, bf16[24,3584]{1,0:T(8,128)(2,1)S(1)}, u32[]{:S(2)}, u32[]{:S(2)}) collective-permute-start(bf16[24,3584]{1,0:T(8,128)(2,1)S(1)} %collective-permute-done.8), channel_id=1, source_target_pairs={{0,32},{32,64},{64,96},{96,128},{128,160},{160,192},{192,224},{224... | collective-permute-start | bytes 516104 | tf_op jit(solution)/shard_map/ppermute | solution.py:12
  41.1 7.5 %collective-permute-start.6 = (bf16[24,3712]{1,0:T(8,128)(2,1)S(1)}, bf16[24,3712]{1,0:T(8,128)(2,1)S(1)}, u32[]{:S(2)}, u32[]{:S(2)}) collective-permute-start(bf16[24,3712]{1,0:T(8,128)(2,1)S(1)} %collective-permute-done.5), channel_id=1, source_target_pairs={{0,224},{32,0},{64,32},{96,64},{128,96},{160,128},{192,160},{224,1... | collective-permute-start | bytes 534536 | tf_op jit(solution)/shard_map/ppermute | solution.py:12
  42.0 7.5 %collective-permute-start.2 = (bf16[24,3712]{1,0:T(8,128)(2,1)S(1)}, bf16[24,3712]{1,0:T(8,128)(2,1)S(1)}, u32[]{:S(2)}, u32[]{:S(2)}) collective-permute-start(bf16[24,3712]{1,0:T(8,128)(2,1)S(1)} %collective-permute-done.1), channel_id=1, source_target_pairs={{0,32},{32,64},{64,96},{96,128},{128,160},{160,192},{192,224},{224... | collective-permute-start | bytes 534536 | tf_op jit(solution)/shard_map/ppermute | solution.py:12
  44.8 17.3 %collective-permute-start.14 = (bf16[24,3584]{1,0:T(8,128)(2,1)S(1)}, bf16[24,3584]{1,0:T(8,128)(2,1)S(1)}, u32[]{:S(2)}, u32[]{:S(2)}) collective-permute-start(bf16[24,3584]{1,0:T(8,128)(2,1)S(1)} %collective-permute-done.13), channel_id=1, source_target_pairs={{0,224},{32,0},{64,32},{96,64},{128,96},{160,128},{192,160},{224,1... | collective-permute-start | bytes 516104 | tf_op jit(solution)/shard_map/ppermute | solution.py:12
  45.7 8.2 %collective-permute-start.10 = (bf16[24,3584]{1,0:T(8,128)(2,1)S(1)}, bf16[24,3584]{1,0:T(8,128)(2,1)S(1)}, u32[]{:S(2)}, u32[]{:S(2)}) collective-permute-start(bf16[24,3584]{1,0:T(8,128)(2,1)S(1)} %collective-permute-done.9), channel_id=1, source_target_pairs={{0,32},{32,64},{64,96},{96,128},{128,160},{160,192},{192,224},{224... | collective-permute-start | bytes 516104 | tf_op jit(solution)/shard_map/ppermute | solution.py:12
  48.6 15.8 %collective-permute-start.7 = (bf16[24,3712]{1,0:T(8,128)(2,1)S(1)}, bf16[24,3712]{1,0:T(8,128)(2,1)S(1)}, u32[]{:S(2)}, u32[]{:S(2)}) collective-permute-start(bf16[24,3712]{1,0:T(8,128)(2,1)S(1)} %collective-permute-done.6), channel_id=1, source_target_pairs={{0,224},{32,0},{64,32},{96,64},{128,96},{160,128},{192,160},{224,1... | collective-permute-start | bytes 534536 | tf_op jit(solution)/shard_map/ppermute | solution.py:12
  49.4 8.3 %collective-permute-start.3 = (bf16[24,3712]{1,0:T(8,128)(2,1)S(1)}, bf16[24,3712]{1,0:T(8,128)(2,1)S(1)}, u32[]{:S(2)}, u32[]{:S(2)}) collective-permute-start(bf16[24,3712]{1,0:T(8,128)(2,1)S(1)} %collective-permute-done.2), channel_id=1, source_target_pairs={{0,32},{32,64},{64,96},{96,128},{128,160},{160,192},{192,224},{224... | collective-permute-start | bytes 534536 | tf_op jit(solution)/shard_map/ppermute | solution.py:12
  53.9 8.2 %collective-permute-start.11 = (bf16[24,3584]{1,0:T(8,128)(2,1)S(1)}, bf16[24,3584]{1,0:T(8,128)(2,1)S(1)}, u32[]{:S(2)}, u32[]{:S(2)}) collective-permute-start(bf16[24,3584]{1,0:T(8,128)(2,1)S(1)} %collective-permute-done.10), channel_id=1, source_target_pairs={{0,32},{32,64},{64,96},{96,128},{128,160},{160,192},{192,224},{224... | collective-permute-start | bytes 516104 | tf_op jit(solution)/shard_map/ppermute | solution.py:12
  57.7 6.7 %collective-permute-start.4 = (bf16[24,3712]{1,0:T(8,128)(2,1)S(1)}, bf16[24,3712]{1,0:T(8,128)(2,1)S(1)}, u32[]{:S(2)}, u32[]{:S(2)}) collective-permute-start(bf16[24,3712]{1,0:T(8,128)(2,1)S(1)} %collective-permute-done.3), channel_id=1, source_target_pairs={{0,32},{32,64},{64,96},{96,128},{128,160},{160,192},{192,224},{224... | collective-permute-start | bytes 534536 | tf_op jit(solution)/shard_map/ppermute | solution.py:12
  65.0 1.5 %copy-start.1 = (bf16[1,128,7168]{2,1,0:T(8,128)(2,1)S(1)}, bf16[1,128,7168]{2,1,0:T(8,128)(2,1)}, u32[]{:S(2)}) copy-start(bf16[1,128,7168]{2,1,0:T(8,128)(2,1)} %param.13) | copy-start | bytes 5505028
  67.6 8.5 %collective-permute-start.22 = (bf16[24,3584]{1,0:T(8,128)(2,1)S(1)}, bf16[24,3584]{1,0:T(8,128)(2,1)S(1)}, u32[]{:S(2)}, u32[]{:S(2)}) collective-permute-start(bf16[24,3584]{1,0:T(8,128)(2,1)S(1)} %get-tuple-element.16), channel_id=1, source_target_pairs={{0,32},{32,64},{64,96},{96,128},{128,160},{160,192},{192,224},{224... | collective-permute-start | bytes 516104 | tf_op jit(solution)/shard_map/ppermute | solution.py:12
  69.5 12.4 %collective-permute-start.26 = (bf16[24,3584]{1,0:T(8,128)(2,1)S(1)}, bf16[24,3584]{1,0:T(8,128)(2,1)S(1)}, u32[]{:S(2)}, u32[]{:S(2)}) collective-permute-start(bf16[24,3584]{1,0:T(8,128)(2,1)S(1)} %get-tuple-element.17), channel_id=1, source_target_pairs={{0,224},{32,0},{64,32},{96,64},{128,96},{160,128},{192,160},{224,1... | collective-permute-start | bytes 516104 | tf_op jit(solution)/shard_map/ppermute | solution.py:12
  71.0 8.8 %collective-permute-start.15 = (bf16[24,3584]{1,0:T(8,128)(2,1)S(1)}, bf16[24,3584]{1,0:T(8,128)(2,1)S(1)}, u32[]{:S(2)}, u32[]{:S(2)}) collective-permute-start(bf16[24,3584]{1,0:T(8,128)(2,1)S(1)} %get-tuple-element.14), channel_id=1, source_target_pairs={{0,32},{32,64},{64,96},{96,128},{128,160},{160,192},{192,224},{224... | collective-permute-start | bytes 516104 | tf_op jit(solution)/shard_map/ppermute | solution.py:12
  73.3 13.4 %collective-permute-start.19 = (bf16[24,3584]{1,0:T(8,128)(2,1)S(1)}, bf16[24,3584]{1,0:T(8,128)(2,1)S(1)}, u32[]{:S(2)}, u32[]{:S(2)}) collective-permute-start(bf16[24,3584]{1,0:T(8,128)(2,1)S(1)} %get-tuple-element.15), channel_id=1, source_target_pairs={{0,224},{32,0},{64,32},{96,64},{128,96},{160,128},{192,160},{224,1... | collective-permute-start | bytes 516104 | tf_op jit(solution)/shard_map/ppermute | solution.py:12
  76.1 7.3 %collective-permute-start.23 = (bf16[24,3584]{1,0:T(8,128)(2,1)S(1)}, bf16[24,3584]{1,0:T(8,128)(2,1)S(1)}, u32[]{:S(2)}, u32[]{:S(2)}) collective-permute-start(bf16[24,3584]{1,0:T(8,128)(2,1)S(1)} %fusion.20), channel_id=1, source_target_pairs={{0,32},{32,64},{64,96},{96,128},{128,160},{160,192},{192,224},{224... | collective-permute-start | bytes 516104 | tf_op jit(solution)/shard_map/ppermute | solution.py:12
  79.8 8.3 %collective-permute-start.16 = (bf16[24,3584]{1,0:T(8,128)(2,1)S(1)}, bf16[24,3584]{1,0:T(8,128)(2,1)S(1)}, u32[]{:S(2)}, u32[]{:S(2)}) collective-permute-start(bf16[24,3584]{1,0:T(8,128)(2,1)S(1)} %fusion.27), channel_id=1, source_target_pairs={{0,32},{32,64},{64,96},{96,128},{128,160},{160,192},{192,224},{224... | collective-permute-start | bytes 516104 | tf_op jit(solution)/shard_map/ppermute | solution.py:12
  83.5 8.1 %collective-permute-start.24 = (bf16[24,3584]{1,0:T(8,128)(2,1)S(1)}, bf16[24,3584]{1,0:T(8,128)(2,1)S(1)}, u32[]{:S(2)}, u32[]{:S(2)}) collective-permute-start(bf16[24,3584]{1,0:T(8,128)(2,1)S(1)} %get-tuple-element.12), channel_id=1, source_target_pairs={{0,32},{32,64},{64,96},{96,128},{128,160},{160,192},{192,224},{224... | collective-permute-start | bytes 516104 | tf_op jit(solution)/shard_map/ppermute | solution.py:12
  85.2 7.1 %collective-permute-start.27 = (bf16[24,3584]{1,0:T(8,128)(2,1)S(1)}, bf16[24,3584]{1,0:T(8,128)(2,1)S(1)}, u32[]{:S(2)}, u32[]{:S(2)}) collective-permute-start(bf16[24,3584]{1,0:T(8,128)(2,1)S(1)} %get-tuple-element.13), channel_id=1, source_target_pairs={{0,224},{32,0},{64,32},{96,64},{128,96},{160,128},{192,160},{224,1... | collective-permute-start | bytes 516104 | tf_op jit(solution)/shard_map/ppermute | solution.py:12
  88.2 8.4 %collective-permute-start.17 = (bf16[24,3584]{1,0:T(8,128)(2,1)S(1)}, bf16[24,3584]{1,0:T(8,128)(2,1)S(1)}, u32[]{:S(2)}, u32[]{:S(2)}) collective-permute-start(bf16[24,3584]{1,0:T(8,128)(2,1)S(1)} %get-tuple-element.8), channel_id=1, source_target_pairs={{0,32},{32,64},{64,96},{96,128},{128,160},{160,192},{192,224},{224... | collective-permute-start | bytes 516104 | tf_op jit(solution)/shard_map/ppermute | solution.py:12
  89.7 8.8 %collective-permute-start.20 = (bf16[24,3584]{1,0:T(8,128)(2,1)S(1)}, bf16[24,3584]{1,0:T(8,128)(2,1)S(1)}, u32[]{:S(2)}, u32[]{:S(2)}) collective-permute-start(bf16[24,3584]{1,0:T(8,128)(2,1)S(1)} %get-tuple-element.9), channel_id=1, source_target_pairs={{0,224},{32,0},{64,32},{96,64},{128,96},{160,128},{192,160},{224,1... | collective-permute-start | bytes 516104 | tf_op jit(solution)/shard_map/ppermute | solution.py:12
  92.5 9.4 %collective-permute-start.25 = (bf16[24,3584]{1,0:T(8,128)(2,1)S(1)}, bf16[24,3584]{1,0:T(8,128)(2,1)S(1)}, u32[]{:S(2)}, u32[]{:S(2)}) collective-permute-start(bf16[24,3584]{1,0:T(8,128)(2,1)S(1)} %get-tuple-element.10), channel_id=1, source_target_pairs={{0,32},{32,64},{64,96},{96,128},{128,160},{160,192},{192,224},{224... | collective-permute-start | bytes 516104 | tf_op jit(solution)/shard_map/ppermute | solution.py:12
  96.6 5.4 %collective-permute-start.28 = (bf16[24,3584]{1,0:T(8,128)(2,1)S(1)}, bf16[24,3584]{1,0:T(8,128)(2,1)S(1)}, u32[]{:S(2)}, u32[]{:S(2)}) collective-permute-start(bf16[24,3584]{1,0:T(8,128)(2,1)S(1)} %get-tuple-element.11), channel_id=1, source_target_pairs={{0,224},{32,0},{64,32},{96,64},{128,96},{160,128},{192,160},{224,1... | collective-permute-start | bytes 516104 | tf_op jit(solution)/shard_map/ppermute | solution.py:12
  98.6 6.2 %collective-permute-start.18 = (bf16[24,3584]{1,0:T(8,128)(2,1)S(1)}, bf16[24,3584]{1,0:T(8,128)(2,1)S(1)}, u32[]{:S(2)}, u32[]{:S(2)}) collective-permute-start(bf16[24,3584]{1,0:T(8,128)(2,1)S(1)} %get-tuple-element.6), channel_id=1, source_target_pairs={{0,32},{32,64},{64,96},{96,128},{128,160},{160,192},{192,224},{224... | collective-permute-start | bytes 516104 | tf_op jit(solution)/shard_map/ppermute | solution.py:12
  101.8 5.4 %collective-permute-start.21 = (bf16[24,3584]{1,0:T(8,128)(2,1)S(1)}, bf16[24,3584]{1,0:T(8,128)(2,1)S(1)}, u32[]{:S(2)}, u32[]{:S(2)}) collective-permute-start(bf16[24,3584]{1,0:T(8,128)(2,1)S(1)} %get-tuple-element.7), channel_id=1, source_target_pairs={{0,224},{32,0},{64,32},{96,64},{128,96},{160,128},{192,160},{224,1... | collective-permute-start | bytes 516104 | tf_op jit(solution)/shard_map/ppermute | solution.py:12
  108.3 1.9 %collective-permute-start.29 = (bf16[32,7168]{1,0:T(8,128)(2,1)S(1)}, bf16[32,7168]{1,0:T(8,128)(2,1)S(1)}, u32[]{:S(2)}, u32[]{:S(2)}) collective-permute-start(bf16[32,7168]{1,0:T(8,128)(2,1)S(1)} %slice.379), channel_id=1, source_target_pairs={{0,1},{1,0},{2,3},{3,2},{4,5},{5,4},{6,7},{7,6},{8,9},{9,8},{10,11... | collective-permute-start | bytes 1376264 | tf_op jit(solution)/shard_map/ppermute | solution.py:16
  111.2 14.9 %all-to-all-start.1 = ((bf16[16,2,7168]{2,1,0:T(2,128)(2,1)}), bf16[16,2,7168]{2,1,0:T(2,128)(2,1)S(1)}, u32[]{:S(2)}, u32[]{:S(2)}) async-start(bf16[16,2,7168]{2,1,0:T(2,128)(2,1)} %reshape.57), calls=%async_computation.1 | async-start | bytes 917504 | tf_op jit(solution)/shard_map/all_to_all | solution.py:138

commit v2 on v1

v2 whole, which is shorter than its diff:
```python
import functools

import jax
import jax.numpy as jnp
from jax import lax
from jax.experimental import pallas as pl
from jax.experimental.pallas import tpu as pltpu
from jax.sharding import PartitionSpec as P

F32, BF16 = jnp.float32, jnp.bfloat16
MOST = 24
META = 128
CHUNKS = 4
SUM_CHUNKS = 2


def core_swap(value, groups):
    return lax.ppermute(value, "expert", [(i, i ^ 1) for i in range(groups)])


def core_ring(value, sign, count, groups):
    pairs = []
    for a in range(count):
        for e in range(groups):
            step = sign if e % 2 == 0 else -sign
            pairs.append((a * groups + e, (a + step) % count * groups + e))
    return lax.ppermute(value, ("attn", "expert"), pairs)


def gather_ring(chunks, count, groups):
    half = count // 2
    moving = [[c] for c in chunks]
    for step in range(1, half + 1):
        for got in moving:
            sending = got[-1] if step < half else got[-1][:MOST]
            got.append(core_ring(sending, 1, count, groups))
    other = [
        core_swap(jnp.concatenate([b[MOST:] for b in got[1:half]], 0), groups) for got in moving
    ]
    return moving, other


def reduce_ring(chunks, count, groups):
    half = count // 2
    fore = [f(half).astype(BF16) for f in chunks]
    back = [f(count - half + 1).astype(BF16) for f in chunks]
    for step in range(half - 1, 0, -1):
        for c, f in enumerate(chunks):
            fore[c] = (core_ring(fore[c], 1, count, groups).astype(F32) + f(step)).astype(BF16)
            if step > 1:
                back[c] = (
                    core_ring(back[c], -1, count, groups).astype(F32) + f(count - step + 1)
                ).astype(BF16)
    return [
        (
            f(0)
            + core_ring(fore[c], 1, count, groups).astype(F32)
            + core_ring(back[c], -1, count, groups).astype(F32)
        ).astype(BF16)
        for c, f in enumerate(chunks)
    ]


def prep_kernel(top, *refs):
    sources, sent, held, sem = refs[:4], refs[4], refs[5:9], refs[9]
    copies = [pltpu.make_async_copy(s, h, sem.at[i]) for i, (s, h) in enumerate(zip(sources, held))]
    for copy in copies:
        copy.start()
    for copy in copies:
        copy.wait()
    tokens, ids, replica, weight = held
    rows, width = tokens.shape
    sent[:, :width] = tokens[...]
    high = weight[...].astype(BF16).astype(F32)
    middle = (weight[...] - high).astype(BF16).astype(F32)
    low = weight[...] - high - middle
    lane = lax.broadcasted_iota(jnp.int32, (rows, META), 1)
    meta = jnp.zeros((rows, META), F32)
    for part, value in enumerate([ids[...].astype(F32), replica[...].astype(F32), high, middle, low]):
        for k in range(top):
            meta = jnp.where(lane == part * top + k, value[:, k : k + 1], meta)
    sent[:, width:] = meta.astype(BF16)


def pack_kernel(top, span, near, far, plan, *outs):
    packed, mix, spare_plan, sem = outs[:CHUNKS], outs[CHUNKS], outs[CHUNKS + 1], outs[CHUNKS + 2]
    plan_copy = pltpu.make_async_copy(plan, spare_plan, sem)
    plan_copy.start()
    half = near.shape[0]
    total = 2 * half
    width = span * CHUNKS
    me = lax.axis_index("expert")
    info = jnp.concatenate([near[:, width:], far[:, width:]], 0)
    source = lax.broadcasted_iota(jnp.int32, (META, META), 0)
    lane = lax.broadcasted_iota(jnp.int32, (META, META), 1)

    def part(number):
        move = ((source == lane + number * top) & (lane < top)).astype(BF16)
        return jnp.dot(info, move, preferred_element_type=F32)

    ids, copies = part(0), part(1)
    weights = [part(2), part(3), part(4)]
    valid = lax.broadcasted_iota(jnp.int32, (total, META), 1) < top
    ones = jnp.ones((8, META), BF16)

    def along(value):
        return lax.dot_general(
            ones, value.astype(BF16), (((1,), (1,)), ((), ())), preferred_element_type=F32
        )

    turn = jnp.where(me % 2 == 0, 0, half)
    first = lax.broadcasted_iota(jnp.int32, (total, total), 0)
    second = lax.broadcasted_iota(jnp.int32, (total, total), 1)
    earlier = ((first + turn) % total < (second + turn) % total).astype(BF16)
    slot = lax.broadcasted_iota(jnp.int32, (MOST, total), 0).astype(F32)
    tail_lane = lax.broadcasted_iota(jnp.int32, (MOST, META), 1)
    chosen, tails = [], []
    plan_copy.wait()
    for which in range(2):
        expert = me if which == 0 else me ^ 1
        named = valid & (ids == expert.astype(F32))
        spare = spare_plan[expert].astype(F32)
        hit = along(named.astype(F32))
        rank = jnp.dot(hit.astype(BF16), earlier, preferred_element_type=F32)
        pick = jnp.where((hit[:1] > 0.0) & (rank[:1] == slot), 1.0, 0.0)
        chosen.append(pick)
        own_count = jnp.sum((named & (copies == 0.0)).astype(F32))
        spare_hit = valid & (ids == spare) & (copies == 1.0)
        spare_count = jnp.sum(spare_hit.astype(F32))
        tails.append(
            jnp.where(tail_lane == 0, own_count, jnp.where(tail_lane == 1, spare_count, 0.0))
        )
        if which == 0:
            coef = sum(along(jnp.where(named, w, 0.0)) for w in weights)
            value = pick * coef[:1]
            high = value.astype(BF16)
            mix[0] = high
            mix[1] = (value - high.astype(F32)).astype(BF16)
    pick = jnp.concatenate(chosen, 0).astype(BF16)
    for c in range(CHUNKS):
        at = slice(c * span, (c + 1) * span)
        value = jnp.dot(pick[:, :half], near[:, at], preferred_element_type=F32)
        value += jnp.dot(pick[:, half:], far[:, at], preferred_element_type=F32)
        packed[c][:, :span] = value.astype(BF16)
    packed[0][:, span:] = jnp.concatenate(tails, 0).astype(BF16)


def body(tokens, expert_ids, replica, route_weight, spare_plan, w_in, w_down):
    rows, width = tokens.shape
    top = expert_ids.shape[1]
    count = lax.axis_size("attn")
    groups = lax.axis_size("expert")
    peers = groups // 2
    half = count // 2
    same_core = [[core + 2 * j for j in range(peers)] for core in range(2)]
    vmem, anywhere = pl.BlockSpec(memory_space=pltpu.VMEM), pl.BlockSpec(memory_space=pltpu.HBM)
    routed = (tokens, expert_ids, replica, route_weight)
    grant = pltpu.CompilerParams(vmem_limit_bytes=16 * 2**20)

    sent = pl.pallas_call(
        functools.partial(prep_kernel, top),
        out_shape=jax.ShapeDtypeStruct((rows, width + META), BF16),
        in_specs=[anywhere] * 4,
        out_specs=vmem,
        scratch_shapes=[pltpu.VMEM(v.shape, v.dtype) for v in routed]
        + [pltpu.SemaphoreType.DMA((4,))],
        compiler_params=grant,
    )(*routed)

    spread = jnp.broadcast_to(sent[None], (peers, rows, width + META))
    near = lax.all_to_all(spread, "expert", 0, 0, axis_index_groups=same_core, tiled=True)
    near = lax.optimization_barrier(near.reshape(peers * rows, width + META))
    far = core_swap(near, groups)
    total = 2 * peers * rows

    span = width // CHUNKS
    cols = [slice(c * span, (c + 1) * span) for c in range(CHUNKS)]
    shapes = [
        jax.ShapeDtypeStruct((2 * MOST, span + (META if c == 0 else 0)), BF16)
        for c in range(CHUNKS)
    ]
    *parts, mix = pl.pallas_call(
        functools.partial(pack_kernel, top, span),
        out_shape=shapes + [jax.ShapeDtypeStruct((2, MOST, total), BF16)],
        in_specs=[vmem, vmem, anywhere],
        out_specs=[vmem] * (CHUNKS + 1),
        scratch_shapes=[
            pltpu.SMEM(spare_plan.shape, spare_plan.dtype), pltpu.SemaphoreType.DMA(())
        ],
        compiler_params=grant,
    )(near, far, spare_plan)

    moving, other = gather_ring(parts, count, groups)

    load = sum(b[0, span : span + 2].astype(F32) for b in moving[0])
    load += jnp.sum(other[0].reshape(half - 1, MOST, -1)[:, 0, span : span + 2].astype(F32), 0)
    slot_load = load.astype(jnp.int32)[None]

    gathered = [
        jnp.concatenate([b[:MOST, :span] for b in got] + [handed[:, :span]], 0)
        for got, handed in zip(moving, other)
    ]

    def up(which):
        return sum(
            jnp.dot(x, w_in[0, which, cols[c]], preferred_element_type=F32)
            for c, x in enumerate(gathered)
        )

    hidden = (jax.nn.silu(up(0)) * up(1)).astype(BF16)
    place_of = {0: 0}
    for s in range(1, half + 1):
        place_of[count - s] = s
    for s in range(1, half):
        place_of[s] = half + s
    wide = width // SUM_CHUNKS
    down = [
        jnp.dot(
            hidden, w_down[0][:, c * wide : (c + 1) * wide], preferred_element_type=F32
        )
        for c in range(SUM_CHUNKS)
    ]

    def block(c):
        return lambda s: down[c][place_of[s] * MOST : (place_of[s] + 1) * MOST]

    summed = jnp.concatenate(
        reduce_ring([block(c) for c in range(SUM_CHUNKS)], count, groups), 1
    )

    share = sum(
        lax.dot_general(mix[i], summed, (((0,), (0,)), ((), ())), preferred_element_type=F32)
        for i in range(2)
    )
    near_count = peers * rows
    swapped = core_swap(share[near_count:].astype(BF16), groups)
    both = (share[:near_count] + swapped.astype(F32)).astype(BF16)
    back = lax.all_to_all(
        both.reshape(peers, rows, width), "expert", 0, 0, axis_index_groups=same_core, tiled=True
    )
    layer_output = jnp.sum(back.astype(F32), 0).astype(BF16)
    return layer_output, slot_load


def solution(mesh):
    placed = (
        P(("attn", "expert"), None),
        P(("attn", "expert"), None),
        P(("attn", "expert"), None),
        P(("attn", "expert"), None),
        P(),
        P("expert", None, None, "attn"),
        P("expert", "attn", None),
    )
    return jax.shard_map(
        body,
        mesh=mesh,
        in_specs=placed,
        out_specs=(P(("attn", "expert"), None), P("expert", None)),
        check_vma=False,
    )
```

time: 129 us -> 124 us (0.961)
  starting transfers between devices: 48.9 us -> 58.4 us
  waiting for transfers between devices: 38 us -> 31.7 us
  other arithmetic: 8.47 us -> 2.22 us
  local copies, waits for them, and re-layouts: 7.36 us -> 5.65 us
  Pallas kernels: 0 us -> 1.68 us
    ppermute x28 -> x30, waiting for transfers between devices: 26.6 us -> 17.2 us  [core_ring(): return lax.ppermute(value, ('attn', 'expert'), pairs)]
    ppermute x28 -> x30, starting transfers between devices: 45.2 us -> 54.1 us  [core_ring(): return lax.ppermute(value, ('attn', 'expert'), pairs)]
    unnamed x20 -> x23, local copies, waits for them, and re-layouts: 1.13 us -> 3.94 us
    convert_element_type x13 -> x9, other arithmetic: 2.74 us -> 0.58 us  [the longest x6 0.38 us: reduce_ring(): (core_ring(fore[c], 1, count, groups).astype(F32) + f(step)).astype(BF16)]
    ppermute x1 -> x0, local copies, waits for them, and re-layouts: 1.85 us -> none  [core_swap(): return lax.ppermute(value, 'expert', [(i, i ^ 1) for i in range(groups)])]
    ppermute x2 -> x6, waiting for transfers between devices: 1.81 us -> 3.63 us  [core_swap(): return lax.ppermute(value, 'expert', [(i, i ^ 1) for i in range(groups)])]
    pallas_call x0 -> x2, Pallas kernels: none -> 1.68 us  [the longest x1 1.52 us: body(): pl.pallas_call(functools.partial(pack_kernel, top, span), out_shape=shape...]
    reshape x3 -> x2, local copies, waits for them, and re-layouts: 2.53 us -> 1.13 us  [the longest x1 0.95 us: body(): both.reshape(peers, rows, width)]
  transfers between devices with their start and end apart: 31 -> 37, of which waited for: 22 -> 16; matrix products, arithmetic and copies ran while one was open for 5% -> 3% of each run, Pallas kernels for 0% -> 0%
where the time goes in v2:
time: 124 us; the launch traced here: 123 us
  starting transfers between devices  58.4 us (47%)
  waiting for transfers between devices  31.7 us (26%)
  blocking collectives  17.7 us (14%)
  local copies, waits for them, and re-layouts  5.65 us (5%)
  matrix products  4.55 us (4%)
  other arithmetic  2.22 us (2%)
  Pallas kernels  1.68 us (1%)
    ppermute x30, starting transfers between devices, core_ring(): return lax.ppermute(value, ('attn', 'expert'), pairs)  54.1 us
    all_to_all x1, blocking collectives, body(): lax.all_to_all(spread, 'expert', 0, 0, axis_index_groups=same_core, tiled...  17.7 us
    ppermute x30, waiting for transfers between devices, core_ring(): return lax.ppermute(value, ('attn', 'expert'), pairs)  17.2 us
    all_to_all x1, waiting for transfers between devices, body(): lax.all_to_all(both.reshape(peers, rows, width), 'expert', 0, 0, axis_ind...  10.8 us
    unnamed x23, local copies, waits for them, and re-layouts  3.94 us
    ppermute x6, waiting for transfers between devices, core_swap(): return lax.ppermute(value, 'expert', [(i, i ^ 1) for i in range(groups)])  3.63 us
    all_to_all x1, starting transfers between devices, body(): lax.all_to_all(both.reshape(peers, rows, width), 'expert', 0, 0, axis_ind...  3.56 us
    dot_general x8, matrix products, up(): jnp.dot(x, w_in[0, which, cols[c]], preferred_element_type=F32)  2.71 us
  transfers between devices with their start and end apart: 37, of which 16 were waited for; matrix products, arithmetic and copies ran while one was open for 3% of the time, Pallas kernels for 0%

profile of v2, /device:TPU:64, one launch (start us, length us, event | category | flops | bytes accessed | tf_op | source)
XLA Modules:
  0.0 123.0 jit_solution(2654111944584637571)
XLA Ops:
  0.6 0.7 copy-done
  1.4 0.7 copy-done.1
  2.1 0.7 copy-done.2
  2.7 0.7 copy-done.3
  3.6 0.2 broadcast_in_dim.2
  3.8 17.7 %all_to_all.10 = bf16[16,2,7296]{2,1,0:T(2,128)(2,1)S(1)} all-to-all(bf16[16,2,7296]{2,1,0:T(2,128)(2,1)S(1)} %broadcast_in_dim.2), channel_id=1, replica_groups={{0,2,4,6,8,10,12,14,16,18,20,22,24,26,28,30},{1,3,5,7,9,11,13,15,17,19,..., dimensions={0} | all-to-all | bytes 933888 | tf_op jit(solution)/shard_map/all_to_all | solution.py:171
  21.8 1.8 %collective-permute-done.far = bf16[32,7296]{1,0:T(8,128)(2,1)S(1)} collective-permute-done((bf16[32,7296]{1,0:T(8,128)(2,1)S(1)}, bf16[32,7296]{1,0:T(8,128)(2,1)S(1)}, u32[]{:S(2)}, u32[]{:S(2)}) %collective-permute-start) | collective-permute-done | bytes 466976 | tf_op jit(solution)/shard_map/ppermute | solution.py:18
  23.7 0.7 copy-done.4
  24.3 1.5 %shard_map.87 = (bf16[48,1920]{1,0:T(8,128)(2,1)S(1)}, bf16[48,1792]{1,0:T(8,128)(2,1)S(1)}, bf16[48,1792]{1,0:T(8,128)(2,1)S(1)}, bf16[48,1792]{1,0:T(8,128)(2,1)S(1)}, bf16[2,24,64]{2,1,0:T(8,128)(2,1)S(1)}) custom-call(bf16[32,7296]{1,0:T(8,128)(2,1)S(1)} %reshape.16.near, bf16[32,7296]{1,0:T(8,128)(2,1)S(1)} %collective-permute-done.far, s32[32]{0:T(128)S(1)} %copy-done.4), custom_call_target="tpu_custom_call" | custom-call | tf_op jit(solution)/shard_map/pallas_call | solution.py:182
  25.8 2.0 %collective-permute-start.6 = (bf16[48,1792]{1,0:T(8,128)(2,1)S(1)}, bf16[48,1792]{1,0:T(8,128)(2,1)S(1)}, u32[]{:S(2)}, u32[]{:S(2)}) collective-permute-start(bf16[48,1792]{1,0:T(8,128)(2,1)S(1)} %get-tuple-element.9), channel_id=1, source_target_pairs={{0,32},{1,225},{2,34},{3,227},{4,36},{5,229},{6,38},{7,231},{8,40}... | collective-permute-start | bytes 516104 | tf_op jit(solution)/shard_map/ppermute | solution.py:27
  27.8 3.1 %collective-permute-start.1 = (bf16[48,1920]{1,0:T(8,128)(2,1)S(1)}, bf16[48,1920]{1,0:T(8,128)(2,1)S(1)}, u32[]{:S(2)}, u32[]{:S(2)}) collective-permute-start(bf16[48,1920]{1,0:T(8,128)(2,1)S(1)} %get-tuple-element.8), channel_id=1, source_target_pairs={{0,32},{1,225},{2,34},{3,227},{4,36},{5,229},{6,38},{7,231},{8,40}... | collective-permute-start | bytes 552968 | tf_op jit(solution)/shard_map/ppermute | solution.py:27
  31.0 1.1 collective-permute-start.11
  32.1 1.0 collective-permute-start.16
  33.1 1.1 collective-permute-start.7
  34.2 2.2 %collective-permute-done.11 = bf16[48,1792]{1,0:T(8,128)(2,1)S(1)} collective-permute-done((bf16[48,1792]{1,0:T(8,128)(2,1)S(1)}, bf16[48,1792]{1,0:T(8,128)(2,1)S(1)}, u32[]{:S(2)}, u32[]{:S(2)}) %collective-permute-start.11) | collective-permute-done | bytes 172064 | tf_op jit(solution)/shard_map/ppermute | solution.py:27
  36.5 1.9 %collective-permute-start.12 = (bf16[48,1792]{1,0:T(8,128)(2,1)S(1)}, bf16[48,1792]{1,0:T(8,128)(2,1)S(1)}, u32[]{:S(2)}, u32[]{:S(2)}) collective-permute-start(bf16[48,1792]{1,0:T(8,128)(2,1)S(1)} %collective-permute-done.11), channel_id=1, source_target_pairs={{0,32},{1,225},{2,34},{3,227},{4,36},{5,229},{6,38},{7,231},{8,40}... | collective-permute-start | bytes 516104 | tf_op jit(solution)/shard_map/ppermute | solution.py:27
  38.3 3.1 %collective-permute-start.17 = (bf16[48,1792]{1,0:T(8,128)(2,1)S(1)}, bf16[48,1792]{1,0:T(8,128)(2,1)S(1)}, u32[]{:S(2)}, u32[]{:S(2)}) collective-permute-start(bf16[48,1792]{1,0:T(8,128)(2,1)S(1)} %collective-permute-done.16), channel_id=1, source_target_pairs={{0,32},{1,225},{2,34},{3,227},{4,36},{5,229},{6,38},{7,231},{8,40}... | collective-permute-start | bytes 516104 | tf_op jit(solution)/shard_map/ppermute | solution.py:27
  41.5 1.9 %collective-permute-start.2 = (bf16[48,1920]{1,0:T(8,128)(2,1)S(1)}, bf16[48,1920]{1,0:T(8,128)(2,1)S(1)}, u32[]{:S(2)}, u32[]{:S(2)}) collective-permute-start(bf16[48,1920]{1,0:T(8,128)(2,1)S(1)} %collective-permute-done.1), channel_id=1, source_target_pairs={{0,32},{1,225},{2,34},{3,227},{4,36},{5,229},{6,38},{7,231},{8,40}... | collective-permute-start | bytes 552968 | tf_op jit(solution)/shard_map/ppermute | solution.py:27
  43.5 1.6 %collective-permute-start.13 = (bf16[48,1792]{1,0:T(8,128)(2,1)S(1)}, bf16[48,1792]{1,0:T(8,128)(2,1)S(1)}, u32[]{:S(2)}, u32[]{:S(2)}) collective-permute-start(bf16[48,1792]{1,0:T(8,128)(2,1)S(1)} %collective-permute-done.12), channel_id=1, source_target_pairs={{0,32},{1,225},{2,34},{3,227},{4,36},{5,229},{6,38},{7,231},{8,40}... | collective-permute-start | bytes 516104 | tf_op jit(solution)/shard_map/ppermute | solution.py:27
  45.1 2.9 %collective-permute-start.18 = (bf16[48,1792]{1,0:T(8,128)(2,1)S(1)}, bf16[48,1792]{1,0:T(8,128)(2,1)S(1)}, u32[]{:S(2)}, u32[]{:S(2)}) collective-permute-start(bf16[48,1792]{1,0:T(8,128)(2,1)S(1)} %collective-permute-done.17), channel_id=1, source_target_pairs={{0,32},{1,225},{2,34},{3,227},{4,36},{5,229},{6,38},{7,231},{8,40}... | collective-permute-start | bytes 516104 | tf_op jit(solution)/shard_map/ppermute | solution.py:27
  48.1 1.9 %collective-permute-start.3 = (bf16[48,1920]{1,0:T(8,128)(2,1)S(1)}, bf16[48,1920]{1,0:T(8,128)(2,1)S(1)}, u32[]{:S(2)}, u32[]{:S(2)}) collective-permute-start(bf16[48,1920]{1,0:T(8,128)(2,1)S(1)} %collective-permute-done.2), channel_id=1, source_target_pairs={{0,32},{1,225},{2,34},{3,227},{4,36},{5,229},{6,38},{7,231},{8,40}... | collective-permute-start | bytes 552968 | tf_op jit(solution)/shard_map/ppermute | solution.py:27
  50.1 2.0 %collective-permute-start.9 = (bf16[24,1792]{1,0:T(8,128)(2,1)S(1)}, bf16[24,1792]{1,0:T(8,128)(2,1)S(1)}, u32[]{:S(2)}, u32[]{:S(2)}) collective-permute-start(bf16[24,1792]{1,0:T(8,128)(2,1)S(1)} %get-tuple-element.32), channel_id=1, source_target_pairs={{0,32},{1,225},{2,34},{3,227},{4,36},{5,229},{6,38},{7,231},{8,40}... | collective-permute-start | bytes 258056 | tf_op jit(solution)/shard_map/ppermute | solution.py:27
  52.0 0.3 collective-permute-start.10
  52.4 1.8 %collective-permute-start.14 = (bf16[24,1792]{1,0:T(8,128)(2,1)S(1)}, bf16[24,1792]{1,0:T(8,128)(2,1)S(1)}, u32[]{:S(2)}, u32[]{:S(2)}) collective-permute-start(bf16[24,1792]{1,0:T(8,128)(2,1)S(1)} %get-tuple-element.39), channel_id=1, source_target_pairs={{0,32},{1,225},{2,34},{3,227},{4,36},{5,229},{6,38},{7,231},{8,40}... | collective-permute-start | bytes 258056 | tf_op jit(solution)/shard_map/ppermute | solution.py:27
  54.6 1.8 %collective-permute-start.19 = (bf16[24,1792]{1,0:T(8,128)(2,1)S(1)}, bf16[24,1792]{1,0:T(8,128)(2,1)S(1)}, u32[]{:S(2)}, u32[]{:S(2)}) collective-permute-start(bf16[24,1792]{1,0:T(8,128)(2,1)S(1)} %get-tuple-element.46), channel_id=1, source_target_pairs={{0,32},{1,225},{2,34},{3,227},{4,36},{5,229},{6,38},{7,231},{8,40}... | collective-permute-start | bytes 258056 | tf_op jit(solution)/shard_map/ppermute | solution.py:27
  56.6 0.3 collective-permute-done.14
  56.9 2.7 %collective-permute-start.4 = (bf16[24,1920]{1,0:T(8,128)(2,1)S(1)}, bf16[24,1920]{1,0:T(8,128)(2,1)S(1)}, u32[]{:S(2)}, u32[]{:S(2)}) collective-permute-start(bf16[24,1920]{1,0:T(8,128)(2,1)S(1)} %get-tuple-element.25), channel_id=1, source_target_pairs={{0,32},{1,225},{2,34},{3,227},{4,36},{5,229},{6,38},{7,231},{8,40}... | collective-permute-start | bytes 276488 | tf_op jit(solution)/shard_map/ppermute | solution.py:27
  59.7 2.0 %collective-permute-done.4 = bf16[24,1920]{1,0:T(8,128)(2,1)S(1)} collective-permute-done((bf16[24,1920]{1,0:T(8,128)(2,1)S(1)}, bf16[24,1920]{1,0:T(8,128)(2,1)S(1)}, u32[]{:S(2)}, u32[]{:S(2)}) %collective-permute-start.4) | collective-permute-done | bytes 92192 | tf_op jit(solution)/shard_map/ppermute | solution.py:27
  61.8 0.3 fusion.13
  62.2 0.3 fusion.20
  62.5 0.3 fusion.11
  62.9 0.3 fusion.18
  63.3 0.3 fusion.9
  63.6 0.3 fusion.16
  64.0 0.3 fusion.2
  64.3 0.3 multiply_convert_fusion
  64.7 0.4 copy-done.6
  65.1 0.5 fusion.71
  65.6 0.5 fusion.72
  66.2 2.5 %collective-permute-start.28 = (bf16[24,3584]{1,0:T(8,128)(2,1)S(1)}, bf16[24,3584]{1,0:T(8,128)(2,1)S(1)}, u32[]{:S(2)}, u32[]{:S(2)}) collective-permute-start(bf16[24,3584]{1,0:T(8,128)(2,1)S(1)} %get-tuple-element.22), channel_id=1, source_target_pairs={{0,32},{1,225},{2,34},{3,227},{4,36},{5,229},{6,38},{7,231},{8,40}... | collective-permute-start | bytes 516104 | tf_op jit(solution)/shard_map/ppermute | solution.py:27
  68.7 3.0 %collective-permute-start.21 = (bf16[24,3584]{1,0:T(8,128)(2,1)S(1)}, bf16[24,3584]{1,0:T(8,128)(2,1)S(1)}, u32[]{:S(2)}, u32[]{:S(2)}) collective-permute-start(bf16[24,3584]{1,0:T(8,128)(2,1)S(1)} %get-tuple-element.20), channel_id=1, source_target_pairs={{0,32},{1,225},{2,34},{3,227},{4,36},{5,229},{6,38},{7,231},{8,40}... | collective-permute-start | bytes 516104 | tf_op jit(solution)/shard_map/ppermute | solution.py:27
  71.7 1.7 %collective-permute-done.28 = bf16[24,3584]{1,0:T(8,128)(2,1)S(1)} collective-permute-done((bf16[24,3584]{1,0:T(8,128)(2,1)S(1)}, bf16[24,3584]{1,0:T(8,128)(2,1)S(1)}, u32[]{:S(2)}, u32[]{:S(2)}) %collective-permute-start.28) | collective-permute-done | bytes 172064 | tf_op jit(solution)/shard_map/ppermute | solution.py:27
  73.4 2.9 %collective-permute-start.29 = (bf16[24,3584]{1,0:T(8,128)(2,1)S(1)}, bf16[24,3584]{1,0:T(8,128)(2,1)S(1)}, u32[]{:S(2)}, u32[]{:S(2)}) collective-permute-start(bf16[24,3584]{1,0:T(8,128)(2,1)S(1)} %fusion.35), channel_id=1, source_target_pairs={{0,32},{1,225},{2,34},{3,227},{4,36},{5,229},{6,38},{7,231},{8,40}... | collective-permute-start | bytes 516104 | tf_op jit(solution)/shard_map/ppermute | solution.py:27
  76.3 0.4 collective-permute-done.21
  76.8 3.4 %collective-permute-start.22 = (bf16[24,3584]{1,0:T(8,128)(2,1)S(1)}, bf16[24,3584]{1,0:T(8,128)(2,1)S(1)}, u32[]{:S(2)}, u32[]{:S(2)}) collective-permute-start(bf16[24,3584]{1,0:T(8,128)(2,1)S(1)} %fusion.42), channel_id=1, source_target_pairs={{0,32},{1,225},{2,34},{3,227},{4,36},{5,229},{6,38},{7,231},{8,40}... | collective-permute-start | bytes 516104 | tf_op jit(solution)/shard_map/ppermute | solution.py:27
  80.2 3.6 %collective-permute-start.30 = (bf16[24,3584]{1,0:T(8,128)(2,1)S(1)}, bf16[24,3584]{1,0:T(8,128)(2,1)S(1)}, u32[]{:S(2)}, u32[]{:S(2)}) collective-permute-start(bf16[24,3584]{1,0:T(8,128)(2,1)S(1)} %get-tuple-element.18), channel_id=1, source_target_pairs={{0,32},{1,225},{2,34},{3,227},{4,36},{5,229},{6,38},{7,231},{8,40}... | collective-permute-start | bytes 516104 | tf_op jit(solution)/shard_map/ppermute | solution.py:27
  83.9 3.3 %collective-permute-start.23 = (bf16[24,3584]{1,0:T(8,128)(2,1)S(1)}, bf16[24,3584]{1,0:T(8,128)(2,1)S(1)}, u32[]{:S(2)}, u32[]{:S(2)}) collective-permute-start(bf16[24,3584]{1,0:T(8,128)(2,1)S(1)} %get-tuple-element.14), channel_id=1, source_target_pairs={{0,32},{1,225},{2,34},{3,227},{4,36},{5,229},{6,38},{7,231},{8,40}... | collective-permute-start | bytes 516104 | tf_op jit(solution)/shard_map/ppermute | solution.py:27
  87.2 0.7 collective-permute-done.30
  87.9 3.5 %collective-permute-done.33 = bf16[24,3584]{1,0:T(8,128)(2,1)S(1)} collective-permute-done((bf16[24,3584]{1,0:T(8,128)(2,1)S(1)}, bf16[24,3584]{1,0:T(8,128)(2,1)S(1)}, u32[]{:S(2)}, u32[]{:S(2)}) %collective-permute-start.33) | collective-permute-done | bytes 172064 | tf_op jit(solution)/shard_map/ppermute | solution.py:27
  91.5 2.9 %collective-permute-start.31 = (bf16[24,3584]{1,0:T(8,128)(2,1)S(1)}, bf16[24,3584]{1,0:T(8,128)(2,1)S(1)}, u32[]{:S(2)}, u32[]{:S(2)}) collective-permute-start(bf16[24,3584]{1,0:T(8,128)(2,1)S(1)} %get-tuple-element.16), channel_id=1, source_target_pairs={{0,32},{1,225},{2,34},{3,227},{4,36},{5,229},{6,38},{7,231},{8,40}... | collective-permute-start | bytes 516104 | tf_op jit(solution)/shard_map/ppermute | solution.py:27
  94.4 0.7 collective-permute-done.26
  95.2 2.6 %collective-permute-start.24 = (bf16[24,3584]{1,0:T(8,128)(2,1)S(1)}, bf16[24,3584]{1,0:T(8,128)(2,1)S(1)}, u32[]{:S(2)}, u32[]{:S(2)}) collective-permute-start(bf16[24,3584]{1,0:T(8,128)(2,1)S(1)} %get-tuple-element.12), channel_id=1, source_target_pairs={{0,32},{1,225},{2,34},{3,227},{4,36},{5,229},{6,38},{7,231},{8,40}... | collective-permute-start | bytes 516104 | tf_op jit(solution)/shard_map/ppermute | solution.py:27
  97.7 0.5 collective-permute-done.31
  98.2 1.6 %collective-permute-done.34 = bf16[24,3584]{1,0:T(8,128)(2,1)S(1)} collective-permute-done((bf16[24,3584]{1,0:T(8,128)(2,1)S(1)}, bf16[24,3584]{1,0:T(8,128)(2,1)S(1)}, u32[]{:S(2)}, u32[]{:S(2)}) %collective-permute-start.34) | collective-permute-done | bytes 172064 | tf_op jit(solution)/shard_map/ppermute | solution.py:27
  99.8 0.8 collective-permute-done.24
  100.7 2.5 %collective-permute-done.27 = bf16[24,3584]{1,0:T(8,128)(2,1)S(1)} collective-permute-done((bf16[24,3584]{1,0:T(8,128)(2,1)S(1)}, bf16[24,3584]{1,0:T(8,128)(2,1)S(1)}, u32[]{:S(2)}, u32[]{:S(2)}) %collective-permute-start.27) | collective-permute-done | bytes 172064 | tf_op jit(solution)/shard_map/ppermute | solution.py:27
  103.2 0.4 fusion.45
  103.6 0.4 convolution_add_fusion
  104.2 1.8 %collective-permute-done.35 = bf16[32,7168]{1,0:T(8,128)(2,1)S(1)} collective-permute-done((bf16[32,7168]{1,0:T(8,128)(2,1)S(1)}, bf16[32,7168]{1,0:T(8,128)(2,1)S(1)}, u32[]{:S(2)}, u32[]{:S(2)}) %collective-permute-start.35) | collective-permute-done | bytes 458784 | tf_op jit(solution)/shard_map/ppermute | solution.py:18
  106.1 1.0 reshape.17
  107.1 3.6 %all-to-all-start.1 = ((bf16[16,2,7168]{2,1,0:T(2,128)(2,1)}), bf16[16,2,7168]{2,1,0:T(2,128)(2,1)S(1)}, u32[]{:S(2)}, u32[]{:S(2)}) async-start(bf16[16,2,7168]{2,1,0:T(2,128)(2,1)} %reshape.17), calls=%async_computation.1 | async-start | bytes 917504 | tf_op jit(solution)/shard_map/all_to_all | solution.py:238
  110.6 0.5 fusion.56
  111.2 10.8 %all-to-all-done.1 = bf16[16,2,7168]{2,1,0:T(2,128)(2,1)S(1)} async-done(((bf16[16,2,7168]{2,1,0:T(2,128)(2,1)}), bf16[16,2,7168]{2,1,0:T(2,128)(2,1)S(1)}, u32[]{:S(2)}, u32[]{:S(2)}) %all-to-all-start.1) | async-done | bytes 458784 | tf_op jit(solution)/shard_map/all_to_all | solution.py:238
  122.0 1.0 reduce_sum.23
  (86 shorter events, 2.3 us)
Async XLA Ops:
  0.6 0.7 copy-start
  1.4 0.7 copy-start.1
  2.1 0.7 copy-start.2
  2.7 0.7 copy-start.3
  21.7 1.9 %collective-permute-start = (bf16[32,7296]{1,0:T(8,128)(2,1)S(1)}, bf16[32,7296]{1,0:T(8,128)(2,1)S(1)}, u32[]{:S(2)}, u32[]{:S(2)}) collective-permute-start(bf16[32,7296]{1,0:T(8,128)(2,1)S(1)} %reshape.16.near), channel_id=1, source_target_pairs={{0,1},{1,0},{2,3},{3,2},{4,5},{5,4},{6,7},{7,6},{8,9},{9,8},{10,11... | collective-permute-start | bytes 1400840 | tf_op jit(solution)/shard_map/ppermute | solution.py:18
  23.6 0.7 copy-start.4
  25.8 7.3 %collective-permute-start.6 = (bf16[48,1792]{1,0:T(8,128)(2,1)S(1)}, bf16[48,1792]{1,0:T(8,128)(2,1)S(1)}, u32[]{:S(2)}, u32[]{:S(2)}) collective-permute-start(bf16[48,1792]{1,0:T(8,128)(2,1)S(1)} %get-tuple-element.9), channel_id=1, source_target_pairs={{0,32},{1,225},{2,34},{3,227},{4,36},{5,229},{6,38},{7,231},{8,40}... | collective-permute-start | bytes 516104 | tf_op jit(solution)/shard_map/ppermute | solution.py:27
  27.8 13.6 %collective-permute-start.1 = (bf16[48,1920]{1,0:T(8,128)(2,1)S(1)}, bf16[48,1920]{1,0:T(8,128)(2,1)S(1)}, u32[]{:S(2)}, u32[]{:S(2)}) collective-permute-start(bf16[48,1920]{1,0:T(8,128)(2,1)S(1)} %get-tuple-element.8), channel_id=1, source_target_pairs={{0,32},{1,225},{2,34},{3,227},{4,36},{5,229},{6,38},{7,231},{8,40}... | collective-permute-start | bytes 552968 | tf_op jit(solution)/shard_map/ppermute | solution.py:27
  31.0 5.5 %collective-permute-start.11 = (bf16[48,1792]{1,0:T(8,128)(2,1)S(1)}, bf16[48,1792]{1,0:T(8,128)(2,1)S(1)}, u32[]{:S(2)}, u32[]{:S(2)}) collective-permute-start(bf16[48,1792]{1,0:T(8,128)(2,1)S(1)} %get-tuple-element.10), channel_id=1, source_target_pairs={{0,32},{1,225},{2,34},{3,227},{4,36},{5,229},{6,38},{7,231},{8,40}... | collective-permute-start | bytes 516104 | tf_op jit(solution)/shard_map/ppermute | solution.py:27
  32.1 6.3 %collective-permute-start.16 = (bf16[48,1792]{1,0:T(8,128)(2,1)S(1)}, bf16[48,1792]{1,0:T(8,128)(2,1)S(1)}, u32[]{:S(2)}, u32[]{:S(2)}) collective-permute-start(bf16[48,1792]{1,0:T(8,128)(2,1)S(1)} %get-tuple-element.11), channel_id=1, source_target_pairs={{0,32},{1,225},{2,34},{3,227},{4,36},{5,229},{6,38},{7,231},{8,40}... | collective-permute-start | bytes 516104 | tf_op jit(solution)/shard_map/ppermute | solution.py:27
  33.1 10.3 %collective-permute-start.7 = (bf16[48,1792]{1,0:T(8,128)(2,1)S(1)}, bf16[48,1792]{1,0:T(8,128)(2,1)S(1)}, u32[]{:S(2)}, u32[]{:S(2)}) collective-permute-start(bf16[48,1792]{1,0:T(8,128)(2,1)S(1)} %collective-permute-done.6), channel_id=1, source_target_pairs={{0,32},{1,225},{2,34},{3,227},{4,36},{5,229},{6,38},{7,231},{8,40}... | collective-permute-start | bytes 516104 | tf_op jit(solution)/shard_map/ppermute | solution.py:27
  36.5 7.1 %collective-permute-start.12 = (bf16[48,1792]{1,0:T(8,128)(2,1)S(1)}, bf16[48,1792]{1,0:T(8,128)(2,1)S(1)}, u32[]{:S(2)}, u32[]{:S(2)}) collective-permute-start(bf16[48,1792]{1,0:T(8,128)(2,1)S(1)} %collective-permute-done.11), channel_id=1, source_target_pairs={{0,32},{1,225},{2,34},{3,227},{4,36},{5,229},{6,38},{7,231},{8,40}... | collective-permute-start | bytes 516104 | tf_op jit(solution)/shard_map/ppermute | solution.py:27
  38.3 6.7 %collective-permute-start.17 = (bf16[48,1792]{1,0:T(8,128)(2,1)S(1)}, bf16[48,1792]{1,0:T(8,128)(2,1)S(1)}, u32[]{:S(2)}, u32[]{:S(2)}) collective-permute-start(bf16[48,1792]{1,0:T(8,128)(2,1)S(1)} %collective-permute-done.16), channel_id=1, source_target_pairs={{0,32},{1,225},{2,34},{3,227},{4,36},{5,229},{6,38},{7,231},{8,40}... | collective-permute-start | bytes 516104 | tf_op jit(solution)/shard_map/ppermute | solution.py:27
  41.5 6.6 %collective-permute-start.2 = (bf16[48,1920]{1,0:T(8,128)(2,1)S(1)}, bf16[48,1920]{1,0:T(8,128)(2,1)S(1)}, u32[]{:S(2)}, u32[]{:S(2)}) collective-permute-start(bf16[48,1920]{1,0:T(8,128)(2,1)S(1)} %collective-permute-done.1), channel_id=1, source_target_pairs={{0,32},{1,225},{2,34},{3,227},{4,36},{5,229},{6,38},{7,231},{8,40}... | collective-permute-start | bytes 552968 | tf_op jit(solution)/shard_map/ppermute | solution.py:27
  43.4 6.6 %collective-permute-start.8 = (bf16[48,1792]{1,0:T(8,128)(2,1)S(1)}, bf16[48,1792]{1,0:T(8,128)(2,1)S(1)}, u32[]{:S(2)}, u32[]{:S(2)}) collective-permute-start(bf16[48,1792]{1,0:T(8,128)(2,1)S(1)} %collective-permute-done.7), channel_id=1, source_target_pairs={{0,32},{1,225},{2,34},{3,227},{4,36},{5,229},{6,38},{7,231},{8,40}... | collective-permute-start | bytes 516104 | tf_op jit(solution)/shard_map/ppermute | solution.py:27
  43.5 8.8 %collective-permute-start.13 = (bf16[48,1792]{1,0:T(8,128)(2,1)S(1)}, bf16[48,1792]{1,0:T(8,128)(2,1)S(1)}, u32[]{:S(2)}, u32[]{:S(2)}) collective-permute-start(bf16[48,1792]{1,0:T(8,128)(2,1)S(1)} %collective-permute-done.12), channel_id=1, source_target_pairs={{0,32},{1,225},{2,34},{3,227},{4,36},{5,229},{6,38},{7,231},{8,40}... | collective-permute-start | bytes 516104 | tf_op jit(solution)/shard_map/ppermute | solution.py:27
  45.1 9.1 %collective-permute-start.18 = (bf16[48,1792]{1,0:T(8,128)(2,1)S(1)}, bf16[48,1792]{1,0:T(8,128)(2,1)S(1)}, u32[]{:S(2)}, u32[]{:S(2)}) collective-permute-start(bf16[48,1792]{1,0:T(8,128)(2,1)S(1)} %collective-permute-done.17), channel_id=1, source_target_pairs={{0,32},{1,225},{2,34},{3,227},{4,36},{5,229},{6,38},{7,231},{8,40}... | collective-permute-start | bytes 516104 | tf_op jit(solution)/shard_map/ppermute | solution.py:27
  48.1 13.7 %copy-start.5 = (bf16[1,2,7168,128]{3,2,1,0:T(8,128)(2,1)S(1)}, bf16[1,2,7168,128]{3,2,1,0:T(8,128)(2,1)}, u32[]{:S(2)}) copy-start(bf16[1,2,7168,128]{3,2,1,0:T(8,128)(2,1)} %param.12) | copy-start | bytes 11010052
  48.1 6.5 %collective-permute-start.3 = (bf16[48,1920]{1,0:T(8,128)(2,1)S(1)}, bf16[48,1920]{1,0:T(8,128)(2,1)S(1)}, u32[]{:S(2)}, u32[]{:S(2)}) collective-permute-start(bf16[48,1920]{1,0:T(8,128)(2,1)S(1)} %collective-permute-done.2), channel_id=1, source_target_pairs={{0,32},{1,225},{2,34},{3,227},{4,36},{5,229},{6,38},{7,231},{8,40}... | collective-permute-start | bytes 552968 | tf_op jit(solution)/shard_map/ppermute | solution.py:27
  50.1 6.4 %collective-permute-start.9 = (bf16[24,1792]{1,0:T(8,128)(2,1)S(1)}, bf16[24,1792]{1,0:T(8,128)(2,1)S(1)}, u32[]{:S(2)}, u32[]{:S(2)}) collective-permute-start(bf16[24,1792]{1,0:T(8,128)(2,1)S(1)} %get-tuple-element.32), channel_id=1, source_target_pairs={{0,32},{1,225},{2,34},{3,227},{4,36},{5,229},{6,38},{7,231},{8,40}... | collective-permute-start | bytes 258056 | tf_op jit(solution)/shard_map/ppermute | solution.py:27
  52.0 9.7 %collective-permute-start.10 = (bf16[72,1792]{1,0:T(8,128)(2,1)S(1)}, bf16[72,1792]{1,0:T(8,128)(2,1)S(1)}, u32[]{:S(2)}, u32[]{:S(2)}) collective-permute-start(bf16[72,1792]{1,0:T(8,128)(2,1)S(1)} %pad_maximum_fusion.2), channel_id=1, source_target_pairs={{0,1},{1,0},{2,3},{3,2},{4,5},{5,4},{6,7},{7,6},{8,9},{9,8},{10,11... | collective-permute-start | bytes 774152 | tf_op jit(solution)/shard_map/ppermute | solution.py:18
  52.4 4.6 %collective-permute-start.14 = (bf16[24,1792]{1,0:T(8,128)(2,1)S(1)}, bf16[24,1792]{1,0:T(8,128)(2,1)S(1)}, u32[]{:S(2)}, u32[]{:S(2)}) collective-permute-start(bf16[24,1792]{1,0:T(8,128)(2,1)S(1)} %get-tuple-element.39), channel_id=1, source_target_pairs={{0,32},{1,225},{2,34},{3,227},{4,36},{5,229},{6,38},{7,231},{8,40}... | collective-permute-start | bytes 258056 | tf_op jit(solution)/shard_map/ppermute | solution.py:27
  54.2 8.3 %collective-permute-start.15 = (bf16[72,1792]{1,0:T(8,128)(2,1)S(1)}, bf16[72,1792]{1,0:T(8,128)(2,1)S(1)}, u32[]{:S(2)}, u32[]{:S(2)}) collective-permute-start(bf16[72,1792]{1,0:T(8,128)(2,1)S(1)} %pad_maximum_fusion.3), channel_id=1, source_target_pairs={{0,1},{1,0},{2,3},{3,2},{4,5},{5,4},{6,7},{7,6},{8,9},{9,8},{10,11... | collective-permute-start | bytes 774152 | tf_op jit(solution)/shard_map/ppermute | solution.py:18
  54.6 5.0 %collective-permute-start.19 = (bf16[24,1792]{1,0:T(8,128)(2,1)S(1)}, bf16[24,1792]{1,0:T(8,128)(2,1)S(1)}, u32[]{:S(2)}, u32[]{:S(2)}) collective-permute-start(bf16[24,1792]{1,0:T(8,128)(2,1)S(1)} %get-tuple-element.46), channel_id=1, source_target_pairs={{0,32},{1,225},{2,34},{3,227},{4,36},{5,229},{6,38},{7,231},{8,40}... | collective-permute-start | bytes 258056 | tf_op jit(solution)/shard_map/ppermute | solution.py:27
  56.5 6.7 %collective-permute-start.20 = (bf16[72,1792]{1,0:T(8,128)(2,1)S(1)}, bf16[72,1792]{1,0:T(8,128)(2,1)S(1)}, u32[]{:S(2)}, u32[]{:S(2)}) collective-permute-start(bf16[72,1792]{1,0:T(8,128)(2,1)S(1)} %pad_maximum_fusion.4), channel_id=1, source_target_pairs={{0,1},{1,0},{2,3},{3,2},{4,5},{5,4},{6,7},{7,6},{8,9},{9,8},{10,11... | collective-permute-start | bytes 774152 | tf_op jit(solution)/shard_map/ppermute | solution.py:18
  56.9 4.8 %collective-permute-start.4 = (bf16[24,1920]{1,0:T(8,128)(2,1)S(1)}, bf16[24,1920]{1,0:T(8,128)(2,1)S(1)}, u32[]{:S(2)}, u32[]{:S(2)}) collective-permute-start(bf16[24,1920]{1,0:T(8,128)(2,1)S(1)} %get-tuple-element.25), channel_id=1, source_target_pairs={{0,32},{1,225},{2,34},{3,227},{4,36},{5,229},{6,38},{7,231},{8,40}... | collective-permute-start | bytes 276488 | tf_op jit(solution)/shard_map/ppermute | solution.py:27
  59.6 4.3 %collective-permute-start.5 = (bf16[72,1920]{1,0:T(8,128)(2,1)S(1)}, bf16[72,1920]{1,0:T(8,128)(2,1)S(1)}, u32[]{:S(2)}, u32[]{:S(2)}) collective-permute-start(bf16[72,1920]{1,0:T(8,128)(2,1)S(1)} %pad_maximum_fusion.1), channel_id=1, source_target_pairs={{0,1},{1,0},{2,3},{3,2},{4,5},{5,4},{6,7},{7,6},{8,9},{9,8},{10,11... | collective-permute-start | bytes 829448 | tf_op jit(solution)/shard_map/ppermute | solution.py:18
  63.6 1.5 %copy-start.6 = (bf16[1,128,7168]{2,1,0:T(8,128)(2,1)S(1)}, bf16[1,128,7168]{2,1,0:T(8,128)(2,1)}, u32[]{:S(2)}) copy-start(bf16[1,128,7168]{2,1,0:T(8,128)(2,1)} %param.13) | copy-start | bytes 5505028
  66.2 7.2 %collective-permute-start.28 = (bf16[24,3584]{1,0:T(8,128)(2,1)S(1)}, bf16[24,3584]{1,0:T(8,128)(2,1)S(1)}, u32[]{:S(2)}, u32[]{:S(2)}) collective-permute-start(bf16[24,3584]{1,0:T(8,128)(2,1)S(1)} %get-tuple-element.22), channel_id=1, source_target_pairs={{0,32},{1,225},{2,34},{3,227},{4,36},{5,229},{6,38},{7,231},{8,40}... | collective-permute-start | bytes 516104 | tf_op jit(solution)/shard_map/ppermute | solution.py:27
  68.6 11.5 %collective-permute-start.32 = (bf16[24,3584]{1,0:T(8,128)(2,1)S(1)}, bf16[24,3584]{1,0:T(8,128)(2,1)S(1)}, u32[]{:S(2)}, u32[]{:S(2)}) collective-permute-start(bf16[24,3584]{1,0:T(8,128)(2,1)S(1)} %get-tuple-element.23), channel_id=1, source_target_pairs={{0,224},{1,33},{2,226},{3,35},{4,228},{5,37},{6,230},{7,39},{8,232... | collective-permute-start | bytes 516104 | tf_op jit(solution)/shard_map/ppermute | solution.py:27
  68.7 8.1 %collective-permute-start.21 = (bf16[24,3584]{1,0:T(8,128)(2,1)S(1)}, bf16[24,3584]{1,0:T(8,128)(2,1)S(1)}, u32[]{:S(2)}, u32[]{:S(2)}) collective-permute-start(bf16[24,3584]{1,0:T(8,128)(2,1)S(1)} %get-tuple-element.20), channel_id=1, source_target_pairs={{0,32},{1,225},{2,34},{3,227},{4,36},{5,229},{6,38},{7,231},{8,40}... | collective-permute-start | bytes 516104 | tf_op jit(solution)/shard_map/ppermute | solution.py:27
  71.7 12.2 %collective-permute-start.25 = (bf16[24,3584]{1,0:T(8,128)(2,1)S(1)}, bf16[24,3584]{1,0:T(8,128)(2,1)S(1)}, u32[]{:S(2)}, u32[]{:S(2)}) collective-permute-start(bf16[24,3584]{1,0:T(8,128)(2,1)S(1)} %get-tuple-element.21), channel_id=1, source_target_pairs={{0,224},{1,33},{2,226},{3,35},{4,228},{5,37},{6,230},{7,39},{8,232... | collective-permute-start | bytes 516104 | tf_op jit(solution)/shard_map/ppermute | solution.py:27
  73.4 6.7 %collective-permute-start.29 = (bf16[24,3584]{1,0:T(8,128)(2,1)S(1)}, bf16[24,3584]{1,0:T(8,128)(2,1)S(1)}, u32[]{:S(2)}, u32[]{:S(2)}) collective-permute-start(bf16[24,3584]{1,0:T(8,128)(2,1)S(1)} %fusion.35), channel_id=1, source_target_pairs={{0,32},{1,225},{2,34},{3,227},{4,36},{5,229},{6,38},{7,231},{8,40}... | collective-permute-start | bytes 516104 | tf_op jit(solution)/shard_map/ppermute | solution.py:27
  76.8 7.0 %collective-permute-start.22 = (bf16[24,3584]{1,0:T(8,128)(2,1)S(1)}, bf16[24,3584]{1,0:T(8,128)(2,1)S(1)}, u32[]{:S(2)}, u32[]{:S(2)}) collective-permute-start(bf16[24,3584]{1,0:T(8,128)(2,1)S(1)} %fusion.42), channel_id=1, source_target_pairs={{0,32},{1,225},{2,34},{3,227},{4,36},{5,229},{6,38},{7,231},{8,40}... | collective-permute-start | bytes 516104 | tf_op jit(solution)/shard_map/ppermute | solution.py:27
  80.2 7.6 %collective-permute-start.30 = (bf16[24,3584]{1,0:T(8,128)(2,1)S(1)}, bf16[24,3584]{1,0:T(8,128)(2,1)S(1)}, u32[]{:S(2)}, u32[]{:S(2)}) collective-permute-start(bf16[24,3584]{1,0:T(8,128)(2,1)S(1)} %get-tuple-element.18), channel_id=1, source_target_pairs={{0,32},{1,225},{2,34},{3,227},{4,36},{5,229},{6,38},{7,231},{8,40}... | collective-permute-start | bytes 516104 | tf_op jit(solution)/shard_map/ppermute | solution.py:27
  83.8 7.6 %collective-permute-start.33 = (bf16[24,3584]{1,0:T(8,128)(2,1)S(1)}, bf16[24,3584]{1,0:T(8,128)(2,1)S(1)}, u32[]{:S(2)}, u32[]{:S(2)}) collective-permute-start(bf16[24,3584]{1,0:T(8,128)(2,1)S(1)} %get-tuple-element.19), channel_id=1, source_target_pairs={{0,224},{1,33},{2,226},{3,35},{4,228},{5,37},{6,230},{7,39},{8,232... | collective-permute-start | bytes 516104 | tf_op jit(solution)/shard_map/ppermute | solution.py:27
  83.9 10.5 %collective-permute-start.23 = (bf16[24,3584]{1,0:T(8,128)(2,1)S(1)}, bf16[24,3584]{1,0:T(8,128)(2,1)S(1)}, u32[]{:S(2)}, u32[]{:S(2)}) collective-permute-start(bf16[24,3584]{1,0:T(8,128)(2,1)S(1)} %get-tuple-element.14), channel_id=1, source_target_pairs={{0,32},{1,225},{2,34},{3,227},{4,36},{5,229},{6,38},{7,231},{8,40}... | collective-permute-start | bytes 516104 | tf_op jit(solution)/shard_map/ppermute | solution.py:27
  87.2 7.9 %collective-permute-start.26 = (bf16[24,3584]{1,0:T(8,128)(2,1)S(1)}, bf16[24,3584]{1,0:T(8,128)(2,1)S(1)}, u32[]{:S(2)}, u32[]{:S(2)}) collective-permute-start(bf16[24,3584]{1,0:T(8,128)(2,1)S(1)} %get-tuple-element.15), channel_id=1, source_target_pairs={{0,224},{1,33},{2,226},{3,35},{4,228},{5,37},{6,230},{7,39},{8,232... | collective-permute-start | bytes 516104 | tf_op jit(solution)/shard_map/ppermute | solution.py:27
  91.5 6.8 %collective-permute-start.31 = (bf16[24,3584]{1,0:T(8,128)(2,1)S(1)}, bf16[24,3584]{1,0:T(8,128)(2,1)S(1)}, u32[]{:S(2)}, u32[]{:S(2)}) collective-permute-start(bf16[24,3584]{1,0:T(8,128)(2,1)S(1)} %get-tuple-element.16), channel_id=1, source_target_pairs={{0,32},{1,225},{2,34},{3,227},{4,36},{5,229},{6,38},{7,231},{8,40}... | collective-permute-start | bytes 516104 | tf_op jit(solution)/shard_map/ppermute | solution.py:27
  94.4 5.4 %collective-permute-start.34 = (bf16[24,3584]{1,0:T(8,128)(2,1)S(1)}, bf16[24,3584]{1,0:T(8,128)(2,1)S(1)}, u32[]{:S(2)}, u32[]{:S(2)}) collective-permute-start(bf16[24,3584]{1,0:T(8,128)(2,1)S(1)} %get-tuple-element.17), channel_id=1, source_target_pairs={{0,224},{1,33},{2,226},{3,35},{4,228},{5,37},{6,230},{7,39},{8,232... | collective-permute-start | bytes 516104 | tf_op jit(solution)/shard_map/ppermute | solution.py:27
  95.2 5.5 %collective-permute-start.24 = (bf16[24,3584]{1,0:T(8,128)(2,1)S(1)}, bf16[24,3584]{1,0:T(8,128)(2,1)S(1)}, u32[]{:S(2)}, u32[]{:S(2)}) collective-permute-start(bf16[24,3584]{1,0:T(8,128)(2,1)S(1)} %get-tuple-element.12), channel_id=1, source_target_pairs={{0,32},{1,225},{2,34},{3,227},{4,36},{5,229},{6,38},{7,231},{8,40}... | collective-permute-start | bytes 516104 | tf_op jit(solution)/shard_map/ppermute | solution.py:27
  97.7 5.4 %collective-permute-start.27 = (bf16[24,3584]{1,0:T(8,128)(2,1)S(1)}, bf16[24,3584]{1,0:T(8,128)(2,1)S(1)}, u32[]{:S(2)}, u32[]{:S(2)}) collective-permute-start(bf16[24,3584]{1,0:T(8,128)(2,1)S(1)} %get-tuple-element.13), channel_id=1, source_target_pairs={{0,224},{1,33},{2,226},{3,35},{4,228},{5,37},{6,230},{7,39},{8,232... | collective-permute-start | bytes 516104 | tf_op jit(solution)/shard_map/ppermute | solution.py:27
  104.1 1.9 %collective-permute-start.35 = (bf16[32,7168]{1,0:T(8,128)(2,1)S(1)}, bf16[32,7168]{1,0:T(8,128)(2,1)S(1)}, u32[]{:S(2)}, u32[]{:S(2)}) collective-permute-start(bf16[32,7168]{1,0:T(8,128)(2,1)S(1)} %slice.468), channel_id=1, source_target_pairs={{0,1},{1,0},{2,3},{3,2},{4,5},{5,4},{6,7},{7,6},{8,9},{9,8},{10,11... | collective-permute-start | bytes 1376264 | tf_op jit(solution)/shard_map/ppermute | solution.py:18
  107.1 14.9 %all-to-all-start.1 = ((bf16[16,2,7168]{2,1,0:T(2,128)(2,1)}), bf16[16,2,7168]{2,1,0:T(2,128)(2,1)S(1)}, u32[]{:S(2)}, u32[]{:S(2)}) async-start(bf16[16,2,7168]{2,1,0:T(2,128)(2,1)} %reshape.17), calls=%async_computation.1 | async-start | bytes 917504 | tf_op jit(solution)/shard_map/all_to_all | solution.py:238

commit v3 on v2

--- a/solution.py
+++ b/solution.py
@@ -10,7 +10,8 @@
 F32, BF16 = jnp.float32, jnp.bfloat16
 MOST = 24
 META = 128
-CHUNKS = 4
+PREP_VMEM = 60 * 2**20
+CHUNKS = 3
 SUM_CHUNKS = 2
 
 
@@ -51,6 +52,7 @@
                 back[c] = (
                     core_ring(back[c], -1, count, groups).astype(F32) + f(count - step + 1)
                 ).astype(BF16)
+            fore[c], back[c] = lax.optimization_barrier((fore[c], back[c]))
     return [
         (
             f(0)
@@ -62,33 +64,37 @@
 
 
 def prep_kernel(top, *refs):
-    sources, sent, held, sem = refs[:4], refs[4], refs[5:9], refs[9]
+    sources, spread, held, sem = refs[:5], refs[5], refs[6:11], refs[11]
     copies = [pltpu.make_async_copy(s, h, sem.at[i]) for i, (s, h) in enumerate(zip(sources, held))]
     for copy in copies:
         copy.start()
     for copy in copies:
         copy.wait()
-    tokens, ids, replica, weight = held
+    tokens, ids, replica, weight, plan = held
     rows, width = tokens.shape
-    sent[:, :width] = tokens[...]
     high = weight[...].astype(BF16).astype(F32)
     middle = (weight[...] - high).astype(BF16).astype(F32)
     low = weight[...] - high - middle
+    host = jnp.zeros(ids.shape, jnp.int32)
+    for index in range(plan.shape[0]):
+        host = jnp.where(ids[...] == plan[index], index, host)
+    parts = [ids[...].astype(F32), replica[...].astype(F32), high, middle, low, host.astype(F32)]
     lane = lax.broadcasted_iota(jnp.int32, (rows, META), 1)
     meta = jnp.zeros((rows, META), F32)
-    for part, value in enumerate([ids[...].astype(F32), replica[...].astype(F32), high, middle, low]):
+    for part, value in enumerate(parts):
         for k in range(top):
             meta = jnp.where(lane == part * top + k, value[:, k : k + 1], meta)
-    sent[:, width:] = meta.astype(BF16)
-
-
-def pack_kernel(top, span, near, far, plan, *outs):
-    packed, mix, spare_plan, sem = outs[:CHUNKS], outs[CHUNKS], outs[CHUNKS + 1], outs[CHUNKS + 2]
-    plan_copy = pltpu.make_async_copy(plan, spare_plan, sem)
-    plan_copy.start()
+    meta = meta.astype(BF16)
+    for peer in range(spread.shape[0]):
+        spread[peer, :, :width] = tokens[...]
+        spread[peer, :, width:] = meta
+
+
+def pack_kernel(top, cols, near, far, *outs):
+    packed, mix = outs[:CHUNKS], outs[CHUNKS]
     half = near.shape[0]
     total = 2 * half
-    width = span * CHUNKS
+    width = cols[-1].stop
     me = lax.axis_index("expert")
     info = jnp.concatenate([near[:, width:], far[:, width:]], 0)
     source = lax.broadcasted_iota(jnp.int32, (META, META), 0)
@@ -98,7 +104,7 @@
         move = ((source == lane + number * top) & (lane < top)).astype(BF16)
         return jnp.dot(info, move, preferred_element_type=F32)
 
-    ids, copies = part(0), part(1)
+    ids, copies, hosts = part(0), part(1), part(5)
     weights = [part(2), part(3), part(4)]
     valid = lax.broadcasted_iota(jnp.int32, (total, META), 1) < top
     ones = jnp.ones((8, META), BF16)
@@ -115,17 +121,15 @@
     slot = lax.broadcasted_iota(jnp.int32, (MOST, total), 0).astype(F32)
     tail_lane = lax.broadcasted_iota(jnp.int32, (MOST, META), 1)
     chosen, tails = [], []
-    plan_copy.wait()
     for which in range(2):
         expert = me if which == 0 else me ^ 1
         named = valid & (ids == expert.astype(F32))
-        spare = spare_plan[expert].astype(F32)
         hit = along(named.astype(F32))
         rank = jnp.dot(hit.astype(BF16), earlier, preferred_element_type=F32)
         pick = jnp.where((hit[:1] > 0.0) & (rank[:1] == slot), 1.0, 0.0)
         chosen.append(pick)
         own_count = jnp.sum((named & (copies == 0.0)).astype(F32))
-        spare_hit = valid & (ids == spare) & (copies == 1.0)
+        spare_hit = valid & (hosts == expert.astype(F32)) & (copies == 1.0)
         spare_count = jnp.sum(spare_hit.astype(F32))
         tails.append(
             jnp.where(tail_lane == 0, own_count, jnp.where(tail_lane == 1, spare_count, 0.0))
@@ -137,12 +141,12 @@
             mix[0] = high
             mix[1] = (value - high.astype(F32)).astype(BF16)
     pick = jnp.concatenate(chosen, 0).astype(BF16)
-    for c in range(CHUNKS):
-        at = slice(c * span, (c + 1) * span)
+    tail = jnp.concatenate(tails, 0).astype(BF16)
+    for out, at in zip(packed, cols):
         value = jnp.dot(pick[:, :half], near[:, at], preferred_element_type=F32)
         value += jnp.dot(pick[:, half:], far[:, at], preferred_element_type=F32)
-        packed[c][:, :span] = value.astype(BF16)
-    packed[0][:, span:] = jnp.concatenate(tails, 0).astype(BF16)
+        out[:, : at.stop - at.start] = value.astype(BF16)
+    packed[-1][:, cols[-1].stop - cols[-1].start :] = tail
 
 
 def body(tokens, expert_ids, replica, route_weight, spare_plan, w_in, w_down):
@@ -157,54 +161,52 @@
     routed = (tokens, expert_ids, replica, route_weight)
     grant = pltpu.CompilerParams(vmem_limit_bytes=16 * 2**20)
 
-    sent = pl.pallas_call(
+    spread = pl.pallas_call(
         functools.partial(prep_kernel, top),
-        out_shape=jax.ShapeDtypeStruct((rows, width + META), BF16),
-        in_specs=[anywhere] * 4,
+        out_shape=jax.ShapeDtypeStruct((peers, rows, width + META), BF16),
+        in_specs=[anywhere] * 5,
         out_specs=vmem,
         scratch_shapes=[pltpu.VMEM(v.shape, v.dtype) for v in routed]
-        + [pltpu.SemaphoreType.DMA((4,))],
-        compiler_params=grant,
-    )(*routed)
-
-    spread = jnp.broadcast_to(sent[None], (peers, rows, width + META))
+        + [pltpu.SMEM(spare_plan.shape, spare_plan.dtype), pltpu.SemaphoreType.DMA((5,))],
+        compiler_params=pltpu.CompilerParams(vmem_limit_bytes=PREP_VMEM),
+    )(*routed, spare_plan)
+
     near = lax.all_to_all(spread, "expert", 0, 0, axis_index_groups=same_core, tiled=True)
     near = lax.optimization_barrier(near.reshape(peers * rows, width + META))
     far = core_swap(near, groups)
     total = 2 * peers * rows
 
-    span = width // CHUNKS
-    cols = [slice(c * span, (c + 1) * span) for c in range(CHUNKS)]
+    span = (width + META) // CHUNKS
+    cols = [slice(c * span, min((c + 1) * span, width)) for c in range(CHUNKS)]
+    last = cols[-1].stop - cols[-1].start
     shapes = [
-        jax.ShapeDtypeStruct((2 * MOST, span + (META if c == 0 else 0)), BF16)
+        jax.ShapeDtypeStruct((2 * MOST, span), BF16)
         for c in range(CHUNKS)
     ]
     *parts, mix = pl.pallas_call(
-        functools.partial(pack_kernel, top, span),
+        functools.partial(pack_kernel, top, cols),
         out_shape=shapes + [jax.ShapeDtypeStruct((2, MOST, total), BF16)],
-        in_specs=[vmem, vmem, anywhere],
+        in_specs=[vmem] * 2,
         out_specs=[vmem] * (CHUNKS + 1),
-        scratch_shapes=[
-            pltpu.SMEM(spare_plan.shape, spare_plan.dtype), pltpu.SemaphoreType.DMA(())
-        ],
         compiler_params=grant,
-    )(near, far, spare_plan)
+    )(near, far)
 
     moving, other = gather_ring(parts, count, groups)
 
-    load = sum(b[0, span : span + 2].astype(F32) for b in moving[0])
-    load += jnp.sum(other[0].reshape(half - 1, MOST, -1)[:, 0, span : span + 2].astype(F32), 0)
+    counts = slice(last, last + 2)
+    load = sum(b[0, counts].astype(F32) for b in moving[-1])
+    load += jnp.sum(other[-1].reshape(half - 1, MOST, span)[:, 0, counts].astype(F32), 0)
     slot_load = load.astype(jnp.int32)[None]
 
     gathered = [
-        jnp.concatenate([b[:MOST, :span] for b in got] + [handed[:, :span]], 0)
-        for got, handed in zip(moving, other)
+        jnp.concatenate([b[:, : at.stop - at.start] for b in [got[0][:MOST]] + [v[:MOST] for v in got[1:]] + [handed]], 0)
+        for got, handed, at in zip(moving, other, cols)
     ]
 
     def up(which):
         return sum(
             jnp.dot(x, w_in[0, which, cols[c]], preferred_element_type=F32)
-            for c, x in enumerate(gathered)
+            for c, x in reversed(list(enumerate(gathered)))
         )
 
     hidden = (jax.nn.silu(up(0)) * up(1)).astype(BF16)

time: 124 us -> 123 us (level)
  waiting for transfers between devices: 31.7 us -> 38.3 us
  starting transfers between devices: 58.4 us -> 54.1 us
  local copies, waits for them, and re-layouts: 5.65 us -> 1.86 us
    ppermute x30 -> x26, waiting for transfers between devices: 17.2 us -> 23.8 us  [core_ring(): return lax.ppermute(value, ('attn', 'expert'), pairs)]
    ppermute x30 -> x26, starting transfers between devices: 54.1 us -> 50.1 us  [core_ring(): return lax.ppermute(value, ('attn', 'expert'), pairs)]
    unnamed x23 -> x12, local copies, waits for them, and re-layouts: 3.94 us -> 0.37 us
    pallas_call x1, Pallas kernels: 0.16 us -> 1.73 us  [body(): pl.pallas_call(functools.partial(prep_kernel, top), out_shape=jax.ShapeDt...]
    dot_general x8 -> x6, matrix products: 2.71 us -> 2.39 us  [up(): jnp.dot(x, w_in[0, which, cols[c]], preferred_element_type=F32)]
    ppermute x6 -> x5, waiting for transfers between devices: 3.63 us -> 3.63 us  [core_swap(): return lax.ppermute(value, 'expert', [(i, i ^ 1) for i in range(groups)])]
  transfers between devices with their start and end apart: 37 -> 32, of which waited for: 16 -> 17; matrix products, arithmetic and copies ran while one was open for 3% -> 3% of each run, Pallas kernels for 0% -> 0%
where the time goes in v3:
time: 123 us; the launch traced here: 122 us
  starting transfers between devices  54.1 us (44%)
  waiting for transfers between devices  38.3 us (31%)
  blocking collectives  17.9 us (15%)
  matrix products  4.24 us (3%)
  Pallas kernels  2.71 us (2%)
  other arithmetic  2.24 us (2%)
  local copies, waits for them, and re-layouts  1.86 us (2%)
    ppermute x26, starting transfers between devices, core_ring(): return lax.ppermute(value, ('attn', 'expert'), pairs)  50.1 us
    ppermute x26, waiting for transfers between devices, core_ring(): return lax.ppermute(value, ('attn', 'expert'), pairs)  23.8 us
    all_to_all x1, blocking collectives, body(): lax.all_to_all(spread, 'expert', 0, 0, axis_index_groups=same_core, tiled...  17.9 us
    all_to_all x1, waiting for transfers between devices, body(): lax.all_to_all(both.reshape(peers, rows, width), 'expert', 0, 0, axis_ind...  10.8 us
    ppermute x5, waiting for transfers between devices, core_swap(): return lax.ppermute(value, 'expert', [(i, i ^ 1) for i in range(groups)])  3.63 us
    all_to_all x1, starting transfers between devices, body(): lax.all_to_all(both.reshape(peers, rows, width), 'expert', 0, 0, axis_ind...  3.56 us
  transfers between devices with their start and end apart: 32, of which 17 were waited for; matrix products, arithmetic and copies ran while one was open for 3% of the time, Pallas kernels for 0%

profile of v3, /device:TPU:64, one launch (start us, length us, event | category | flops | bytes accessed | tf_op | source)
XLA Modules:
  0.0 122.4 jit_solution(16805760747804450653)
XLA Ops:
  0.6 1.7 %shard_map.86 = bf16[16,2,7296]{2,1,0:T(2,128)(2,1)} custom-call(bf16[2,7168]{1,0:T(2,128)(2,1)} %refs_0_.1, s32[2,8]{1,0:T(2,128)} %refs_1_.1, s32[2,8]{1,0:T(2,128)} %refs_2_.1, f32[2,8]{1,0:T(2,128)} %refs_3_.1, s32[32]{0:T(128)} %refs_4_.1), custom_call_target="tpu_custom_call" | custom-call | tf_op jit(solution)/shard_map/pallas_call | solution.py:164
  2.4 17.9 %all_to_all.10 = bf16[16,2,7296]{2,1,0:T(2,128)(2,1)S(1)} all-to-all(bf16[16,2,7296]{2,1,0:T(2,128)(2,1)} %shard_map.86), channel_id=1, replica_groups={{0,2,4,6,8,10,12,14,16,18,20,22,24,26,28,30},{1,3,5,7,9,11,13,15,17,19,..., dimensions={0} | all-to-all | bytes 933888 | tf_op jit(solution)/shard_map/all_to_all | solution.py:174
  20.3 0.2 reshape.15.near
  20.5 0.1 collective-permute-start
  20.6 1.8 %collective-permute-done.far = bf16[32,7296]{1,0:T(8,128)(2,1)S(1)} collective-permute-done((bf16[32,7296]{1,0:T(8,128)(2,1)S(1)}, bf16[32,7296]{1,0:T(8,128)(2,1)S(1)}, u32[]{:S(2)}, u32[]{:S(2)}) %collective-permute-start) | collective-permute-done | bytes 466976 | tf_op jit(solution)/shard_map/ppermute | solution.py:19
  22.4 1.0 shard_map.87
  23.4 2.0 %collective-permute-start.6 = (bf16[48,2432]{1,0:T(8,128)(2,1)S(1)}, bf16[48,2432]{1,0:T(8,128)(2,1)S(1)}, u32[]{:S(2)}, u32[]{:S(2)}) collective-permute-start(bf16[48,2432]{1,0:T(8,128)(2,1)S(1)} %get-tuple-element.20), channel_id=1, source_target_pairs={{0,32},{1,225},{2,34},{3,227},{4,36},{5,229},{6,38},{7,231},{8,40}... | collective-permute-start | bytes 700424 | tf_op jit(solution)/shard_map/ppermute | solution.py:28
  25.4 3.2 %collective-permute-start.11 = (bf16[48,2432]{1,0:T(8,128)(2,1)S(1)}, bf16[48,2432]{1,0:T(8,128)(2,1)S(1)}, u32[]{:S(2)}, u32[]{:S(2)}) collective-permute-start(bf16[48,2432]{1,0:T(8,128)(2,1)S(1)} %get-tuple-element.21), channel_id=1, source_target_pairs={{0,32},{1,225},{2,34},{3,227},{4,36},{5,229},{6,38},{7,231},{8,40}... | collective-permute-start | bytes 700424 | tf_op jit(solution)/shard_map/ppermute | solution.py:28
  28.5 1.1 collective-permute-start.1
  29.6 2.5 %collective-permute-start.7 = (bf16[48,2432]{1,0:T(8,128)(2,1)S(1)}, bf16[48,2432]{1,0:T(8,128)(2,1)S(1)}, u32[]{:S(2)}, u32[]{:S(2)}) collective-permute-start(bf16[48,2432]{1,0:T(8,128)(2,1)S(1)} %collective-permute-done.6), channel_id=1, source_target_pairs={{0,32},{1,225},{2,34},{3,227},{4,36},{5,229},{6,38},{7,231},{8,40}... | collective-permute-start | bytes 700424 | tf_op jit(solution)/shard_map/ppermute | solution.py:28
  32.1 3.7 %collective-permute-start.12 = (bf16[48,2432]{1,0:T(8,128)(2,1)S(1)}, bf16[48,2432]{1,0:T(8,128)(2,1)S(1)}, u32[]{:S(2)}, u32[]{:S(2)}) collective-permute-start(bf16[48,2432]{1,0:T(8,128)(2,1)S(1)} %collective-permute-done.11), channel_id=1, source_target_pairs={{0,32},{1,225},{2,34},{3,227},{4,36},{5,229},{6,38},{7,231},{8,40}... | collective-permute-start | bytes 700424 | tf_op jit(solution)/shard_map/ppermute | solution.py:28
  35.8 2.5 %collective-permute-start.2 = (bf16[48,2432]{1,0:T(8,128)(2,1)S(1)}, bf16[48,2432]{1,0:T(8,128)(2,1)S(1)}, u32[]{:S(2)}, u32[]{:S(2)}) collective-permute-start(bf16[48,2432]{1,0:T(8,128)(2,1)S(1)} %collective-permute-done.1), channel_id=1, source_target_pairs={{0,32},{1,225},{2,34},{3,227},{4,36},{5,229},{6,38},{7,231},{8,40}... | collective-permute-start | bytes 700424 | tf_op jit(solution)/shard_map/ppermute | solution.py:28
  38.4 2.6 %collective-permute-start.8 = (bf16[48,2432]{1,0:T(8,128)(2,1)S(1)}, bf16[48,2432]{1,0:T(8,128)(2,1)S(1)}, u32[]{:S(2)}, u32[]{:S(2)}) collective-permute-start(bf16[48,2432]{1,0:T(8,128)(2,1)S(1)} %collective-permute-done.7), channel_id=1, source_target_pairs={{0,32},{1,225},{2,34},{3,227},{4,36},{5,229},{6,38},{7,231},{8,40}... | collective-permute-start | bytes 700424 | tf_op jit(solution)/shard_map/ppermute | solution.py:28
  41.0 2.3 %collective-permute-start.13 = (bf16[48,2432]{1,0:T(8,128)(2,1)S(1)}, bf16[48,2432]{1,0:T(8,128)(2,1)S(1)}, u32[]{:S(2)}, u32[]{:S(2)}) collective-permute-start(bf16[48,2432]{1,0:T(8,128)(2,1)S(1)} %collective-permute-done.12), channel_id=1, source_target_pairs={{0,32},{1,225},{2,34},{3,227},{4,36},{5,229},{6,38},{7,231},{8,40}... | collective-permute-start | bytes 700424 | tf_op jit(solution)/shard_map/ppermute | solution.py:28
  43.3 2.5 %collective-permute-start.3 = (bf16[48,2432]{1,0:T(8,128)(2,1)S(1)}, bf16[48,2432]{1,0:T(8,128)(2,1)S(1)}, u32[]{:S(2)}, u32[]{:S(2)}) collective-permute-start(bf16[48,2432]{1,0:T(8,128)(2,1)S(1)} %collective-permute-done.2), channel_id=1, source_target_pairs={{0,32},{1,225},{2,34},{3,227},{4,36},{5,229},{6,38},{7,231},{8,40}... | collective-permute-start | bytes 700424 | tf_op jit(solution)/shard_map/ppermute | solution.py:28
  45.9 3.8 %collective-permute-done.3 = bf16[48,2432]{1,0:T(8,128)(2,1)S(1)} collective-permute-done((bf16[48,2432]{1,0:T(8,128)(2,1)S(1)}, bf16[48,2432]{1,0:T(8,128)(2,1)S(1)}, u32[]{:S(2)}, u32[]{:S(2)}) %collective-permute-start.3) | collective-permute-done | bytes 233504 | tf_op jit(solution)/shard_map/ppermute | solution.py:28
  49.7 2.5 %collective-permute-start.4 = (bf16[24,2432]{1,0:T(8,128)(2,1)S(1)}, bf16[24,2432]{1,0:T(8,128)(2,1)S(1)}, u32[]{:S(2)}, u32[]{:S(2)}) collective-permute-start(bf16[24,2432]{1,0:T(8,128)(2,1)S(1)} %get-tuple-element.47), channel_id=1, source_target_pairs={{0,32},{1,225},{2,34},{3,227},{4,36},{5,229},{6,38},{7,231},{8,40}... | collective-permute-start | bytes 350216 | tf_op jit(solution)/shard_map/ppermute | solution.py:28
  52.2 0.1 collective-permute-start.5
  52.4 3.8 %collective-permute-start.9 = (bf16[24,2432]{1,0:T(8,128)(2,1)S(1)}, bf16[24,2432]{1,0:T(8,128)(2,1)S(1)}, u32[]{:S(2)}, u32[]{:S(2)}) collective-permute-start(bf16[24,2432]{1,0:T(8,128)(2,1)S(1)} %get-tuple-element.54), channel_id=1, source_target_pairs={{0,32},{1,225},{2,34},{3,227},{4,36},{5,229},{6,38},{7,231},{8,40}... | collective-permute-start | bytes 350216 | tf_op jit(solution)/shard_map/ppermute | solution.py:28
  56.2 0.1 collective-permute-start.10
  56.3 0.7 collective-permute-start.14
  57.1 0.1 collective-permute-start.15
  57.3 1.3 %collective-permute-done.9 = bf16[24,2432]{1,0:T(8,128)(2,1)S(1)} collective-permute-done((bf16[24,2432]{1,0:T(8,128)(2,1)S(1)}, bf16[24,2432]{1,0:T(8,128)(2,1)S(1)}, u32[]{:S(2)}, u32[]{:S(2)}) %collective-permute-start.9) | collective-permute-done | bytes 116768 | tf_op jit(solution)/shard_map/ppermute | solution.py:28
  58.6 2.8 %collective-permute-done.14 = bf16[24,2432]{1,0:T(8,128)(2,1)S(1)} collective-permute-done((bf16[24,2432]{1,0:T(8,128)(2,1)S(1)}, bf16[24,2432]{1,0:T(8,128)(2,1)S(1)}, u32[]{:S(2)}, u32[]{:S(2)}) %collective-permute-start.14) | collective-permute-done | bytes 116768 | tf_op jit(solution)/shard_map/ppermute | solution.py:28
  61.5 0.4 fusion.9
  61.9 0.4 fusion.13
  62.3 0.4 fusion.7
  62.8 0.4 fusion.11
  63.2 0.4 fusion
  63.6 0.4 multiply_convert_fusion
  64.0 0.3 copy-done
  64.3 0.5 fusion.60
  64.8 0.5 fusion.61
  65.3 0.1 collective-permute-start.24
  65.4 2.0 %collective-permute-start.23 = (bf16[24,3584]{1,0:T(8,128)(2,1)S(1)}, bf16[24,3584]{1,0:T(8,128)(2,1)S(1)}, u32[]{:S(2)}, u32[]{:S(2)}) collective-permute-start(bf16[24,3584]{1,0:T(8,128)(2,1)S(1)} %get-tuple-element.45), channel_id=1, source_target_pairs={{0,32},{1,225},{2,34},{3,227},{4,36},{5,229},{6,38},{7,231},{8,40}... | collective-permute-start | bytes 516104 | tf_op jit(solution)/shard_map/ppermute | solution.py:28
  67.4 0.5 collective-permute-start.17
  67.9 2.4 %collective-permute-start.16 = (bf16[24,3584]{1,0:T(8,128)(2,1)S(1)}, bf16[24,3584]{1,0:T(8,128)(2,1)S(1)}, u32[]{:S(2)}, u32[]{:S(2)}) collective-permute-start(bf16[24,3584]{1,0:T(8,128)(2,1)S(1)} %get-tuple-element.43), channel_id=1, source_target_pairs={{0,32},{1,225},{2,34},{3,227},{4,36},{5,229},{6,38},{7,231},{8,40}... | collective-permute-start | bytes 516104 | tf_op jit(solution)/shard_map/ppermute | solution.py:28
  70.3 2.2 %collective-permute-done.24 = bf16[24,3584]{1,0:T(8,128)(2,1)S(1)} collective-permute-done((bf16[24,3584]{1,0:T(8,128)(2,1)S(1)}, bf16[24,3584]{1,0:T(8,128)(2,1)S(1)}, u32[]{:S(2)}, u32[]{:S(2)}) %collective-permute-start.24) | collective-permute-done | bytes 172064 | tf_op jit(solution)/shard_map/ppermute | solution.py:28
  72.5 0.5 collective-permute-done.23
  73.1 0.1 fusion.26
  73.2 2.1 %collective-permute-start.25 = (bf16[24,3584]{1,0:T(8,128)(2,1)S(1)}, bf16[24,3584]{1,0:T(8,128)(2,1)S(1)}, u32[]{:S(2)}, u32[]{:S(2)}) collective-permute-start(bf16[24,3584]{1,0:T(8,128)(2,1)S(1)} %get-tuple-element.28), channel_id=1, source_target_pairs={{0,32},{1,225},{2,34},{3,227},{4,36},{5,229},{6,38},{7,231},{8,40}... | collective-permute-start | bytes 516104 | tf_op jit(solution)/shard_map/ppermute | solution.py:28
  75.3 0.9 collective-permute-done.17
  76.3 2.4 %collective-permute-start.18 = (bf16[24,3584]{1,0:T(8,128)(2,1)S(1)}, bf16[24,3584]{1,0:T(8,128)(2,1)S(1)}, u32[]{:S(2)}, u32[]{:S(2)}) collective-permute-start(bf16[24,3584]{1,0:T(8,128)(2,1)S(1)} %get-tuple-element.22), channel_id=1, source_target_pairs={{0,32},{1,225},{2,34},{3,227},{4,36},{5,229},{6,38},{7,231},{8,40}... | collective-permute-start | bytes 516104 | tf_op jit(solution)/shard_map/ppermute | solution.py:28
  78.8 0.8 collective-permute-done.25
  79.5 3.8 %collective-permute-done.26 = bf16[24,3584]{1,0:T(8,128)(2,1)S(1)} collective-permute-done((bf16[24,3584]{1,0:T(8,128)(2,1)S(1)}, bf16[24,3584]{1,0:T(8,128)(2,1)S(1)}, u32[]{:S(2)}, u32[]{:S(2)}) %collective-permute-start.26) | collective-permute-done | bytes 172064 | tf_op jit(solution)/shard_map/ppermute | solution.py:28
  83.4 3.2 %collective-permute-start.27 = (bf16[24,3584]{1,0:T(8,128)(2,1)S(1)}, bf16[24,3584]{1,0:T(8,128)(2,1)S(1)}, u32[]{:S(2)}, u32[]{:S(2)}) collective-permute-start(bf16[24,3584]{1,0:T(8,128)(2,1)S(1)} %get-tuple-element.30), channel_id=1, source_target_pairs={{0,32},{1,225},{2,34},{3,227},{4,36},{5,229},{6,38},{7,231},{8,40}... | collective-permute-start | bytes 516104 | tf_op jit(solution)/shard_map/ppermute | solution.py:28
  86.7 0.2 collective-permute-done.19
  86.9 3.0 %collective-permute-start.20 = (bf16[24,3584]{1,0:T(8,128)(2,1)S(1)}, bf16[24,3584]{1,0:T(8,128)(2,1)S(1)}, u32[]{:S(2)}, u32[]{:S(2)}) collective-permute-start(bf16[24,3584]{1,0:T(8,128)(2,1)S(1)} %get-tuple-element.24), channel_id=1, source_target_pairs={{0,32},{1,225},{2,34},{3,227},{4,36},{5,229},{6,38},{7,231},{8,40}... | collective-permute-start | bytes 516104 | tf_op jit(solution)/shard_map/ppermute | solution.py:28
  90.0 2.4 %collective-permute-start.28 = (bf16[24,3584]{1,0:T(8,128)(2,1)S(1)}, bf16[24,3584]{1,0:T(8,128)(2,1)S(1)}, u32[]{:S(2)}, u32[]{:S(2)}) collective-permute-start(bf16[24,3584]{1,0:T(8,128)(2,1)S(1)} %fusion.23), channel_id=1, source_target_pairs={{0,32},{1,225},{2,34},{3,227},{4,36},{5,229},{6,38},{7,231},{8,40}... | collective-permute-start | bytes 516104 | tf_op jit(solution)/shard_map/ppermute | solution.py:28
  92.4 2.1 %collective-permute-done.20 = bf16[24,3584]{1,0:T(8,128)(2,1)S(1)} collective-permute-done((bf16[24,3584]{1,0:T(8,128)(2,1)S(1)}, bf16[24,3584]{1,0:T(8,128)(2,1)S(1)}, u32[]{:S(2)}, u32[]{:S(2)}) %collective-permute-start.20) | collective-permute-done | bytes 172064 | tf_op jit(solution)/shard_map/ppermute | solution.py:28
  94.6 2.6 %collective-permute-start.21 = (bf16[24,3584]{1,0:T(8,128)(2,1)S(1)}, bf16[24,3584]{1,0:T(8,128)(2,1)S(1)}, u32[]{:S(2)}, u32[]{:S(2)}) collective-permute-start(bf16[24,3584]{1,0:T(8,128)(2,1)S(1)} %fusion.30), channel_id=1, source_target_pairs={{0,32},{1,225},{2,34},{3,227},{4,36},{5,229},{6,38},{7,231},{8,40}... | collective-permute-start | bytes 516104 | tf_op jit(solution)/shard_map/ppermute | solution.py:28
  97.1 0.3 collective-permute-done.28
  97.4 0.4 collective-permute-done.29
  97.9 2.2 %collective-permute-done.21 = bf16[24,3584]{1,0:T(8,128)(2,1)S(1)} collective-permute-done((bf16[24,3584]{1,0:T(8,128)(2,1)S(1)}, bf16[24,3584]{1,0:T(8,128)(2,1)S(1)}, u32[]{:S(2)}, u32[]{:S(2)}) %collective-permute-start.21) | collective-permute-done | bytes 172064 | tf_op jit(solution)/shard_map/ppermute | solution.py:28
  100.0 2.5 %collective-permute-done.22 = bf16[24,3584]{1,0:T(8,128)(2,1)S(1)} collective-permute-done((bf16[24,3584]{1,0:T(8,128)(2,1)S(1)}, bf16[24,3584]{1,0:T(8,128)(2,1)S(1)}, u32[]{:S(2)}, u32[]{:S(2)}) %collective-permute-start.22) | collective-permute-done | bytes 172064 | tf_op jit(solution)/shard_map/ppermute | solution.py:28
  102.6 0.4 fusion.37
  103.0 0.4 convolution_add_fusion
  103.5 0.1 collective-permute-start.30
  103.6 1.8 %collective-permute-done.30 = bf16[32,7168]{1,0:T(8,128)(2,1)S(1)} collective-permute-done((bf16[32,7168]{1,0:T(8,128)(2,1)S(1)}, bf16[32,7168]{1,0:T(8,128)(2,1)S(1)}, u32[]{:S(2)}, u32[]{:S(2)}) %collective-permute-start.30) | collective-permute-done | bytes 458784 | tf_op jit(solution)/shard_map/ppermute | solution.py:19
  105.5 0.9 reshape.16
  106.4 3.6 %all-to-all-start.1 = ((bf16[16,2,7168]{2,1,0:T(2,128)(2,1)}), bf16[16,2,7168]{2,1,0:T(2,128)(2,1)S(1)}, u32[]{:S(2)}, u32[]{:S(2)}) async-start(bf16[16,2,7168]{2,1,0:T(2,128)(2,1)} %reshape.16), calls=%async_computation.1 | async-start | bytes 917504 | tf_op jit(solution)/shard_map/all_to_all | solution.py:240
  110.0 0.5 fusion.48
  110.5 10.8 %all-to-all-done.1 = bf16[16,2,7168]{2,1,0:T(2,128)(2,1)S(1)} async-done(((bf16[16,2,7168]{2,1,0:T(2,128)(2,1)}), bf16[16,2,7168]{2,1,0:T(2,128)(2,1)S(1)}, u32[]{:S(2)}, u32[]{:S(2)}) %all-to-all-start.1) | async-done | bytes 458784 | tf_op jit(solution)/shard_map/all_to_all | solution.py:240
  121.4 1.0 reduce_sum.23
  (57 shorter events, 1.2 us)
Async XLA Ops:
  20.5 1.9 %collective-permute-start = (bf16[32,7296]{1,0:T(8,128)(2,1)S(1)}, bf16[32,7296]{1,0:T(8,128)(2,1)S(1)}, u32[]{:S(2)}, u32[]{:S(2)}) collective-permute-start(bf16[32,7296]{1,0:T(8,128)(2,1)S(1)} %reshape.15.near), channel_id=1, source_target_pairs={{0,1},{1,0},{2,3},{3,2},{4,5},{5,4},{6,7},{7,6},{8,9},{9,8},{10,11... | collective-permute-start | bytes 1400840 | tf_op jit(solution)/shard_map/ppermute | solution.py:19
  23.4 6.3 %collective-permute-start.6 = (bf16[48,2432]{1,0:T(8,128)(2,1)S(1)}, bf16[48,2432]{1,0:T(8,128)(2,1)S(1)}, u32[]{:S(2)}, u32[]{:S(2)}) collective-permute-start(bf16[48,2432]{1,0:T(8,128)(2,1)S(1)} %get-tuple-element.20), channel_id=1, source_target_pairs={{0,32},{1,225},{2,34},{3,227},{4,36},{5,229},{6,38},{7,231},{8,40}... | collective-permute-start | bytes 700424 | tf_op jit(solution)/shard_map/ppermute | solution.py:28
  25.4 6.7 %collective-permute-start.11 = (bf16[48,2432]{1,0:T(8,128)(2,1)S(1)}, bf16[48,2432]{1,0:T(8,128)(2,1)S(1)}, u32[]{:S(2)}, u32[]{:S(2)}) collective-permute-start(bf16[48,2432]{1,0:T(8,128)(2,1)S(1)} %get-tuple-element.21), channel_id=1, source_target_pairs={{0,32},{1,225},{2,34},{3,227},{4,36},{5,229},{6,38},{7,231},{8,40}... | collective-permute-start | bytes 700424 | tf_op jit(solution)/shard_map/ppermute | solution.py:28
  28.5 7.3 %collective-permute-start.1 = (bf16[48,2432]{1,0:T(8,128)(2,1)S(1)}, bf16[48,2432]{1,0:T(8,128)(2,1)S(1)}, u32[]{:S(2)}, u32[]{:S(2)}) collective-permute-start(bf16[48,2432]{1,0:T(8,128)(2,1)S(1)} %get-tuple-element.19), channel_id=1, source_target_pairs={{0,32},{1,225},{2,34},{3,227},{4,36},{5,229},{6,38},{7,231},{8,40}... | collective-permute-start | bytes 700424 | tf_op jit(solution)/shard_map/ppermute | solution.py:28
  29.6 8.8 %collective-permute-start.7 = (bf16[48,2432]{1,0:T(8,128)(2,1)S(1)}, bf16[48,2432]{1,0:T(8,128)(2,1)S(1)}, u32[]{:S(2)}, u32[]{:S(2)}) collective-permute-start(bf16[48,2432]{1,0:T(8,128)(2,1)S(1)} %collective-permute-done.6), channel_id=1, source_target_pairs={{0,32},{1,225},{2,34},{3,227},{4,36},{5,229},{6,38},{7,231},{8,40}... | collective-permute-start | bytes 700424 | tf_op jit(solution)/shard_map/ppermute | solution.py:28
  32.1 8.9 %collective-permute-start.12 = (bf16[48,2432]{1,0:T(8,128)(2,1)S(1)}, bf16[48,2432]{1,0:T(8,128)(2,1)S(1)}, u32[]{:S(2)}, u32[]{:S(2)}) collective-permute-start(bf16[48,2432]{1,0:T(8,128)(2,1)S(1)} %collective-permute-done.11), channel_id=1, source_target_pairs={{0,32},{1,225},{2,34},{3,227},{4,36},{5,229},{6,38},{7,231},{8,40}... | collective-permute-start | bytes 700424 | tf_op jit(solution)/shard_map/ppermute | solution.py:28
  35.8 7.5 %collective-permute-start.2 = (bf16[48,2432]{1,0:T(8,128)(2,1)S(1)}, bf16[48,2432]{1,0:T(8,128)(2,1)S(1)}, u32[]{:S(2)}, u32[]{:S(2)}) collective-permute-start(bf16[48,2432]{1,0:T(8,128)(2,1)S(1)} %collective-permute-done.1), channel_id=1, source_target_pairs={{0,32},{1,225},{2,34},{3,227},{4,36},{5,229},{6,38},{7,231},{8,40}... | collective-permute-start | bytes 700424 | tf_op jit(solution)/shard_map/ppermute | solution.py:28
  38.4 13.9 %collective-permute-start.8 = (bf16[48,2432]{1,0:T(8,128)(2,1)S(1)}, bf16[48,2432]{1,0:T(8,128)(2,1)S(1)}, u32[]{:S(2)}, u32[]{:S(2)}) collective-permute-start(bf16[48,2432]{1,0:T(8,128)(2,1)S(1)} %collective-permute-done.7), channel_id=1, source_target_pairs={{0,32},{1,225},{2,34},{3,227},{4,36},{5,229},{6,38},{7,231},{8,40}... | collective-permute-start | bytes 700424 | tf_op jit(solution)/shard_map/ppermute | solution.py:28
  41.0 15.3 %collective-permute-start.13 = (bf16[48,2432]{1,0:T(8,128)(2,1)S(1)}, bf16[48,2432]{1,0:T(8,128)(2,1)S(1)}, u32[]{:S(2)}, u32[]{:S(2)}) collective-permute-start(bf16[48,2432]{1,0:T(8,128)(2,1)S(1)} %collective-permute-done.12), channel_id=1, source_target_pairs={{0,32},{1,225},{2,34},{3,227},{4,36},{5,229},{6,38},{7,231},{8,40}... | collective-permute-start | bytes 700424 | tf_op jit(solution)/shard_map/ppermute | solution.py:28
  43.3 6.4 %collective-permute-start.3 = (bf16[48,2432]{1,0:T(8,128)(2,1)S(1)}, bf16[48,2432]{1,0:T(8,128)(2,1)S(1)}, u32[]{:S(2)}, u32[]{:S(2)}) collective-permute-start(bf16[48,2432]{1,0:T(8,128)(2,1)S(1)} %collective-permute-done.2), channel_id=1, source_target_pairs={{0,32},{1,225},{2,34},{3,227},{4,36},{5,229},{6,38},{7,231},{8,40}... | collective-permute-start | bytes 700424 | tf_op jit(solution)/shard_map/ppermute | solution.py:28
  45.9 15.6 %copy-start.1 = (bf16[1,2,7168,128]{3,2,1,0:T(8,128)(2,1)S(1)}, bf16[1,2,7168,128]{3,2,1,0:T(8,128)(2,1)}, u32[]{:S(2)}) copy-start(bf16[1,2,7168,128]{3,2,1,0:T(8,128)(2,1)} %param.12) | copy-start | bytes 11010052
  49.7 7.4 %collective-permute-start.4 = (bf16[24,2432]{1,0:T(8,128)(2,1)S(1)}, bf16[24,2432]{1,0:T(8,128)(2,1)S(1)}, u32[]{:S(2)}, u32[]{:S(2)}) collective-permute-start(bf16[24,2432]{1,0:T(8,128)(2,1)S(1)} %get-tuple-element.47), channel_id=1, source_target_pairs={{0,32},{1,225},{2,34},{3,227},{4,36},{5,229},{6,38},{7,231},{8,40}... | collective-permute-start | bytes 350216 | tf_op jit(solution)/shard_map/ppermute | solution.py:28
  52.2 10.9 %collective-permute-start.5 = (bf16[72,2432]{1,0:T(8,128)(2,1)S(1)}, bf16[72,2432]{1,0:T(8,128)(2,1)S(1)}, u32[]{:S(2)}, u32[]{:S(2)}) collective-permute-start(bf16[72,2432]{1,0:T(8,128)(2,1)S(1)} %pad_maximum_fusion), channel_id=1, source_target_pairs={{0,1},{1,0},{2,3},{3,2},{4,5},{5,4},{6,7},{7,6},{8,9},{9,8},{10,11... | collective-permute-start | bytes 1050632 | tf_op jit(solution)/shard_map/ppermute | solution.py:19
  52.4 6.2 %collective-permute-start.9 = (bf16[24,2432]{1,0:T(8,128)(2,1)S(1)}, bf16[24,2432]{1,0:T(8,128)(2,1)S(1)}, u32[]{:S(2)}, u32[]{:S(2)}) collective-permute-start(bf16[24,2432]{1,0:T(8,128)(2,1)S(1)} %get-tuple-element.54), channel_id=1, source_target_pairs={{0,32},{1,225},{2,34},{3,227},{4,36},{5,229},{6,38},{7,231},{8,40}... | collective-permute-start | bytes 350216 | tf_op jit(solution)/shard_map/ppermute | solution.py:28
  56.2 5.2 %collective-permute-start.10 = (bf16[72,2432]{1,0:T(8,128)(2,1)S(1)}, bf16[72,2432]{1,0:T(8,128)(2,1)S(1)}, u32[]{:S(2)}, u32[]{:S(2)}) collective-permute-start(bf16[72,2432]{1,0:T(8,128)(2,1)S(1)} %pad_maximum_fusion.1), channel_id=1, source_target_pairs={{0,1},{1,0},{2,3},{3,2},{4,5},{5,4},{6,7},{7,6},{8,9},{9,8},{10,11... | collective-permute-start | bytes 1050632 | tf_op jit(solution)/shard_map/ppermute | solution.py:19
  56.3 5.1 %collective-permute-start.14 = (bf16[24,2432]{1,0:T(8,128)(2,1)S(1)}, bf16[24,2432]{1,0:T(8,128)(2,1)S(1)}, u32[]{:S(2)}, u32[]{:S(2)}) collective-permute-start(bf16[24,2432]{1,0:T(8,128)(2,1)S(1)} %get-tuple-element.61), channel_id=1, source_target_pairs={{0,32},{1,225},{2,34},{3,227},{4,36},{5,229},{6,38},{7,231},{8,40}... | collective-permute-start | bytes 350216 | tf_op jit(solution)/shard_map/ppermute | solution.py:28
  57.1 5.2 %collective-permute-start.15 = (bf16[72,2432]{1,0:T(8,128)(2,1)S(1)}, bf16[72,2432]{1,0:T(8,128)(2,1)S(1)}, u32[]{:S(2)}, u32[]{:S(2)}) collective-permute-start(bf16[72,2432]{1,0:T(8,128)(2,1)S(1)} %pad_maximum_fusion.2), channel_id=1, source_target_pairs={{0,1},{1,0},{2,3},{3,2},{4,5},{5,4},{6,7},{7,6},{8,9},{9,8},{10,11... | collective-permute-start | bytes 1050632 | tf_op jit(solution)/shard_map/ppermute | solution.py:19
  62.8 1.5 %copy-start = (bf16[1,128,7168]{2,1,0:T(8,128)(2,1)S(1)}, bf16[1,128,7168]{2,1,0:T(8,128)(2,1)}, u32[]{:S(2)}) copy-start(bf16[1,128,7168]{2,1,0:T(8,128)(2,1)} %param.13) | copy-start | bytes 5505028
  65.3 7.2 %collective-permute-start.24 = (bf16[24,3584]{1,0:T(8,128)(2,1)S(1)}, bf16[24,3584]{1,0:T(8,128)(2,1)S(1)}, u32[]{:S(2)}, u32[]{:S(2)}) collective-permute-start(bf16[24,3584]{1,0:T(8,128)(2,1)S(1)} %get-tuple-element.44), channel_id=1, source_target_pairs={{0,224},{1,33},{2,226},{3,35},{4,228},{5,37},{6,230},{7,39},{8,232... | collective-permute-start | bytes 516104 | tf_op jit(solution)/shard_map/ppermute | solution.py:28
  65.4 7.7 %collective-permute-start.23 = (bf16[24,3584]{1,0:T(8,128)(2,1)S(1)}, bf16[24,3584]{1,0:T(8,128)(2,1)S(1)}, u32[]{:S(2)}, u32[]{:S(2)}) collective-permute-start(bf16[24,3584]{1,0:T(8,128)(2,1)S(1)} %get-tuple-element.45), channel_id=1, source_target_pairs={{0,32},{1,225},{2,34},{3,227},{4,36},{5,229},{6,38},{7,231},{8,40}... | collective-permute-start | bytes 516104 | tf_op jit(solution)/shard_map/ppermute | solution.py:28
  67.4 8.8 %collective-permute-start.17 = (bf16[24,3584]{1,0:T(8,128)(2,1)S(1)}, bf16[24,3584]{1,0:T(8,128)(2,1)S(1)}, u32[]{:S(2)}, u32[]{:S(2)}) collective-permute-start(bf16[24,3584]{1,0:T(8,128)(2,1)S(1)} %get-tuple-element.42), channel_id=1, source_target_pairs={{0,224},{1,33},{2,226},{3,35},{4,228},{5,37},{6,230},{7,39},{8,232... | collective-permute-start | bytes 516104 | tf_op jit(solution)/shard_map/ppermute | solution.py:28
  67.9 8.3 %collective-permute-start.16 = (bf16[24,3584]{1,0:T(8,128)(2,1)S(1)}, bf16[24,3584]{1,0:T(8,128)(2,1)S(1)}, u32[]{:S(2)}, u32[]{:S(2)}) collective-permute-start(bf16[24,3584]{1,0:T(8,128)(2,1)S(1)} %get-tuple-element.43), channel_id=1, source_target_pairs={{0,32},{1,225},{2,34},{3,227},{4,36},{5,229},{6,38},{7,231},{8,40}... | collective-permute-start | bytes 516104 | tf_op jit(solution)/shard_map/ppermute | solution.py:28
  73.2 6.3 %collective-permute-start.25 = (bf16[24,3584]{1,0:T(8,128)(2,1)S(1)}, bf16[24,3584]{1,0:T(8,128)(2,1)S(1)}, u32[]{:S(2)}, u32[]{:S(2)}) collective-permute-start(bf16[24,3584]{1,0:T(8,128)(2,1)S(1)} %get-tuple-element.28), channel_id=1, source_target_pairs={{0,32},{1,225},{2,34},{3,227},{4,36},{5,229},{6,38},{7,231},{8,40}... | collective-permute-start | bytes 516104 | tf_op jit(solution)/shard_map/ppermute | solution.py:28
  75.3 8.0 %collective-permute-start.26 = (bf16[24,3584]{1,0:T(8,128)(2,1)S(1)}, bf16[24,3584]{1,0:T(8,128)(2,1)S(1)}, u32[]{:S(2)}, u32[]{:S(2)}) collective-permute-start(bf16[24,3584]{1,0:T(8,128)(2,1)S(1)} %get-tuple-element.29), channel_id=1, source_target_pairs={{0,224},{1,33},{2,226},{3,35},{4,228},{5,37},{6,230},{7,39},{8,232... | collective-permute-start | bytes 516104 | tf_op jit(solution)/shard_map/ppermute | solution.py:28
  76.3 10.3 %collective-permute-start.18 = (bf16[24,3584]{1,0:T(8,128)(2,1)S(1)}, bf16[24,3584]{1,0:T(8,128)(2,1)S(1)}, u32[]{:S(2)}, u32[]{:S(2)}) collective-permute-start(bf16[24,3584]{1,0:T(8,128)(2,1)S(1)} %get-tuple-element.22), channel_id=1, source_target_pairs={{0,32},{1,225},{2,34},{3,227},{4,36},{5,229},{6,38},{7,231},{8,40}... | collective-permute-start | bytes 516104 | tf_op jit(solution)/shard_map/ppermute | solution.py:28
  78.8 8.1 %collective-permute-start.19 = (bf16[24,3584]{1,0:T(8,128)(2,1)S(1)}, bf16[24,3584]{1,0:T(8,128)(2,1)S(1)}, u32[]{:S(2)}, u32[]{:S(2)}) collective-permute-start(bf16[24,3584]{1,0:T(8,128)(2,1)S(1)} %get-tuple-element.23), channel_id=1, source_target_pairs={{0,224},{1,33},{2,226},{3,35},{4,228},{5,37},{6,230},{7,39},{8,232... | collective-permute-start | bytes 516104 | tf_op jit(solution)/shard_map/ppermute | solution.py:28
  83.4 6.5 %collective-permute-start.27 = (bf16[24,3584]{1,0:T(8,128)(2,1)S(1)}, bf16[24,3584]{1,0:T(8,128)(2,1)S(1)}, u32[]{:S(2)}, u32[]{:S(2)}) collective-permute-start(bf16[24,3584]{1,0:T(8,128)(2,1)S(1)} %get-tuple-element.30), channel_id=1, source_target_pairs={{0,32},{1,225},{2,34},{3,227},{4,36},{5,229},{6,38},{7,231},{8,40}... | collective-permute-start | bytes 516104 | tf_op jit(solution)/shard_map/ppermute | solution.py:28
  86.9 7.6 %collective-permute-start.20 = (bf16[24,3584]{1,0:T(8,128)(2,1)S(1)}, bf16[24,3584]{1,0:T(8,128)(2,1)S(1)}, u32[]{:S(2)}, u32[]{:S(2)}) collective-permute-start(bf16[24,3584]{1,0:T(8,128)(2,1)S(1)} %get-tuple-element.24), channel_id=1, source_target_pairs={{0,32},{1,225},{2,34},{3,227},{4,36},{5,229},{6,38},{7,231},{8,40}... | collective-permute-start | bytes 516104 | tf_op jit(solution)/shard_map/ppermute | solution.py:28
  90.0 7.4 %collective-permute-start.28 = (bf16[24,3584]{1,0:T(8,128)(2,1)S(1)}, bf16[24,3584]{1,0:T(8,128)(2,1)S(1)}, u32[]{:S(2)}, u32[]{:S(2)}) collective-permute-start(bf16[24,3584]{1,0:T(8,128)(2,1)S(1)} %fusion.23), channel_id=1, source_target_pairs={{0,32},{1,225},{2,34},{3,227},{4,36},{5,229},{6,38},{7,231},{8,40}... | collective-permute-start | bytes 516104 | tf_op jit(solution)/shard_map/ppermute | solution.py:28
  92.4 5.4 %collective-permute-start.29 = (bf16[24,3584]{1,0:T(8,128)(2,1)S(1)}, bf16[24,3584]{1,0:T(8,128)(2,1)S(1)}, u32[]{:S(2)}, u32[]{:S(2)}) collective-permute-start(bf16[24,3584]{1,0:T(8,128)(2,1)S(1)} %get-tuple-element.33), channel_id=1, source_target_pairs={{0,224},{1,33},{2,226},{3,35},{4,228},{5,37},{6,230},{7,39},{8,232... | collective-permute-start | bytes 516104 | tf_op jit(solution)/shard_map/ppermute | solution.py:28
  94.6 5.5 %collective-permute-start.21 = (bf16[24,3584]{1,0:T(8,128)(2,1)S(1)}, bf16[24,3584]{1,0:T(8,128)(2,1)S(1)}, u32[]{:S(2)}, u32[]{:S(2)}) collective-permute-start(bf16[24,3584]{1,0:T(8,128)(2,1)S(1)} %fusion.30), channel_id=1, source_target_pairs={{0,32},{1,225},{2,34},{3,227},{4,36},{5,229},{6,38},{7,231},{8,40}... | collective-permute-start | bytes 516104 | tf_op jit(solution)/shard_map/ppermute | solution.py:28
  97.1 5.4 %collective-permute-start.22 = (bf16[24,3584]{1,0:T(8,128)(2,1)S(1)}, bf16[24,3584]{1,0:T(8,128)(2,1)S(1)}, u32[]{:S(2)}, u32[]{:S(2)}) collective-permute-start(bf16[24,3584]{1,0:T(8,128)(2,1)S(1)} %get-tuple-element.27), channel_id=1, source_target_pairs={{0,224},{1,33},{2,226},{3,35},{4,228},{5,37},{6,230},{7,39},{8,232... | collective-permute-start | bytes 516104 | tf_op jit(solution)/shard_map/ppermute | solution.py:28
  103.5 1.9 %collective-permute-start.30 = (bf16[32,7168]{1,0:T(8,128)(2,1)S(1)}, bf16[32,7168]{1,0:T(8,128)(2,1)S(1)}, u32[]{:S(2)}, u32[]{:S(2)}) collective-permute-start(bf16[32,7168]{1,0:T(8,128)(2,1)S(1)} %slice.421), channel_id=1, source_target_pairs={{0,1},{1,0},{2,3},{3,2},{4,5},{5,4},{6,7},{7,6},{8,9},{9,8},{10,11... | collective-permute-start | bytes 1376264 | tf_op jit(solution)/shard_map/ppermute | solution.py:19
  106.4 14.9 %all-to-all-start.1 = ((bf16[16,2,7168]{2,1,0:T(2,128)(2,1)}), bf16[16,2,7168]{2,1,0:T(2,128)(2,1)S(1)}, u32[]{:S(2)}, u32[]{:S(2)}) async-start(bf16[16,2,7168]{2,1,0:T(2,128)(2,1)} %reshape.16), calls=%async_computation.1 | async-start | bytes 917504 | tf_op jit(solution)/shard_map/all_to_all | solution.py:240

commit v4 on v3

--- a/solution.py
+++ b/solution.py
@@ -12,6 +12,7 @@
 META = 128
 PREP_VMEM = 60 * 2**20
 CHUNKS = 3
+TILE = 512
 SUM_CHUNKS = 2
 
 
@@ -149,6 +150,31 @@
     packed[-1][:, cols[-1].stop - cols[-1].start :] = tail
 
 
+def mix_kernel(near, mix, *refs):
+    chunks, mine, theirs = refs[:-2], refs[-2], refs[-1]
+    at = 0
+    for chunk in chunks:
+        for k in range(0, chunk.shape[1], TILE):
+            value = sum(
+                lax.dot_general(
+                    mix[i], chunk[:, k : k + TILE], (((0,), (0,)), ((), ())),
+                    preferred_element_type=F32,
+                )
+                for i in range(2)
+            )
+            mine[:, at : at + TILE] = value[:near]
+            theirs[:, at : at + TILE] = value[near:].astype(BF16)
+            at += TILE
+
+
+def close_kernel(mine, other, result):
+    peers, rows, _ = result.shape
+    for k in range(0, result.shape[2], TILE):
+        value = (mine[:, k : k + TILE] + other[:, k : k + TILE].astype(F32)).astype(BF16)
+        for peer in range(peers):
+            result[peer, :, k : k + TILE] = value[peer * rows : (peer + 1) * rows]
+
+
 def body(tokens, expert_ids, replica, route_weight, spare_plan, w_in, w_down):
     rows, width = tokens.shape
     top = expert_ids.shape[1]
@@ -226,19 +252,28 @@
     def block(c):
         return lambda s: down[c][place_of[s] * MOST : (place_of[s] + 1) * MOST]
 
-    summed = jnp.concatenate(
-        reduce_ring([block(c) for c in range(SUM_CHUNKS)], count, groups), 1
-    )
-
-    share = sum(
-        lax.dot_general(mix[i], summed, (((0,), (0,)), ((), ())), preferred_element_type=F32)
-        for i in range(2)
-    )
+    sums = reduce_ring([block(c) for c in range(SUM_CHUNKS)], count, groups)
+
     near_count = peers * rows
-    swapped = core_swap(share[near_count:].astype(BF16), groups)
-    both = (share[:near_count] + swapped.astype(F32)).astype(BF16)
+    mine, theirs = pl.pallas_call(
+        functools.partial(mix_kernel, near_count),
+        out_shape=[
+            jax.ShapeDtypeStruct((near_count, width), F32),
+            jax.ShapeDtypeStruct((near_count, width), BF16),
+        ],
+        in_specs=[vmem] * (1 + SUM_CHUNKS),
+        out_specs=[vmem] * 2,
+        compiler_params=grant,
+    )(mix, *sums)
+    both = pl.pallas_call(
+        close_kernel,
+        out_shape=jax.ShapeDtypeStruct((peers, rows, width), BF16),
+        in_specs=[vmem] * 2,
+        out_specs=vmem,
+        compiler_params=grant,
+    )(mine, core_swap(theirs, groups))
     back = lax.all_to_all(
-        both.reshape(peers, rows, width), "expert", 0, 0, axis_index_groups=same_core, tiled=True
+        both, "expert", 0, 0, axis_index_groups=same_core, tiled=True
     )
     layer_output = jnp.sum(back.astype(F32), 0).astype(BF16)
     return layer_output, slot_load

time: 123 us -> 122 us (level)
  Pallas kernels: 2.71 us -> 4.32 us
    pallas_call x0 -> x2, Pallas kernels: none -> 1.56 us  [the longest x1 0.9 us: body(): pl.pallas_call(close_kernel, out_shape=jax.ShapeDtypeStruct((peers, rows,...]
where the time goes in v4:
time: 122 us
  starting transfers between devices  54 us (44%)
  waiting for transfers between devices  38.3 us (31%)
  blocking collectives  17.9 us (15%)
  Pallas kernels  4.32 us (4%)
  matrix products  3.39 us (3%)
  other arithmetic  2.16 us (2%)
    ppermute x26, starting transfers between devices, core_ring(): return lax.ppermute(value, ('attn', 'expert'), pairs)  50 us
    ppermute x26, waiting for transfers between devices, core_ring(): return lax.ppermute(value, ('attn', 'expert'), pairs)  23.8 us
    all_to_all x1, blocking collectives, body(): lax.all_to_all(spread, 'expert', 0, 0, axis_index_groups=same_core, tiled...  17.9 us
    all_to_all x1, waiting for transfers between devices, body(): lax.all_to_all(both, 'expert', 0, 0, axis_index_groups=same_core, tiled=T...  10.8 us
    ppermute x5, waiting for transfers between devices, core_swap(): return lax.ppermute(value, 'expert', [(i, i ^ 1) for i in range(groups)])  3.63 us
    all_to_all x1, starting transfers between devices, body(): lax.all_to_all(both, 'expert', 0, 0, axis_index_groups=same_core, tiled=T...  3.56 us
  transfers between devices with their start and end apart: 32, of which 17 were waited for; matrix products, arithmetic and copies ran while one was open for 3% of the time, Pallas kernels for 0%

profile of v4, /device:TPU:64, one launch (start us, length us, event | category | flops | bytes accessed | tf_op | source)
XLA Modules:
  0.0 122.0 jit_solution(4134044639121061262)
XLA Ops:
  0.6 1.7 %shard_map.86 = bf16[16,2,7296]{2,1,0:T(2,128)(2,1)} custom-call(bf16[2,7168]{1,0:T(2,128)(2,1)} %refs_0_.1, s32[2,8]{1,0:T(2,128)} %refs_1_.1, s32[2,8]{1,0:T(2,128)} %refs_2_.1, f32[2,8]{1,0:T(2,128)} %refs_3_.1, s32[32]{0:T(128)} %refs_4_.1), custom_call_target="tpu_custom_call" | custom-call | tf_op jit(solution)/shard_map/pallas_call | solution.py:190
  2.4 17.9 %all_to_all.10 = bf16[16,2,7296]{2,1,0:T(2,128)(2,1)S(1)} all-to-all(bf16[16,2,7296]{2,1,0:T(2,128)(2,1)} %shard_map.86), channel_id=1, replica_groups={{0,2,4,6,8,10,12,14,16,18,20,22,24,26,28,30},{1,3,5,7,9,11,13,15,17,19,..., dimensions={0} | all-to-all | bytes 933888 | tf_op jit(solution)/shard_map/all_to_all | solution.py:200
  20.3 0.2 reshape.12.near
  20.5 0.1 collective-permute-start
  20.6 1.8 %collective-permute-done.far = bf16[32,7296]{1,0:T(8,128)(2,1)S(1)} collective-permute-done((bf16[32,7296]{1,0:T(8,128)(2,1)S(1)}, bf16[32,7296]{1,0:T(8,128)(2,1)S(1)}, u32[]{:S(2)}, u32[]{:S(2)}) %collective-permute-start) | collective-permute-done | bytes 466976 | tf_op jit(solution)/shard_map/ppermute | solution.py:20
  22.4 1.0 shard_map.87
  23.4 2.0 %collective-permute-start.6 = (bf16[48,2432]{1,0:T(8,128)(2,1)S(1)}, bf16[48,2432]{1,0:T(8,128)(2,1)S(1)}, u32[]{:S(2)}, u32[]{:S(2)}) collective-permute-start(bf16[48,2432]{1,0:T(8,128)(2,1)S(1)} %get-tuple-element.22), channel_id=1, source_target_pairs={{0,32},{1,225},{2,34},{3,227},{4,36},{5,229},{6,38},{7,231},{8,40}... | collective-permute-start | bytes 700424 | tf_op jit(solution)/shard_map/ppermute | solution.py:29
  25.4 3.1 %collective-permute-start.11 = (bf16[48,2432]{1,0:T(8,128)(2,1)S(1)}, bf16[48,2432]{1,0:T(8,128)(2,1)S(1)}, u32[]{:S(2)}, u32[]{:S(2)}) collective-permute-start(bf16[48,2432]{1,0:T(8,128)(2,1)S(1)} %get-tuple-element.23), channel_id=1, source_target_pairs={{0,32},{1,225},{2,34},{3,227},{4,36},{5,229},{6,38},{7,231},{8,40}... | collective-permute-start | bytes 700424 | tf_op jit(solution)/shard_map/ppermute | solution.py:29
  28.5 1.1 collective-permute-start.1
  29.7 2.4 %collective-permute-start.7 = (bf16[48,2432]{1,0:T(8,128)(2,1)S(1)}, bf16[48,2432]{1,0:T(8,128)(2,1)S(1)}, u32[]{:S(2)}, u32[]{:S(2)}) collective-permute-start(bf16[48,2432]{1,0:T(8,128)(2,1)S(1)} %collective-permute-done.6), channel_id=1, source_target_pairs={{0,32},{1,225},{2,34},{3,227},{4,36},{5,229},{6,38},{7,231},{8,40}... | collective-permute-start | bytes 700424 | tf_op jit(solution)/shard_map/ppermute | solution.py:29
  32.1 3.7 %collective-permute-start.12 = (bf16[48,2432]{1,0:T(8,128)(2,1)S(1)}, bf16[48,2432]{1,0:T(8,128)(2,1)S(1)}, u32[]{:S(2)}, u32[]{:S(2)}) collective-permute-start(bf16[48,2432]{1,0:T(8,128)(2,1)S(1)} %collective-permute-done.11), channel_id=1, source_target_pairs={{0,32},{1,225},{2,34},{3,227},{4,36},{5,229},{6,38},{7,231},{8,40}... | collective-permute-start | bytes 700424 | tf_op jit(solution)/shard_map/ppermute | solution.py:29
  35.8 2.5 %collective-permute-start.2 = (bf16[48,2432]{1,0:T(8,128)(2,1)S(1)}, bf16[48,2432]{1,0:T(8,128)(2,1)S(1)}, u32[]{:S(2)}, u32[]{:S(2)}) collective-permute-start(bf16[48,2432]{1,0:T(8,128)(2,1)S(1)} %collective-permute-done.1), channel_id=1, source_target_pairs={{0,32},{1,225},{2,34},{3,227},{4,36},{5,229},{6,38},{7,231},{8,40}... | collective-permute-start | bytes 700424 | tf_op jit(solution)/shard_map/ppermute | solution.py:29
  38.4 2.6 %collective-permute-start.8 = (bf16[48,2432]{1,0:T(8,128)(2,1)S(1)}, bf16[48,2432]{1,0:T(8,128)(2,1)S(1)}, u32[]{:S(2)}, u32[]{:S(2)}) collective-permute-start(bf16[48,2432]{1,0:T(8,128)(2,1)S(1)} %collective-permute-done.7), channel_id=1, source_target_pairs={{0,32},{1,225},{2,34},{3,227},{4,36},{5,229},{6,38},{7,231},{8,40}... | collective-permute-start | bytes 700424 | tf_op jit(solution)/shard_map/ppermute | solution.py:29
  41.0 2.3 %collective-permute-start.13 = (bf16[48,2432]{1,0:T(8,128)(2,1)S(1)}, bf16[48,2432]{1,0:T(8,128)(2,1)S(1)}, u32[]{:S(2)}, u32[]{:S(2)}) collective-permute-start(bf16[48,2432]{1,0:T(8,128)(2,1)S(1)} %collective-permute-done.12), channel_id=1, source_target_pairs={{0,32},{1,225},{2,34},{3,227},{4,36},{5,229},{6,38},{7,231},{8,40}... | collective-permute-start | bytes 700424 | tf_op jit(solution)/shard_map/ppermute | solution.py:29
  43.3 2.5 %collective-permute-start.3 = (bf16[48,2432]{1,0:T(8,128)(2,1)S(1)}, bf16[48,2432]{1,0:T(8,128)(2,1)S(1)}, u32[]{:S(2)}, u32[]{:S(2)}) collective-permute-start(bf16[48,2432]{1,0:T(8,128)(2,1)S(1)} %collective-permute-done.2), channel_id=1, source_target_pairs={{0,32},{1,225},{2,34},{3,227},{4,36},{5,229},{6,38},{7,231},{8,40}... | collective-permute-start | bytes 700424 | tf_op jit(solution)/shard_map/ppermute | solution.py:29
  45.9 3.8 %collective-permute-done.3 = bf16[48,2432]{1,0:T(8,128)(2,1)S(1)} collective-permute-done((bf16[48,2432]{1,0:T(8,128)(2,1)S(1)}, bf16[48,2432]{1,0:T(8,128)(2,1)S(1)}, u32[]{:S(2)}, u32[]{:S(2)}) %collective-permute-start.3) | collective-permute-done | bytes 233504 | tf_op jit(solution)/shard_map/ppermute | solution.py:29
  49.7 2.5 %collective-permute-start.4 = (bf16[24,2432]{1,0:T(8,128)(2,1)S(1)}, bf16[24,2432]{1,0:T(8,128)(2,1)S(1)}, u32[]{:S(2)}, u32[]{:S(2)}) collective-permute-start(bf16[24,2432]{1,0:T(8,128)(2,1)S(1)} %get-tuple-element.51), channel_id=1, source_target_pairs={{0,32},{1,225},{2,34},{3,227},{4,36},{5,229},{6,38},{7,231},{8,40}... | collective-permute-start | bytes 350216 | tf_op jit(solution)/shard_map/ppermute | solution.py:29
  52.2 0.1 collective-permute-start.5
  52.4 3.8 %collective-permute-start.9 = (bf16[24,2432]{1,0:T(8,128)(2,1)S(1)}, bf16[24,2432]{1,0:T(8,128)(2,1)S(1)}, u32[]{:S(2)}, u32[]{:S(2)}) collective-permute-start(bf16[24,2432]{1,0:T(8,128)(2,1)S(1)} %get-tuple-element.58), channel_id=1, source_target_pairs={{0,32},{1,225},{2,34},{3,227},{4,36},{5,229},{6,38},{7,231},{8,40}... | collective-permute-start | bytes 350216 | tf_op jit(solution)/shard_map/ppermute | solution.py:29
  56.2 0.1 collective-permute-start.10
  56.3 0.7 collective-permute-start.14
  57.1 0.1 collective-permute-start.15
  57.2 1.3 %collective-permute-done.9 = bf16[24,2432]{1,0:T(8,128)(2,1)S(1)} collective-permute-done((bf16[24,2432]{1,0:T(8,128)(2,1)S(1)}, bf16[24,2432]{1,0:T(8,128)(2,1)S(1)}, u32[]{:S(2)}, u32[]{:S(2)}) %collective-permute-start.9) | collective-permute-done | bytes 116768 | tf_op jit(solution)/shard_map/ppermute | solution.py:29
  58.6 2.8 %collective-permute-done.14 = bf16[24,2432]{1,0:T(8,128)(2,1)S(1)} collective-permute-done((bf16[24,2432]{1,0:T(8,128)(2,1)S(1)}, bf16[24,2432]{1,0:T(8,128)(2,1)S(1)}, u32[]{:S(2)}, u32[]{:S(2)}) %collective-permute-start.14) | collective-permute-done | bytes 116768 | tf_op jit(solution)/shard_map/ppermute | solution.py:29
  61.5 0.4 fusion.8
  61.9 0.4 fusion.12
  62.3 0.4 fusion.6
  62.8 0.4 fusion.10
  63.2 0.4 fusion
  63.6 0.4 multiply_convert_fusion
  64.0 0.3 copy-done
  64.3 0.5 fusion.53
  64.8 0.5 fusion.52
  65.3 0.1 collective-permute-start.24
  65.4 2.0 %collective-permute-start.23 = (bf16[24,3584]{1,0:T(8,128)(2,1)S(1)}, bf16[24,3584]{1,0:T(8,128)(2,1)S(1)}, u32[]{:S(2)}, u32[]{:S(2)}) collective-permute-start(bf16[24,3584]{1,0:T(8,128)(2,1)S(1)} %get-tuple-element.47), channel_id=1, source_target_pairs={{0,32},{1,225},{2,34},{3,227},{4,36},{5,229},{6,38},{7,231},{8,40}... | collective-permute-start | bytes 516104 | tf_op jit(solution)/shard_map/ppermute | solution.py:29
  67.4 0.5 collective-permute-start.17
  67.9 2.4 %collective-permute-start.16 = (bf16[24,3584]{1,0:T(8,128)(2,1)S(1)}, bf16[24,3584]{1,0:T(8,128)(2,1)S(1)}, u32[]{:S(2)}, u32[]{:S(2)}) collective-permute-start(bf16[24,3584]{1,0:T(8,128)(2,1)S(1)} %get-tuple-element.49), channel_id=1, source_target_pairs={{0,32},{1,225},{2,34},{3,227},{4,36},{5,229},{6,38},{7,231},{8,40}... | collective-permute-start | bytes 516104 | tf_op jit(solution)/shard_map/ppermute | solution.py:29
  70.3 2.2 %collective-permute-done.24 = bf16[24,3584]{1,0:T(8,128)(2,1)S(1)} collective-permute-done((bf16[24,3584]{1,0:T(8,128)(2,1)S(1)}, bf16[24,3584]{1,0:T(8,128)(2,1)S(1)}, u32[]{:S(2)}, u32[]{:S(2)}) %collective-permute-start.24) | collective-permute-done | bytes 172064 | tf_op jit(solution)/shard_map/ppermute | solution.py:29
  72.5 0.6 collective-permute-done.23
  73.1 0.1 fusion.25
  73.2 2.1 %collective-permute-start.25 = (bf16[24,3584]{1,0:T(8,128)(2,1)S(1)}, bf16[24,3584]{1,0:T(8,128)(2,1)S(1)}, u32[]{:S(2)}, u32[]{:S(2)}) collective-permute-start(bf16[24,3584]{1,0:T(8,128)(2,1)S(1)} %get-tuple-element.30), channel_id=1, source_target_pairs={{0,32},{1,225},{2,34},{3,227},{4,36},{5,229},{6,38},{7,231},{8,40}... | collective-permute-start | bytes 516104 | tf_op jit(solution)/shard_map/ppermute | solution.py:29
  75.3 0.9 collective-permute-done.17
  76.2 0.1 fusion.32
  76.3 2.4 %collective-permute-start.18 = (bf16[24,3584]{1,0:T(8,128)(2,1)S(1)}, bf16[24,3584]{1,0:T(8,128)(2,1)S(1)}, u32[]{:S(2)}, u32[]{:S(2)}) collective-permute-start(bf16[24,3584]{1,0:T(8,128)(2,1)S(1)} %get-tuple-element.24), channel_id=1, source_target_pairs={{0,32},{1,225},{2,34},{3,227},{4,36},{5,229},{6,38},{7,231},{8,40}... | collective-permute-start | bytes 516104 | tf_op jit(solution)/shard_map/ppermute | solution.py:29
  78.7 0.8 collective-permute-done.25
  79.5 3.8 %collective-permute-done.26 = bf16[24,3584]{1,0:T(8,128)(2,1)S(1)} collective-permute-done((bf16[24,3584]{1,0:T(8,128)(2,1)S(1)}, bf16[24,3584]{1,0:T(8,128)(2,1)S(1)}, u32[]{:S(2)}, u32[]{:S(2)}) %collective-permute-start.26) | collective-permute-done | bytes 172064 | tf_op jit(solution)/shard_map/ppermute | solution.py:29
  83.4 3.2 %collective-permute-start.27 = (bf16[24,3584]{1,0:T(8,128)(2,1)S(1)}, bf16[24,3584]{1,0:T(8,128)(2,1)S(1)}, u32[]{:S(2)}, u32[]{:S(2)}) collective-permute-start(bf16[24,3584]{1,0:T(8,128)(2,1)S(1)} %get-tuple-element.32), channel_id=1, source_target_pairs={{0,32},{1,225},{2,34},{3,227},{4,36},{5,229},{6,38},{7,231},{8,40}... | collective-permute-start | bytes 516104 | tf_op jit(solution)/shard_map/ppermute | solution.py:29
  86.7 0.2 collective-permute-done.19
  86.9 3.0 %collective-permute-start.20 = (bf16[24,3584]{1,0:T(8,128)(2,1)S(1)}, bf16[24,3584]{1,0:T(8,128)(2,1)S(1)}, u32[]{:S(2)}, u32[]{:S(2)}) collective-permute-start(bf16[24,3584]{1,0:T(8,128)(2,1)S(1)} %get-tuple-element.26), channel_id=1, source_target_pairs={{0,32},{1,225},{2,34},{3,227},{4,36},{5,229},{6,38},{7,231},{8,40}... | collective-permute-start | bytes 516104 | tf_op jit(solution)/shard_map/ppermute | solution.py:29
  90.0 2.4 %collective-permute-start.28 = (bf16[24,3584]{1,0:T(8,128)(2,1)S(1)}, bf16[24,3584]{1,0:T(8,128)(2,1)S(1)}, u32[]{:S(2)}, u32[]{:S(2)}) collective-permute-start(bf16[24,3584]{1,0:T(8,128)(2,1)S(1)} %fusion.22), channel_id=1, source_target_pairs={{0,32},{1,225},{2,34},{3,227},{4,36},{5,229},{6,38},{7,231},{8,40}... | collective-permute-start | bytes 516104 | tf_op jit(solution)/shard_map/ppermute | solution.py:29
  92.4 2.1 %collective-permute-done.20 = bf16[24,3584]{1,0:T(8,128)(2,1)S(1)} collective-permute-done((bf16[24,3584]{1,0:T(8,128)(2,1)S(1)}, bf16[24,3584]{1,0:T(8,128)(2,1)S(1)}, u32[]{:S(2)}, u32[]{:S(2)}) %collective-permute-start.20) | collective-permute-done | bytes 172064 | tf_op jit(solution)/shard_map/ppermute | solution.py:29
  94.6 2.6 %collective-permute-start.21 = (bf16[24,3584]{1,0:T(8,128)(2,1)S(1)}, bf16[24,3584]{1,0:T(8,128)(2,1)S(1)}, u32[]{:S(2)}, u32[]{:S(2)}) collective-permute-start(bf16[24,3584]{1,0:T(8,128)(2,1)S(1)} %fusion.29), channel_id=1, source_target_pairs={{0,32},{1,225},{2,34},{3,227},{4,36},{5,229},{6,38},{7,231},{8,40}... | collective-permute-start | bytes 516104 | tf_op jit(solution)/shard_map/ppermute | solution.py:29
  97.1 0.3 collective-permute-done.28
  97.4 0.4 collective-permute-done.29
  97.9 2.2 %collective-permute-done.21 = bf16[24,3584]{1,0:T(8,128)(2,1)S(1)} collective-permute-done((bf16[24,3584]{1,0:T(8,128)(2,1)S(1)}, bf16[24,3584]{1,0:T(8,128)(2,1)S(1)}, u32[]{:S(2)}, u32[]{:S(2)}) %collective-permute-start.21) | collective-permute-done | bytes 172064 | tf_op jit(solution)/shard_map/ppermute | solution.py:29
  100.0 2.5 %collective-permute-done.22 = bf16[24,3584]{1,0:T(8,128)(2,1)S(1)} collective-permute-done((bf16[24,3584]{1,0:T(8,128)(2,1)S(1)}, bf16[24,3584]{1,0:T(8,128)(2,1)S(1)}, u32[]{:S(2)}, u32[]{:S(2)}) %collective-permute-start.22) | collective-permute-done | bytes 172064 | tf_op jit(solution)/shard_map/ppermute | solution.py:29
  102.6 0.7 shard_map.88
  103.3 0.1 collective-permute-start.30
  103.4 1.8 %collective-permute-done.30.other = bf16[32,7168]{1,0:T(8,128)(2,1)S(1)} collective-permute-done((bf16[32,7168]{1,0:T(8,128)(2,1)S(1)}, bf16[32,7168]{1,0:T(8,128)(2,1)S(1)}, u32[]{:S(2)}, u32[]{:S(2)}) %collective-permute-start.30) | collective-permute-done | bytes 458784 | tf_op jit(solution)/shard_map/ppermute | solution.py:20
  105.2 0.9 shard_map.89
  106.1 3.6 %all-to-all-start.1 = ((bf16[16,2,7168]{2,1,0:T(2,128)(2,1)}), bf16[16,2,7168]{2,1,0:T(2,128)(2,1)S(1)}, u32[]{:S(2)}, u32[]{:S(2)}) async-start(bf16[16,2,7168]{2,1,0:T(2,128)(2,1)} %shard_map.89), calls=%async_computation.1 | async-start | bytes 917504 | tf_op jit(solution)/shard_map/all_to_all | solution.py:275
  109.7 0.5 fusion.42
  110.2 10.8 %all-to-all-done.1 = bf16[16,2,7168]{2,1,0:T(2,128)(2,1)S(1)} async-done(((bf16[16,2,7168]{2,1,0:T(2,128)(2,1)}), bf16[16,2,7168]{2,1,0:T(2,128)(2,1)S(1)}, u32[]{:S(2)}, u32[]{:S(2)}) %all-to-all-start.1) | async-done | bytes 458784 | tf_op jit(solution)/shard_map/all_to_all | solution.py:275
  121.0 1.0 reduce_sum.23
  (54 shorter events, 1.0 us)
Async XLA Ops:
  20.5 1.9 %collective-permute-start = (bf16[32,7296]{1,0:T(8,128)(2,1)S(1)}, bf16[32,7296]{1,0:T(8,128)(2,1)S(1)}, u32[]{:S(2)}, u32[]{:S(2)}) collective-permute-start(bf16[32,7296]{1,0:T(8,128)(2,1)S(1)} %reshape.12.near), channel_id=1, source_target_pairs={{0,1},{1,0},{2,3},{3,2},{4,5},{5,4},{6,7},{7,6},{8,9},{9,8},{10,11... | collective-permute-start | bytes 1400840 | tf_op jit(solution)/shard_map/ppermute | solution.py:20
  23.4 6.2 %collective-permute-start.6 = (bf16[48,2432]{1,0:T(8,128)(2,1)S(1)}, bf16[48,2432]{1,0:T(8,128)(2,1)S(1)}, u32[]{:S(2)}, u32[]{:S(2)}) collective-permute-start(bf16[48,2432]{1,0:T(8,128)(2,1)S(1)} %get-tuple-element.22), channel_id=1, source_target_pairs={{0,32},{1,225},{2,34},{3,227},{4,36},{5,229},{6,38},{7,231},{8,40}... | collective-permute-start | bytes 700424 | tf_op jit(solution)/shard_map/ppermute | solution.py:29
  25.4 6.7 %collective-permute-start.11 = (bf16[48,2432]{1,0:T(8,128)(2,1)S(1)}, bf16[48,2432]{1,0:T(8,128)(2,1)S(1)}, u32[]{:S(2)}, u32[]{:S(2)}) collective-permute-start(bf16[48,2432]{1,0:T(8,128)(2,1)S(1)} %get-tuple-element.23), channel_id=1, source_target_pairs={{0,32},{1,225},{2,34},{3,227},{4,36},{5,229},{6,38},{7,231},{8,40}... | collective-permute-start | bytes 700424 | tf_op jit(solution)/shard_map/ppermute | solution.py:29
  28.5 7.3 %collective-permute-start.1 = (bf16[48,2432]{1,0:T(8,128)(2,1)S(1)}, bf16[48,2432]{1,0:T(8,128)(2,1)S(1)}, u32[]{:S(2)}, u32[]{:S(2)}) collective-permute-start(bf16[48,2432]{1,0:T(8,128)(2,1)S(1)} %get-tuple-element.21), channel_id=1, source_target_pairs={{0,32},{1,225},{2,34},{3,227},{4,36},{5,229},{6,38},{7,231},{8,40}... | collective-permute-start | bytes 700424 | tf_op jit(solution)/shard_map/ppermute | solution.py:29
  29.7 8.7 %collective-permute-start.7 = (bf16[48,2432]{1,0:T(8,128)(2,1)S(1)}, bf16[48,2432]{1,0:T(8,128)(2,1)S(1)}, u32[]{:S(2)}, u32[]{:S(2)}) collective-permute-start(bf16[48,2432]{1,0:T(8,128)(2,1)S(1)} %collective-permute-done.6), channel_id=1, source_target_pairs={{0,32},{1,225},{2,34},{3,227},{4,36},{5,229},{6,38},{7,231},{8,40}... | collective-permute-start | bytes 700424 | tf_op jit(solution)/shard_map/ppermute | solution.py:29
  32.1 8.9 %collective-permute-start.12 = (bf16[48,2432]{1,0:T(8,128)(2,1)S(1)}, bf16[48,2432]{1,0:T(8,128)(2,1)S(1)}, u32[]{:S(2)}, u32[]{:S(2)}) collective-permute-start(bf16[48,2432]{1,0:T(8,128)(2,1)S(1)} %collective-permute-done.11), channel_id=1, source_target_pairs={{0,32},{1,225},{2,34},{3,227},{4,36},{5,229},{6,38},{7,231},{8,40}... | collective-permute-start | bytes 700424 | tf_op jit(solution)/shard_map/ppermute | solution.py:29
  35.8 7.5 %collective-permute-start.2 = (bf16[48,2432]{1,0:T(8,128)(2,1)S(1)}, bf16[48,2432]{1,0:T(8,128)(2,1)S(1)}, u32[]{:S(2)}, u32[]{:S(2)}) collective-permute-start(bf16[48,2432]{1,0:T(8,128)(2,1)S(1)} %collective-permute-done.1), channel_id=1, source_target_pairs={{0,32},{1,225},{2,34},{3,227},{4,36},{5,229},{6,38},{7,231},{8,40}... | collective-permute-start | bytes 700424 | tf_op jit(solution)/shard_map/ppermute | solution.py:29
  38.4 13.9 %collective-permute-start.8 = (bf16[48,2432]{1,0:T(8,128)(2,1)S(1)}, bf16[48,2432]{1,0:T(8,128)(2,1)S(1)}, u32[]{:S(2)}, u32[]{:S(2)}) collective-permute-start(bf16[48,2432]{1,0:T(8,128)(2,1)S(1)} %collective-permute-done.7), channel_id=1, source_target_pairs={{0,32},{1,225},{2,34},{3,227},{4,36},{5,229},{6,38},{7,231},{8,40}... | collective-permute-start | bytes 700424 | tf_op jit(solution)/shard_map/ppermute | solution.py:29
  41.0 15.3 %collective-permute-start.13 = (bf16[48,2432]{1,0:T(8,128)(2,1)S(1)}, bf16[48,2432]{1,0:T(8,128)(2,1)S(1)}, u32[]{:S(2)}, u32[]{:S(2)}) collective-permute-start(bf16[48,2432]{1,0:T(8,128)(2,1)S(1)} %collective-permute-done.12), channel_id=1, source_target_pairs={{0,32},{1,225},{2,34},{3,227},{4,36},{5,229},{6,38},{7,231},{8,40}... | collective-permute-start | bytes 700424 | tf_op jit(solution)/shard_map/ppermute | solution.py:29
  43.3 6.4 %collective-permute-start.3 = (bf16[48,2432]{1,0:T(8,128)(2,1)S(1)}, bf16[48,2432]{1,0:T(8,128)(2,1)S(1)}, u32[]{:S(2)}, u32[]{:S(2)}) collective-permute-start(bf16[48,2432]{1,0:T(8,128)(2,1)S(1)} %collective-permute-done.2), channel_id=1, source_target_pairs={{0,32},{1,225},{2,34},{3,227},{4,36},{5,229},{6,38},{7,231},{8,40}... | collective-permute-start | bytes 700424 | tf_op jit(solution)/shard_map/ppermute | solution.py:29
  45.9 15.6 %copy-start.1 = (bf16[1,2,7168,128]{3,2,1,0:T(8,128)(2,1)S(1)}, bf16[1,2,7168,128]{3,2,1,0:T(8,128)(2,1)}, u32[]{:S(2)}) copy-start(bf16[1,2,7168,128]{3,2,1,0:T(8,128)(2,1)} %param.12) | copy-start | bytes 11010052
  49.7 7.4 %collective-permute-start.4 = (bf16[24,2432]{1,0:T(8,128)(2,1)S(1)}, bf16[24,2432]{1,0:T(8,128)(2,1)S(1)}, u32[]{:S(2)}, u32[]{:S(2)}) collective-permute-start(bf16[24,2432]{1,0:T(8,128)(2,1)S(1)} %get-tuple-element.51), channel_id=1, source_target_pairs={{0,32},{1,225},{2,34},{3,227},{4,36},{5,229},{6,38},{7,231},{8,40}... | collective-permute-start | bytes 350216 | tf_op jit(solution)/shard_map/ppermute | solution.py:29
  52.2 10.9 %collective-permute-start.5 = (bf16[72,2432]{1,0:T(8,128)(2,1)S(1)}, bf16[72,2432]{1,0:T(8,128)(2,1)S(1)}, u32[]{:S(2)}, u32[]{:S(2)}) collective-permute-start(bf16[72,2432]{1,0:T(8,128)(2,1)S(1)} %pad_maximum_fusion), channel_id=1, source_target_pairs={{0,1},{1,0},{2,3},{3,2},{4,5},{5,4},{6,7},{7,6},{8,9},{9,8},{10,11... | collective-permute-start | bytes 1050632 | tf_op jit(solution)/shard_map/ppermute | solution.py:20
  52.4 6.2 %collective-permute-start.9 = (bf16[24,2432]{1,0:T(8,128)(2,1)S(1)}, bf16[24,2432]{1,0:T(8,128)(2,1)S(1)}, u32[]{:S(2)}, u32[]{:S(2)}) collective-permute-start(bf16[24,2432]{1,0:T(8,128)(2,1)S(1)} %get-tuple-element.58), channel_id=1, source_target_pairs={{0,32},{1,225},{2,34},{3,227},{4,36},{5,229},{6,38},{7,231},{8,40}... | collective-permute-start | bytes 350216 | tf_op jit(solution)/shard_map/ppermute | solution.py:29
  56.2 5.2 %collective-permute-start.10 = (bf16[72,2432]{1,0:T(8,128)(2,1)S(1)}, bf16[72,2432]{1,0:T(8,128)(2,1)S(1)}, u32[]{:S(2)}, u32[]{:S(2)}) collective-permute-start(bf16[72,2432]{1,0:T(8,128)(2,1)S(1)} %pad_maximum_fusion.1), channel_id=1, source_target_pairs={{0,1},{1,0},{2,3},{3,2},{4,5},{5,4},{6,7},{7,6},{8,9},{9,8},{10,11... | collective-permute-start | bytes 1050632 | tf_op jit(solution)/shard_map/ppermute | solution.py:20
  56.3 5.1 %collective-permute-start.14 = (bf16[24,2432]{1,0:T(8,128)(2,1)S(1)}, bf16[24,2432]{1,0:T(8,128)(2,1)S(1)}, u32[]{:S(2)}, u32[]{:S(2)}) collective-permute-start(bf16[24,2432]{1,0:T(8,128)(2,1)S(1)} %get-tuple-element.65), channel_id=1, source_target_pairs={{0,32},{1,225},{2,34},{3,227},{4,36},{5,229},{6,38},{7,231},{8,40}... | collective-permute-start | bytes 350216 | tf_op jit(solution)/shard_map/ppermute | solution.py:29
  57.1 5.2 %collective-permute-start.15 = (bf16[72,2432]{1,0:T(8,128)(2,1)S(1)}, bf16[72,2432]{1,0:T(8,128)(2,1)S(1)}, u32[]{:S(2)}, u32[]{:S(2)}) collective-permute-start(bf16[72,2432]{1,0:T(8,128)(2,1)S(1)} %pad_maximum_fusion.2), channel_id=1, source_target_pairs={{0,1},{1,0},{2,3},{3,2},{4,5},{5,4},{6,7},{7,6},{8,9},{9,8},{10,11... | collective-permute-start | bytes 1050632 | tf_op jit(solution)/shard_map/ppermute | solution.py:20
  62.7 1.5 %copy-start = (bf16[1,128,7168]{2,1,0:T(8,128)(2,1)S(1)}, bf16[1,128,7168]{2,1,0:T(8,128)(2,1)}, u32[]{:S(2)}) copy-start(bf16[1,128,7168]{2,1,0:T(8,128)(2,1)} %param.13) | copy-start | bytes 5505028
  65.3 7.2 %collective-permute-start.24 = (bf16[24,3584]{1,0:T(8,128)(2,1)S(1)}, bf16[24,3584]{1,0:T(8,128)(2,1)S(1)}, u32[]{:S(2)}, u32[]{:S(2)}) collective-permute-start(bf16[24,3584]{1,0:T(8,128)(2,1)S(1)} %get-tuple-element.46), channel_id=1, source_target_pairs={{0,224},{1,33},{2,226},{3,35},{4,228},{5,37},{6,230},{7,39},{8,232... | collective-permute-start | bytes 516104 | tf_op jit(solution)/shard_map/ppermute | solution.py:29
  65.4 7.7 %collective-permute-start.23 = (bf16[24,3584]{1,0:T(8,128)(2,1)S(1)}, bf16[24,3584]{1,0:T(8,128)(2,1)S(1)}, u32[]{:S(2)}, u32[]{:S(2)}) collective-permute-start(bf16[24,3584]{1,0:T(8,128)(2,1)S(1)} %get-tuple-element.47), channel_id=1, source_target_pairs={{0,32},{1,225},{2,34},{3,227},{4,36},{5,229},{6,38},{7,231},{8,40}... | collective-permute-start | bytes 516104 | tf_op jit(solution)/shard_map/ppermute | solution.py:29
  67.4 8.8 %collective-permute-start.17 = (bf16[24,3584]{1,0:T(8,128)(2,1)S(1)}, bf16[24,3584]{1,0:T(8,128)(2,1)S(1)}, u32[]{:S(2)}, u32[]{:S(2)}) collective-permute-start(bf16[24,3584]{1,0:T(8,128)(2,1)S(1)} %get-tuple-element.48), channel_id=1, source_target_pairs={{0,224},{1,33},{2,226},{3,35},{4,228},{5,37},{6,230},{7,39},{8,232... | collective-permute-start | bytes 516104 | tf_op jit(solution)/shard_map/ppermute | solution.py:29
  67.9 8.3 %collective-permute-start.16 = (bf16[24,3584]{1,0:T(8,128)(2,1)S(1)}, bf16[24,3584]{1,0:T(8,128)(2,1)S(1)}, u32[]{:S(2)}, u32[]{:S(2)}) collective-permute-start(bf16[24,3584]{1,0:T(8,128)(2,1)S(1)} %get-tuple-element.49), channel_id=1, source_target_pairs={{0,32},{1,225},{2,34},{3,227},{4,36},{5,229},{6,38},{7,231},{8,40}... | collective-permute-start | bytes 516104 | tf_op jit(solution)/shard_map/ppermute | solution.py:29
  73.2 6.4 %collective-permute-start.25 = (bf16[24,3584]{1,0:T(8,128)(2,1)S(1)}, bf16[24,3584]{1,0:T(8,128)(2,1)S(1)}, u32[]{:S(2)}, u32[]{:S(2)}) collective-permute-start(bf16[24,3584]{1,0:T(8,128)(2,1)S(1)} %get-tuple-element.30), channel_id=1, source_target_pairs={{0,32},{1,225},{2,34},{3,227},{4,36},{5,229},{6,38},{7,231},{8,40}... | collective-permute-start | bytes 516104 | tf_op jit(solution)/shard_map/ppermute | solution.py:29
  75.3 8.0 %collective-permute-start.26 = (bf16[24,3584]{1,0:T(8,128)(2,1)S(1)}, bf16[24,3584]{1,0:T(8,128)(2,1)S(1)}, u32[]{:S(2)}, u32[]{:S(2)}) collective-permute-start(bf16[24,3584]{1,0:T(8,128)(2,1)S(1)} %get-tuple-element.31), channel_id=1, source_target_pairs={{0,224},{1,33},{2,226},{3,35},{4,228},{5,37},{6,230},{7,39},{8,232... | collective-permute-start | bytes 516104 | tf_op jit(solution)/shard_map/ppermute | solution.py:29
  76.3 10.4 %collective-permute-start.18 = (bf16[24,3584]{1,0:T(8,128)(2,1)S(1)}, bf16[24,3584]{1,0:T(8,128)(2,1)S(1)}, u32[]{:S(2)}, u32[]{:S(2)}) collective-permute-start(bf16[24,3584]{1,0:T(8,128)(2,1)S(1)} %get-tuple-element.24), channel_id=1, source_target_pairs={{0,32},{1,225},{2,34},{3,227},{4,36},{5,229},{6,38},{7,231},{8,40}... | collective-permute-start | bytes 516104 | tf_op jit(solution)/shard_map/ppermute | solution.py:29
  78.7 8.1 %collective-permute-start.19 = (bf16[24,3584]{1,0:T(8,128)(2,1)S(1)}, bf16[24,3584]{1,0:T(8,128)(2,1)S(1)}, u32[]{:S(2)}, u32[]{:S(2)}) collective-permute-start(bf16[24,3584]{1,0:T(8,128)(2,1)S(1)} %get-tuple-element.25), channel_id=1, source_target_pairs={{0,224},{1,33},{2,226},{3,35},{4,228},{5,37},{6,230},{7,39},{8,232... | collective-permute-start | bytes 516104 | tf_op jit(solution)/shard_map/ppermute | solution.py:29
  83.4 6.5 %collective-permute-start.27 = (bf16[24,3584]{1,0:T(8,128)(2,1)S(1)}, bf16[24,3584]{1,0:T(8,128)(2,1)S(1)}, u32[]{:S(2)}, u32[]{:S(2)}) collective-permute-start(bf16[24,3584]{1,0:T(8,128)(2,1)S(1)} %get-tuple-element.32), channel_id=1, source_target_pairs={{0,32},{1,225},{2,34},{3,227},{4,36},{5,229},{6,38},{7,231},{8,40}... | collective-permute-start | bytes 516104 | tf_op jit(solution)/shard_map/ppermute | solution.py:29
  86.9 7.6 %collective-permute-start.20 = (bf16[24,3584]{1,0:T(8,128)(2,1)S(1)}, bf16[24,3584]{1,0:T(8,128)(2,1)S(1)}, u32[]{:S(2)}, u32[]{:S(2)}) collective-permute-start(bf16[24,3584]{1,0:T(8,128)(2,1)S(1)} %get-tuple-element.26), channel_id=1, source_target_pairs={{0,32},{1,225},{2,34},{3,227},{4,36},{5,229},{6,38},{7,231},{8,40}... | collective-permute-start | bytes 516104 | tf_op jit(solution)/shard_map/ppermute | solution.py:29
  90.0 7.4 %collective-permute-start.28 = (bf16[24,3584]{1,0:T(8,128)(2,1)S(1)}, bf16[24,3584]{1,0:T(8,128)(2,1)S(1)}, u32[]{:S(2)}, u32[]{:S(2)}) collective-permute-start(bf16[24,3584]{1,0:T(8,128)(2,1)S(1)} %fusion.22), channel_id=1, source_target_pairs={{0,32},{1,225},{2,34},{3,227},{4,36},{5,229},{6,38},{7,231},{8,40}... | collective-permute-start | bytes 516104 | tf_op jit(solution)/shard_map/ppermute | solution.py:29
  92.4 5.4 %collective-permute-start.29 = (bf16[24,3584]{1,0:T(8,128)(2,1)S(1)}, bf16[24,3584]{1,0:T(8,128)(2,1)S(1)}, u32[]{:S(2)}, u32[]{:S(2)}) collective-permute-start(bf16[24,3584]{1,0:T(8,128)(2,1)S(1)} %get-tuple-element.35), channel_id=1, source_target_pairs={{0,224},{1,33},{2,226},{3,35},{4,228},{5,37},{6,230},{7,39},{8,232... | collective-permute-start | bytes 516104 | tf_op jit(solution)/shard_map/ppermute | solution.py:29
  94.6 5.5 %collective-permute-start.21 = (bf16[24,3584]{1,0:T(8,128)(2,1)S(1)}, bf16[24,3584]{1,0:T(8,128)(2,1)S(1)}, u32[]{:S(2)}, u32[]{:S(2)}) collective-permute-start(bf16[24,3584]{1,0:T(8,128)(2,1)S(1)} %fusion.29), channel_id=1, source_target_pairs={{0,32},{1,225},{2,34},{3,227},{4,36},{5,229},{6,38},{7,231},{8,40}... | collective-permute-start | bytes 516104 | tf_op jit(solution)/shard_map/ppermute | solution.py:29
  97.1 5.4 %collective-permute-start.22 = (bf16[24,3584]{1,0:T(8,128)(2,1)S(1)}, bf16[24,3584]{1,0:T(8,128)(2,1)S(1)}, u32[]{:S(2)}, u32[]{:S(2)}) collective-permute-start(bf16[24,3584]{1,0:T(8,128)(2,1)S(1)} %get-tuple-element.29), channel_id=1, source_target_pairs={{0,224},{1,33},{2,226},{3,35},{4,228},{5,37},{6,230},{7,39},{8,232... | collective-permute-start | bytes 516104 | tf_op jit(solution)/shard_map/ppermute | solution.py:29
  103.3 1.9 %collective-permute-start.30 = (bf16[32,7168]{1,0:T(8,128)(2,1)S(1)}, bf16[32,7168]{1,0:T(8,128)(2,1)S(1)}, u32[]{:S(2)}, u32[]{:S(2)}) collective-permute-start(bf16[32,7168]{1,0:T(8,128)(2,1)S(1)} %get-tuple-element.37), channel_id=1, source_target_pairs={{0,1},{1,0},{2,3},{3,2},{4,5},{5,4},{6,7},{7,6},{8,9},{9,8},{10,11... | collective-permute-start | bytes 1376264 | tf_op jit(solution)/shard_map/ppermute | solution.py:20
  106.1 14.9 %all-to-all-start.1 = ((bf16[16,2,7168]{2,1,0:T(2,128)(2,1)}), bf16[16,2,7168]{2,1,0:T(2,128)(2,1)S(1)}, u32[]{:S(2)}, u32[]{:S(2)}) async-start(bf16[16,2,7168]{2,1,0:T(2,128)(2,1)} %shard_map.89), calls=%async_computation.1 | async-start | bytes 917504 | tf_op jit(solution)/shard_map/all_to_all | solution.py:275

commit v5 on v3

--- a/solution.py
+++ b/solution.py
@@ -149,6 +149,15 @@
     packed[-1][:, cols[-1].stop - cols[-1].start :] = tail
 
 
+def up_kernel(cols, w, *refs):
+    acc = 0.0
+    for x, at in zip(refs[:-1], cols):
+        both = jnp.concatenate([w[0, 0, at, :], w[0, 1, at, :]], 1)
+        acc += jnp.dot(x[...], both, preferred_element_type=F32)
+    ff = w.shape[3]
+    refs[-1][...] = (jax.nn.silu(acc[:, :ff]) * acc[:, ff:]).astype(BF16)
+
+
 def body(tokens, expert_ids, replica, route_weight, spare_plan, w_in, w_down):
     rows, width = tokens.shape
     top = expert_ids.shape[1]
@@ -203,13 +212,13 @@
         for got, handed, at in zip(moving, other, cols)
     ]
 
-    def up(which):
-        return sum(
-            jnp.dot(x, w_in[0, which, cols[c]], preferred_element_type=F32)
-            for c, x in reversed(list(enumerate(gathered)))
-        )
-
-    hidden = (jax.nn.silu(up(0)) * up(1)).astype(BF16)
+    hidden = pl.pallas_call(
+        functools.partial(up_kernel, cols),
+        out_shape=jax.ShapeDtypeStruct((count * MOST, w_in.shape[3]), BF16),
+        in_specs=[vmem] * (1 + CHUNKS),
+        out_specs=vmem,
+        compiler_params=grant,
+    )(w_in, *gathered)
     place_of = {0: 0}
     for s in range(1, half + 1):
         place_of[count - s] = s

time: 123 us -> 121 us (0.984)
  matrix products: 4.24 us -> 1.86 us
    dot_general x6 -> x0, matrix products: 2.39 us -> none  [up(): jnp.dot(x, w_in[0, which, cols[c]], preferred_element_type=F32)]
  transfers between devices with their start and end apart: 32 -> 32, of which waited for: 17 -> 17; matrix products, arithmetic and copies ran while one was open for 3% -> 1% of each run, Pallas kernels for 0% -> 0%
where the time goes in v5:
time: 121 us
  starting transfers between devices  54.1 us (45%)
  waiting for transfers between devices  38.1 us (31%)
  blocking collectives  17.9 us (15%)
  Pallas kernels  3.61 us (3%)
  other arithmetic  2.24 us (2%)
  local copies, waits for them, and re-layouts  2.18 us (2%)
  matrix products  1.86 us (2%)
    ppermute x26, starting transfers between devices, core_ring(): return lax.ppermute(value, ('attn', 'expert'), pairs)  50 us
    ppermute x26, waiting for transfers between devices, core_ring(): return lax.ppermute(value, ('attn', 'expert'), pairs)  23.6 us
    all_to_all x1, blocking collectives, body(): lax.all_to_all(spread, 'expert', 0, 0, axis_index_groups=same_core, tiled...  17.9 us
    all_to_all x1, waiting for transfers between devices, body(): lax.all_to_all(both.reshape(peers, rows, width), 'expert', 0, 0, axis_ind...  10.8 us
    ppermute x5, waiting for transfers between devices, core_swap(): return lax.ppermute(value, 'expert', [(i, i ^ 1) for i in range(groups)])  3.63 us
    all_to_all x1, starting transfers between devices, body(): lax.all_to_all(both.reshape(peers, rows, width), 'expert', 0, 0, axis_ind...  3.56 us
  transfers between devices with their start and end apart: 32, of which 17 were waited for; matrix products, arithmetic and copies ran while one was open for 1% of the time, Pallas kernels for 0%

profile of v5, /device:TPU:64, one launch (start us, length us, event | category | flops | bytes accessed | tf_op | source)
XLA Modules:
  0.0 121.0 jit_solution(15557757631654144899)
XLA Ops:
  0.6 1.7 %shard_map.86 = bf16[16,2,7296]{2,1,0:T(2,128)(2,1)} custom-call(bf16[2,7168]{1,0:T(2,128)(2,1)} %refs_0_.1, s32[2,8]{1,0:T(2,128)} %refs_1_.1, s32[2,8]{1,0:T(2,128)} %refs_2_.1, f32[2,8]{1,0:T(2,128)} %refs_3_.1, s32[32]{0:T(128)} %refs_4_.1), custom_call_target="tpu_custom_call" | custom-call | tf_op jit(solution)/shard_map/pallas_call | solution.py:173
  2.4 17.9 %all_to_all.10 = bf16[16,2,7296]{2,1,0:T(2,128)(2,1)S(1)} all-to-all(bf16[16,2,7296]{2,1,0:T(2,128)(2,1)} %shard_map.86), channel_id=1, replica_groups={{0,2,4,6,8,10,12,14,16,18,20,22,24,26,28,30},{1,3,5,7,9,11,13,15,17,19,..., dimensions={0} | all-to-all | bytes 933888 | tf_op jit(solution)/shard_map/all_to_all | solution.py:183
  20.3 0.2 reshape.15.near
  20.5 0.1 collective-permute-start
  20.6 1.8 %collective-permute-done.far = bf16[32,7296]{1,0:T(8,128)(2,1)S(1)} collective-permute-done((bf16[32,7296]{1,0:T(8,128)(2,1)S(1)}, bf16[32,7296]{1,0:T(8,128)(2,1)S(1)}, u32[]{:S(2)}, u32[]{:S(2)}) %collective-permute-start) | collective-permute-done | bytes 466976 | tf_op jit(solution)/shard_map/ppermute | solution.py:19
  22.4 1.0 shard_map.87
  23.4 2.0 %collective-permute-start.1 = (bf16[48,2432]{1,0:T(8,128)(2,1)S(1)}, bf16[48,2432]{1,0:T(8,128)(2,1)S(1)}, u32[]{:S(2)}, u32[]{:S(2)}) collective-permute-start(bf16[48,2432]{1,0:T(8,128)(2,1)S(1)} %get-tuple-element.19), channel_id=1, source_target_pairs={{0,32},{1,225},{2,34},{3,227},{4,36},{5,229},{6,38},{7,231},{8,40}... | collective-permute-start | bytes 700424 | tf_op jit(solution)/shard_map/ppermute | solution.py:28
  25.4 3.1 %collective-permute-start.6 = (bf16[48,2432]{1,0:T(8,128)(2,1)S(1)}, bf16[48,2432]{1,0:T(8,128)(2,1)S(1)}, u32[]{:S(2)}, u32[]{:S(2)}) collective-permute-start(bf16[48,2432]{1,0:T(8,128)(2,1)S(1)} %get-tuple-element.20), channel_id=1, source_target_pairs={{0,32},{1,225},{2,34},{3,227},{4,36},{5,229},{6,38},{7,231},{8,40}... | collective-permute-start | bytes 700424 | tf_op jit(solution)/shard_map/ppermute | solution.py:28
  28.5 1.1 collective-permute-start.11
  29.6 2.5 %collective-permute-start.2 = (bf16[48,2432]{1,0:T(8,128)(2,1)S(1)}, bf16[48,2432]{1,0:T(8,128)(2,1)S(1)}, u32[]{:S(2)}, u32[]{:S(2)}) collective-permute-start(bf16[48,2432]{1,0:T(8,128)(2,1)S(1)} %collective-permute-done.1), channel_id=1, source_target_pairs={{0,32},{1,225},{2,34},{3,227},{4,36},{5,229},{6,38},{7,231},{8,40}... | collective-permute-start | bytes 700424 | tf_op jit(solution)/shard_map/ppermute | solution.py:28
  32.1 3.7 %collective-permute-start.7 = (bf16[48,2432]{1,0:T(8,128)(2,1)S(1)}, bf16[48,2432]{1,0:T(8,128)(2,1)S(1)}, u32[]{:S(2)}, u32[]{:S(2)}) collective-permute-start(bf16[48,2432]{1,0:T(8,128)(2,1)S(1)} %collective-permute-done.6), channel_id=1, source_target_pairs={{0,32},{1,225},{2,34},{3,227},{4,36},{5,229},{6,38},{7,231},{8,40}... | collective-permute-start | bytes 700424 | tf_op jit(solution)/shard_map/ppermute | solution.py:28
  35.8 2.5 %collective-permute-start.12 = (bf16[48,2432]{1,0:T(8,128)(2,1)S(1)}, bf16[48,2432]{1,0:T(8,128)(2,1)S(1)}, u32[]{:S(2)}, u32[]{:S(2)}) collective-permute-start(bf16[48,2432]{1,0:T(8,128)(2,1)S(1)} %collective-permute-done.11), channel_id=1, source_target_pairs={{0,32},{1,225},{2,34},{3,227},{4,36},{5,229},{6,38},{7,231},{8,40}... | collective-permute-start | bytes 700424 | tf_op jit(solution)/shard_map/ppermute | solution.py:28
  38.4 2.6 %collective-permute-start.3 = (bf16[48,2432]{1,0:T(8,128)(2,1)S(1)}, bf16[48,2432]{1,0:T(8,128)(2,1)S(1)}, u32[]{:S(2)}, u32[]{:S(2)}) collective-permute-start(bf16[48,2432]{1,0:T(8,128)(2,1)S(1)} %collective-permute-done.2), channel_id=1, source_target_pairs={{0,32},{1,225},{2,34},{3,227},{4,36},{5,229},{6,38},{7,231},{8,40}... | collective-permute-start | bytes 700424 | tf_op jit(solution)/shard_map/ppermute | solution.py:28
  41.0 2.3 %collective-permute-start.8 = (bf16[48,2432]{1,0:T(8,128)(2,1)S(1)}, bf16[48,2432]{1,0:T(8,128)(2,1)S(1)}, u32[]{:S(2)}, u32[]{:S(2)}) collective-permute-start(bf16[48,2432]{1,0:T(8,128)(2,1)S(1)} %collective-permute-done.7), channel_id=1, source_target_pairs={{0,32},{1,225},{2,34},{3,227},{4,36},{5,229},{6,38},{7,231},{8,40}... | collective-permute-start | bytes 700424 | tf_op jit(solution)/shard_map/ppermute | solution.py:28
  43.3 2.5 %collective-permute-start.13 = (bf16[48,2432]{1,0:T(8,128)(2,1)S(1)}, bf16[48,2432]{1,0:T(8,128)(2,1)S(1)}, u32[]{:S(2)}, u32[]{:S(2)}) collective-permute-start(bf16[48,2432]{1,0:T(8,128)(2,1)S(1)} %collective-permute-done.12), channel_id=1, source_target_pairs={{0,32},{1,225},{2,34},{3,227},{4,36},{5,229},{6,38},{7,231},{8,40}... | collective-permute-start | bytes 700424 | tf_op jit(solution)/shard_map/ppermute | solution.py:28
  45.9 3.8 %collective-permute-done.13 = bf16[48,2432]{1,0:T(8,128)(2,1)S(1)} collective-permute-done((bf16[48,2432]{1,0:T(8,128)(2,1)S(1)}, bf16[48,2432]{1,0:T(8,128)(2,1)S(1)}, u32[]{:S(2)}, u32[]{:S(2)}) %collective-permute-start.13) | collective-permute-done | bytes 233504 | tf_op jit(solution)/shard_map/ppermute | solution.py:28
  49.7 2.5 %collective-permute-start.14 = (bf16[24,2432]{1,0:T(8,128)(2,1)S(1)}, bf16[24,2432]{1,0:T(8,128)(2,1)S(1)}, u32[]{:S(2)}, u32[]{:S(2)}) collective-permute-start(bf16[24,2432]{1,0:T(8,128)(2,1)S(1)} %get-tuple-element.47), channel_id=1, source_target_pairs={{0,32},{1,225},{2,34},{3,227},{4,36},{5,229},{6,38},{7,231},{8,40}... | collective-permute-start | bytes 350216 | tf_op jit(solution)/shard_map/ppermute | solution.py:28
  52.2 0.1 collective-permute-start.15
  52.4 3.8 %collective-permute-start.4 = (bf16[24,2432]{1,0:T(8,128)(2,1)S(1)}, bf16[24,2432]{1,0:T(8,128)(2,1)S(1)}, u32[]{:S(2)}, u32[]{:S(2)}) collective-permute-start(bf16[24,2432]{1,0:T(8,128)(2,1)S(1)} %get-tuple-element.61), channel_id=1, source_target_pairs={{0,32},{1,225},{2,34},{3,227},{4,36},{5,229},{6,38},{7,231},{8,40}... | collective-permute-start | bytes 350216 | tf_op jit(solution)/shard_map/ppermute | solution.py:28
  56.2 0.1 collective-permute-start.5
  56.3 0.7 collective-permute-start.9
  57.1 0.1 collective-permute-start.10
  57.3 1.3 %collective-permute-done.4 = bf16[24,2432]{1,0:T(8,128)(2,1)S(1)} collective-permute-done((bf16[24,2432]{1,0:T(8,128)(2,1)S(1)}, bf16[24,2432]{1,0:T(8,128)(2,1)S(1)}, u32[]{:S(2)}, u32[]{:S(2)}) %collective-permute-start.4) | collective-permute-done | bytes 116768 | tf_op jit(solution)/shard_map/ppermute | solution.py:28
  58.5 2.9 %collective-permute-done.9 = bf16[24,2432]{1,0:T(8,128)(2,1)S(1)} collective-permute-done((bf16[24,2432]{1,0:T(8,128)(2,1)S(1)}, bf16[24,2432]{1,0:T(8,128)(2,1)S(1)}, u32[]{:S(2)}, u32[]{:S(2)}) %collective-permute-start.9) | collective-permute-done | bytes 116768 | tf_op jit(solution)/shard_map/ppermute | solution.py:28
  61.6 0.9 shard_map.88
  62.5 0.6 copy-done.1
  63.1 0.5 fusion.42
  63.6 0.5 fusion.43
  64.1 0.1 collective-permute-start.24
  64.2 2.0 %collective-permute-start.23 = (bf16[24,3584]{1,0:T(8,128)(2,1)S(1)}, bf16[24,3584]{1,0:T(8,128)(2,1)S(1)}, u32[]{:S(2)}, u32[]{:S(2)}) collective-permute-start(bf16[24,3584]{1,0:T(8,128)(2,1)S(1)} %get-tuple-element.45), channel_id=1, source_target_pairs={{0,32},{1,225},{2,34},{3,227},{4,36},{5,229},{6,38},{7,231},{8,40}... | collective-permute-start | bytes 516104 | tf_op jit(solution)/shard_map/ppermute | solution.py:28
  66.3 0.5 collective-permute-start.17
  66.7 2.4 %collective-permute-start.16 = (bf16[24,3584]{1,0:T(8,128)(2,1)S(1)}, bf16[24,3584]{1,0:T(8,128)(2,1)S(1)}, u32[]{:S(2)}, u32[]{:S(2)}) collective-permute-start(bf16[24,3584]{1,0:T(8,128)(2,1)S(1)} %get-tuple-element.43), channel_id=1, source_target_pairs={{0,32},{1,225},{2,34},{3,227},{4,36},{5,229},{6,38},{7,231},{8,40}... | collective-permute-start | bytes 516104 | tf_op jit(solution)/shard_map/ppermute | solution.py:28
  69.1 2.2 %collective-permute-done.24 = bf16[24,3584]{1,0:T(8,128)(2,1)S(1)} collective-permute-done((bf16[24,3584]{1,0:T(8,128)(2,1)S(1)}, bf16[24,3584]{1,0:T(8,128)(2,1)S(1)}, u32[]{:S(2)}, u32[]{:S(2)}) %collective-permute-start.24) | collective-permute-done | bytes 172064 | tf_op jit(solution)/shard_map/ppermute | solution.py:28
  71.4 0.6 collective-permute-done.23
  71.9 0.1 fusion.8
  72.0 2.1 %collective-permute-start.25 = (bf16[24,3584]{1,0:T(8,128)(2,1)S(1)}, bf16[24,3584]{1,0:T(8,128)(2,1)S(1)}, u32[]{:S(2)}, u32[]{:S(2)}) collective-permute-start(bf16[24,3584]{1,0:T(8,128)(2,1)S(1)} %get-tuple-element.28), channel_id=1, source_target_pairs={{0,32},{1,225},{2,34},{3,227},{4,36},{5,229},{6,38},{7,231},{8,40}... | collective-permute-start | bytes 516104 | tf_op jit(solution)/shard_map/ppermute | solution.py:28
  74.1 0.9 collective-permute-done.17
  75.0 0.1 fusion.15
  75.1 2.4 %collective-permute-start.18 = (bf16[24,3584]{1,0:T(8,128)(2,1)S(1)}, bf16[24,3584]{1,0:T(8,128)(2,1)S(1)}, u32[]{:S(2)}, u32[]{:S(2)}) collective-permute-start(bf16[24,3584]{1,0:T(8,128)(2,1)S(1)} %get-tuple-element.22), channel_id=1, source_target_pairs={{0,32},{1,225},{2,34},{3,227},{4,36},{5,229},{6,38},{7,231},{8,40}... | collective-permute-start | bytes 516104 | tf_op jit(solution)/shard_map/ppermute | solution.py:28
  77.6 0.8 collective-permute-done.25
  78.3 3.8 %collective-permute-done.26 = bf16[24,3584]{1,0:T(8,128)(2,1)S(1)} collective-permute-done((bf16[24,3584]{1,0:T(8,128)(2,1)S(1)}, bf16[24,3584]{1,0:T(8,128)(2,1)S(1)}, u32[]{:S(2)}, u32[]{:S(2)}) %collective-permute-start.26) | collective-permute-done | bytes 172064 | tf_op jit(solution)/shard_map/ppermute | solution.py:28
  82.2 0.1 fusion.6
  82.2 3.2 %collective-permute-start.27 = (bf16[24,3584]{1,0:T(8,128)(2,1)S(1)}, bf16[24,3584]{1,0:T(8,128)(2,1)S(1)}, u32[]{:S(2)}, u32[]{:S(2)}) collective-permute-start(bf16[24,3584]{1,0:T(8,128)(2,1)S(1)} %get-tuple-element.30), channel_id=1, source_target_pairs={{0,32},{1,225},{2,34},{3,227},{4,36},{5,229},{6,38},{7,231},{8,40}... | collective-permute-start | bytes 516104 | tf_op jit(solution)/shard_map/ppermute | solution.py:28
  85.5 0.2 collective-permute-done.19
  85.6 0.1 fusion.13
  85.7 3.0 %collective-permute-start.20 = (bf16[24,3584]{1,0:T(8,128)(2,1)S(1)}, bf16[24,3584]{1,0:T(8,128)(2,1)S(1)}, u32[]{:S(2)}, u32[]{:S(2)}) collective-permute-start(bf16[24,3584]{1,0:T(8,128)(2,1)S(1)} %get-tuple-element.24), channel_id=1, source_target_pairs={{0,32},{1,225},{2,34},{3,227},{4,36},{5,229},{6,38},{7,231},{8,40}... | collective-permute-start | bytes 516104 | tf_op jit(solution)/shard_map/ppermute | solution.py:28
  88.8 2.2 %collective-permute-start.28 = (bf16[24,3584]{1,0:T(8,128)(2,1)S(1)}, bf16[24,3584]{1,0:T(8,128)(2,1)S(1)}, u32[]{:S(2)}, u32[]{:S(2)}) collective-permute-start(bf16[24,3584]{1,0:T(8,128)(2,1)S(1)} %fusion.5), channel_id=1, source_target_pairs={{0,32},{1,225},{2,34},{3,227},{4,36},{5,229},{6,38},{7,231},{8,40}... | collective-permute-start | bytes 516104 | tf_op jit(solution)/shard_map/ppermute | solution.py:28
  91.0 1.9 %collective-permute-done.20 = bf16[24,3584]{1,0:T(8,128)(2,1)S(1)} collective-permute-done((bf16[24,3584]{1,0:T(8,128)(2,1)S(1)}, bf16[24,3584]{1,0:T(8,128)(2,1)S(1)}, u32[]{:S(2)}, u32[]{:S(2)}) %collective-permute-start.20) | collective-permute-done | bytes 172064 | tf_op jit(solution)/shard_map/ppermute | solution.py:28
  92.9 2.8 %collective-permute-start.21 = (bf16[24,3584]{1,0:T(8,128)(2,1)S(1)}, bf16[24,3584]{1,0:T(8,128)(2,1)S(1)}, u32[]{:S(2)}, u32[]{:S(2)}) collective-permute-start(bf16[24,3584]{1,0:T(8,128)(2,1)S(1)} %fusion.12), channel_id=1, source_target_pairs={{0,32},{1,225},{2,34},{3,227},{4,36},{5,229},{6,38},{7,231},{8,40}... | collective-permute-start | bytes 516104 | tf_op jit(solution)/shard_map/ppermute | solution.py:28
  95.7 0.3 collective-permute-done.28
  96.0 0.4 collective-permute-done.29
  96.4 0.1 fusion.11
  96.5 2.2 %collective-permute-done.21 = bf16[24,3584]{1,0:T(8,128)(2,1)S(1)} collective-permute-done((bf16[24,3584]{1,0:T(8,128)(2,1)S(1)}, bf16[24,3584]{1,0:T(8,128)(2,1)S(1)}, u32[]{:S(2)}, u32[]{:S(2)}) %collective-permute-start.21) | collective-permute-done | bytes 172064 | tf_op jit(solution)/shard_map/ppermute | solution.py:28
  98.6 2.5 %collective-permute-done.22 = bf16[24,3584]{1,0:T(8,128)(2,1)S(1)} collective-permute-done((bf16[24,3584]{1,0:T(8,128)(2,1)S(1)}, bf16[24,3584]{1,0:T(8,128)(2,1)S(1)}, u32[]{:S(2)}, u32[]{:S(2)}) %collective-permute-start.22) | collective-permute-done | bytes 172064 | tf_op jit(solution)/shard_map/ppermute | solution.py:28
  101.2 0.4 fusion.19
  101.6 0.4 convolution_add_fusion
  102.1 0.1 collective-permute-start.30
  102.2 1.8 %collective-permute-done.30 = bf16[32,7168]{1,0:T(8,128)(2,1)S(1)} collective-permute-done((bf16[32,7168]{1,0:T(8,128)(2,1)S(1)}, bf16[32,7168]{1,0:T(8,128)(2,1)S(1)}, u32[]{:S(2)}, u32[]{:S(2)}) %collective-permute-start.30) | collective-permute-done | bytes 458784 | tf_op jit(solution)/shard_map/ppermute | solution.py:19
  104.0 0.1 fusion
  104.1 0.9 reshape.16
  105.0 3.6 %all-to-all-start.1 = ((bf16[16,2,7168]{2,1,0:T(2,128)(2,1)}), bf16[16,2,7168]{2,1,0:T(2,128)(2,1)S(1)}, u32[]{:S(2)}, u32[]{:S(2)}) async-start(bf16[16,2,7168]{2,1,0:T(2,128)(2,1)} %reshape.16), calls=%async_computation.1 | async-start | bytes 917504 | tf_op jit(solution)/shard_map/all_to_all | solution.py:249
  108.6 0.5 fusion.30
  109.1 10.8 %all-to-all-done.1 = bf16[16,2,7168]{2,1,0:T(2,128)(2,1)S(1)} async-done(((bf16[16,2,7168]{2,1,0:T(2,128)(2,1)}), bf16[16,2,7168]{2,1,0:T(2,128)(2,1)S(1)}, u32[]{:S(2)}, u32[]{:S(2)}) %all-to-all-start.1) | async-done | bytes 458784 | tf_op jit(solution)/shard_map/all_to_all | solution.py:249
  120.0 1.0 reduce_sum.23
  (52 shorter events, 0.8 us)
Async XLA Ops:
  20.5 1.9 %collective-permute-start = (bf16[32,7296]{1,0:T(8,128)(2,1)S(1)}, bf16[32,7296]{1,0:T(8,128)(2,1)S(1)}, u32[]{:S(2)}, u32[]{:S(2)}) collective-permute-start(bf16[32,7296]{1,0:T(8,128)(2,1)S(1)} %reshape.15.near), channel_id=1, source_target_pairs={{0,1},{1,0},{2,3},{3,2},{4,5},{5,4},{6,7},{7,6},{8,9},{9,8},{10,11... | collective-permute-start | bytes 1400840 | tf_op jit(solution)/shard_map/ppermute | solution.py:19
  23.4 6.3 %collective-permute-start.1 = (bf16[48,2432]{1,0:T(8,128)(2,1)S(1)}, bf16[48,2432]{1,0:T(8,128)(2,1)S(1)}, u32[]{:S(2)}, u32[]{:S(2)}) collective-permute-start(bf16[48,2432]{1,0:T(8,128)(2,1)S(1)} %get-tuple-element.19), channel_id=1, source_target_pairs={{0,32},{1,225},{2,34},{3,227},{4,36},{5,229},{6,38},{7,231},{8,40}... | collective-permute-start | bytes 700424 | tf_op jit(solution)/shard_map/ppermute | solution.py:28
  25.4 6.7 %collective-permute-start.6 = (bf16[48,2432]{1,0:T(8,128)(2,1)S(1)}, bf16[48,2432]{1,0:T(8,128)(2,1)S(1)}, u32[]{:S(2)}, u32[]{:S(2)}) collective-permute-start(bf16[48,2432]{1,0:T(8,128)(2,1)S(1)} %get-tuple-element.20), channel_id=1, source_target_pairs={{0,32},{1,225},{2,34},{3,227},{4,36},{5,229},{6,38},{7,231},{8,40}... | collective-permute-start | bytes 700424 | tf_op jit(solution)/shard_map/ppermute | solution.py:28
  28.5 7.3 %collective-permute-start.11 = (bf16[48,2432]{1,0:T(8,128)(2,1)S(1)}, bf16[48,2432]{1,0:T(8,128)(2,1)S(1)}, u32[]{:S(2)}, u32[]{:S(2)}) collective-permute-start(bf16[48,2432]{1,0:T(8,128)(2,1)S(1)} %get-tuple-element.21), channel_id=1, source_target_pairs={{0,32},{1,225},{2,34},{3,227},{4,36},{5,229},{6,38},{7,231},{8,40}... | collective-permute-start | bytes 700424 | tf_op jit(solution)/shard_map/ppermute | solution.py:28
  29.6 8.7 %collective-permute-start.2 = (bf16[48,2432]{1,0:T(8,128)(2,1)S(1)}, bf16[48,2432]{1,0:T(8,128)(2,1)S(1)}, u32[]{:S(2)}, u32[]{:S(2)}) collective-permute-start(bf16[48,2432]{1,0:T(8,128)(2,1)S(1)} %collective-permute-done.1), channel_id=1, source_target_pairs={{0,32},{1,225},{2,34},{3,227},{4,36},{5,229},{6,38},{7,231},{8,40}... | collective-permute-start | bytes 700424 | tf_op jit(solution)/shard_map/ppermute | solution.py:28
  32.1 8.9 %collective-permute-start.7 = (bf16[48,2432]{1,0:T(8,128)(2,1)S(1)}, bf16[48,2432]{1,0:T(8,128)(2,1)S(1)}, u32[]{:S(2)}, u32[]{:S(2)}) collective-permute-start(bf16[48,2432]{1,0:T(8,128)(2,1)S(1)} %collective-permute-done.6), channel_id=1, source_target_pairs={{0,32},{1,225},{2,34},{3,227},{4,36},{5,229},{6,38},{7,231},{8,40}... | collective-permute-start | bytes 700424 | tf_op jit(solution)/shard_map/ppermute | solution.py:28
  35.8 7.5 %collective-permute-start.12 = (bf16[48,2432]{1,0:T(8,128)(2,1)S(1)}, bf16[48,2432]{1,0:T(8,128)(2,1)S(1)}, u32[]{:S(2)}, u32[]{:S(2)}) collective-permute-start(bf16[48,2432]{1,0:T(8,128)(2,1)S(1)} %collective-permute-done.11), channel_id=1, source_target_pairs={{0,32},{1,225},{2,34},{3,227},{4,36},{5,229},{6,38},{7,231},{8,40}... | collective-permute-start | bytes 700424 | tf_op jit(solution)/shard_map/ppermute | solution.py:28
  38.4 13.9 %collective-permute-start.3 = (bf16[48,2432]{1,0:T(8,128)(2,1)S(1)}, bf16[48,2432]{1,0:T(8,128)(2,1)S(1)}, u32[]{:S(2)}, u32[]{:S(2)}) collective-permute-start(bf16[48,2432]{1,0:T(8,128)(2,1)S(1)} %collective-permute-done.2), channel_id=1, source_target_pairs={{0,32},{1,225},{2,34},{3,227},{4,36},{5,229},{6,38},{7,231},{8,40}... | collective-permute-start | bytes 700424 | tf_op jit(solution)/shard_map/ppermute | solution.py:28
  41.0 15.3 %collective-permute-start.8 = (bf16[48,2432]{1,0:T(8,128)(2,1)S(1)}, bf16[48,2432]{1,0:T(8,128)(2,1)S(1)}, u32[]{:S(2)}, u32[]{:S(2)}) collective-permute-start(bf16[48,2432]{1,0:T(8,128)(2,1)S(1)} %collective-permute-done.7), channel_id=1, source_target_pairs={{0,32},{1,225},{2,34},{3,227},{4,36},{5,229},{6,38},{7,231},{8,40}... | collective-permute-start | bytes 700424 | tf_op jit(solution)/shard_map/ppermute | solution.py:28
  43.3 6.4 %collective-permute-start.13 = (bf16[48,2432]{1,0:T(8,128)(2,1)S(1)}, bf16[48,2432]{1,0:T(8,128)(2,1)S(1)}, u32[]{:S(2)}, u32[]{:S(2)}) collective-permute-start(bf16[48,2432]{1,0:T(8,128)(2,1)S(1)} %collective-permute-done.12), channel_id=1, source_target_pairs={{0,32},{1,225},{2,34},{3,227},{4,36},{5,229},{6,38},{7,231},{8,40}... | collective-permute-start | bytes 700424 | tf_op jit(solution)/shard_map/ppermute | solution.py:28
  49.7 7.4 %collective-permute-start.14 = (bf16[24,2432]{1,0:T(8,128)(2,1)S(1)}, bf16[24,2432]{1,0:T(8,128)(2,1)S(1)}, u32[]{:S(2)}, u32[]{:S(2)}) collective-permute-start(bf16[24,2432]{1,0:T(8,128)(2,1)S(1)} %get-tuple-element.47), channel_id=1, source_target_pairs={{0,32},{1,225},{2,34},{3,227},{4,36},{5,229},{6,38},{7,231},{8,40}... | collective-permute-start | bytes 350216 | tf_op jit(solution)/shard_map/ppermute | solution.py:28
  52.2 9.2 %collective-permute-start.15 = (bf16[72,2432]{1,0:T(8,128)(2,1)S(1)}, bf16[72,2432]{1,0:T(8,128)(2,1)S(1)}, u32[]{:S(2)}, u32[]{:S(2)}) collective-permute-start(bf16[72,2432]{1,0:T(8,128)(2,1)S(1)} %pad_maximum_fusion.2), channel_id=1, source_target_pairs={{0,1},{1,0},{2,3},{3,2},{4,5},{5,4},{6,7},{7,6},{8,9},{9,8},{10,11... | collective-permute-start | bytes 1050632 | tf_op jit(solution)/shard_map/ppermute | solution.py:19
  52.4 6.2 %collective-permute-start.4 = (bf16[24,2432]{1,0:T(8,128)(2,1)S(1)}, bf16[24,2432]{1,0:T(8,128)(2,1)S(1)}, u32[]{:S(2)}, u32[]{:S(2)}) collective-permute-start(bf16[24,2432]{1,0:T(8,128)(2,1)S(1)} %get-tuple-element.61), channel_id=1, source_target_pairs={{0,32},{1,225},{2,34},{3,227},{4,36},{5,229},{6,38},{7,231},{8,40}... | collective-permute-start | bytes 350216 | tf_op jit(solution)/shard_map/ppermute | solution.py:28
  56.2 5.3 %collective-permute-start.5 = (bf16[72,2432]{1,0:T(8,128)(2,1)S(1)}, bf16[72,2432]{1,0:T(8,128)(2,1)S(1)}, u32[]{:S(2)}, u32[]{:S(2)}) collective-permute-start(bf16[72,2432]{1,0:T(8,128)(2,1)S(1)} %pad_maximum_fusion), channel_id=1, source_target_pairs={{0,1},{1,0},{2,3},{3,2},{4,5},{5,4},{6,7},{7,6},{8,9},{9,8},{10,11... | collective-permute-start | bytes 1050632 | tf_op jit(solution)/shard_map/ppermute | solution.py:19
  56.3 5.2 %copy-start = (bf16[1,2,7168,128]{3,2,1,0:T(8,128)(2,1)S(1)}, bf16[1,2,7168,128]{3,2,1,0:T(8,128)(2,1)}, u32[]{:S(2)}) copy-start(bf16[1,2,7168,128]{3,2,1,0:T(8,128)(2,1)} %w.1) | copy-start | bytes 11010052
  56.3 5.1 %collective-permute-start.9 = (bf16[24,2432]{1,0:T(8,128)(2,1)S(1)}, bf16[24,2432]{1,0:T(8,128)(2,1)S(1)}, u32[]{:S(2)}, u32[]{:S(2)}) collective-permute-start(bf16[24,2432]{1,0:T(8,128)(2,1)S(1)} %get-tuple-element.54), channel_id=1, source_target_pairs={{0,32},{1,225},{2,34},{3,227},{4,36},{5,229},{6,38},{7,231},{8,40}... | collective-permute-start | bytes 350216 | tf_op jit(solution)/shard_map/ppermute | solution.py:28
  57.1 4.4 %collective-permute-start.10 = (bf16[72,2432]{1,0:T(8,128)(2,1)S(1)}, bf16[72,2432]{1,0:T(8,128)(2,1)S(1)}, u32[]{:S(2)}, u32[]{:S(2)}) collective-permute-start(bf16[72,2432]{1,0:T(8,128)(2,1)S(1)} %pad_maximum_fusion.1), channel_id=1, source_target_pairs={{0,1},{1,0},{2,3},{3,2},{4,5},{5,4},{6,7},{7,6},{8,9},{9,8},{10,11... | collective-permute-start | bytes 1050632 | tf_op jit(solution)/shard_map/ppermute | solution.py:19
  61.6 1.5 %copy-start.1 = (bf16[1,128,7168]{2,1,0:T(8,128)(2,1)S(1)}, bf16[1,128,7168]{2,1,0:T(8,128)(2,1)}, u32[]{:S(2)}) copy-start(bf16[1,128,7168]{2,1,0:T(8,128)(2,1)} %param.13) | copy-start | bytes 5505028
  64.1 7.2 %collective-permute-start.24 = (bf16[24,3584]{1,0:T(8,128)(2,1)S(1)}, bf16[24,3584]{1,0:T(8,128)(2,1)S(1)}, u32[]{:S(2)}, u32[]{:S(2)}) collective-permute-start(bf16[24,3584]{1,0:T(8,128)(2,1)S(1)} %get-tuple-element.44), channel_id=1, source_target_pairs={{0,224},{1,33},{2,226},{3,35},{4,228},{5,37},{6,230},{7,39},{8,232... | collective-permute-start | bytes 516104 | tf_op jit(solution)/shard_map/ppermute | solution.py:28
  64.2 7.7 %collective-permute-start.23 = (bf16[24,3584]{1,0:T(8,128)(2,1)S(1)}, bf16[24,3584]{1,0:T(8,128)(2,1)S(1)}, u32[]{:S(2)}, u32[]{:S(2)}) collective-permute-start(bf16[24,3584]{1,0:T(8,128)(2,1)S(1)} %get-tuple-element.45), channel_id=1, source_target_pairs={{0,32},{1,225},{2,34},{3,227},{4,36},{5,229},{6,38},{7,231},{8,40}... | collective-permute-start | bytes 516104 | tf_op jit(solution)/shard_map/ppermute | solution.py:28
  66.3 8.8 %collective-permute-start.17 = (bf16[24,3584]{1,0:T(8,128)(2,1)S(1)}, bf16[24,3584]{1,0:T(8,128)(2,1)S(1)}, u32[]{:S(2)}, u32[]{:S(2)}) collective-permute-start(bf16[24,3584]{1,0:T(8,128)(2,1)S(1)} %get-tuple-element.42), channel_id=1, source_target_pairs={{0,224},{1,33},{2,226},{3,35},{4,228},{5,37},{6,230},{7,39},{8,232... | collective-permute-start | bytes 516104 | tf_op jit(solution)/shard_map/ppermute | solution.py:28
  66.7 8.3 %collective-permute-start.16 = (bf16[24,3584]{1,0:T(8,128)(2,1)S(1)}, bf16[24,3584]{1,0:T(8,128)(2,1)S(1)}, u32[]{:S(2)}, u32[]{:S(2)}) collective-permute-start(bf16[24,3584]{1,0:T(8,128)(2,1)S(1)} %get-tuple-element.43), channel_id=1, source_target_pairs={{0,32},{1,225},{2,34},{3,227},{4,36},{5,229},{6,38},{7,231},{8,40}... | collective-permute-start | bytes 516104 | tf_op jit(solution)/shard_map/ppermute | solution.py:28
  72.0 6.3 %collective-permute-start.25 = (bf16[24,3584]{1,0:T(8,128)(2,1)S(1)}, bf16[24,3584]{1,0:T(8,128)(2,1)S(1)}, u32[]{:S(2)}, u32[]{:S(2)}) collective-permute-start(bf16[24,3584]{1,0:T(8,128)(2,1)S(1)} %get-tuple-element.28), channel_id=1, source_target_pairs={{0,32},{1,225},{2,34},{3,227},{4,36},{5,229},{6,38},{7,231},{8,40}... | collective-permute-start | bytes 516104 | tf_op jit(solution)/shard_map/ppermute | solution.py:28
  74.1 8.0 %collective-permute-start.26 = (bf16[24,3584]{1,0:T(8,128)(2,1)S(1)}, bf16[24,3584]{1,0:T(8,128)(2,1)S(1)}, u32[]{:S(2)}, u32[]{:S(2)}) collective-permute-start(bf16[24,3584]{1,0:T(8,128)(2,1)S(1)} %get-tuple-element.29), channel_id=1, source_target_pairs={{0,224},{1,33},{2,226},{3,35},{4,228},{5,37},{6,230},{7,39},{8,232... | collective-permute-start | bytes 516104 | tf_op jit(solution)/shard_map/ppermute | solution.py:28
  75.1 10.3 %collective-permute-start.18 = (bf16[24,3584]{1,0:T(8,128)(2,1)S(1)}, bf16[24,3584]{1,0:T(8,128)(2,1)S(1)}, u32[]{:S(2)}, u32[]{:S(2)}) collective-permute-start(bf16[24,3584]{1,0:T(8,128)(2,1)S(1)} %get-tuple-element.22), channel_id=1, source_target_pairs={{0,32},{1,225},{2,34},{3,227},{4,36},{5,229},{6,38},{7,231},{8,40}... | collective-permute-start | bytes 516104 | tf_op jit(solution)/shard_map/ppermute | solution.py:28
  77.6 8.1 %collective-permute-start.19 = (bf16[24,3584]{1,0:T(8,128)(2,1)S(1)}, bf16[24,3584]{1,0:T(8,128)(2,1)S(1)}, u32[]{:S(2)}, u32[]{:S(2)}) collective-permute-start(bf16[24,3584]{1,0:T(8,128)(2,1)S(1)} %get-tuple-element.23), channel_id=1, source_target_pairs={{0,224},{1,33},{2,226},{3,35},{4,228},{5,37},{6,230},{7,39},{8,232... | collective-permute-start | bytes 516104 | tf_op jit(solution)/shard_map/ppermute | solution.py:28
  82.2 6.5 %collective-permute-start.27 = (bf16[24,3584]{1,0:T(8,128)(2,1)S(1)}, bf16[24,3584]{1,0:T(8,128)(2,1)S(1)}, u32[]{:S(2)}, u32[]{:S(2)}) collective-permute-start(bf16[24,3584]{1,0:T(8,128)(2,1)S(1)} %get-tuple-element.30), channel_id=1, source_target_pairs={{0,32},{1,225},{2,34},{3,227},{4,36},{5,229},{6,38},{7,231},{8,40}... | collective-permute-start | bytes 516104 | tf_op jit(solution)/shard_map/ppermute | solution.py:28
  85.7 7.2 %collective-permute-start.20 = (bf16[24,3584]{1,0:T(8,128)(2,1)S(1)}, bf16[24,3584]{1,0:T(8,128)(2,1)S(1)}, u32[]{:S(2)}, u32[]{:S(2)}) collective-permute-start(bf16[24,3584]{1,0:T(8,128)(2,1)S(1)} %get-tuple-element.24), channel_id=1, source_target_pairs={{0,32},{1,225},{2,34},{3,227},{4,36},{5,229},{6,38},{7,231},{8,40}... | collective-permute-start | bytes 516104 | tf_op jit(solution)/shard_map/ppermute | solution.py:28
  88.8 7.2 %collective-permute-start.28 = (bf16[24,3584]{1,0:T(8,128)(2,1)S(1)}, bf16[24,3584]{1,0:T(8,128)(2,1)S(1)}, u32[]{:S(2)}, u32[]{:S(2)}) collective-permute-start(bf16[24,3584]{1,0:T(8,128)(2,1)S(1)} %fusion.5), channel_id=1, source_target_pairs={{0,32},{1,225},{2,34},{3,227},{4,36},{5,229},{6,38},{7,231},{8,40}... | collective-permute-start | bytes 516104 | tf_op jit(solution)/shard_map/ppermute | solution.py:28
  91.0 5.4 %collective-permute-start.29 = (bf16[24,3584]{1,0:T(8,128)(2,1)S(1)}, bf16[24,3584]{1,0:T(8,128)(2,1)S(1)}, u32[]{:S(2)}, u32[]{:S(2)}) collective-permute-start(bf16[24,3584]{1,0:T(8,128)(2,1)S(1)} %get-tuple-element.33), channel_id=1, source_target_pairs={{0,224},{1,33},{2,226},{3,35},{4,228},{5,37},{6,230},{7,39},{8,232... | collective-permute-start | bytes 516104 | tf_op jit(solution)/shard_map/ppermute | solution.py:28
  92.9 5.7 %collective-permute-start.21 = (bf16[24,3584]{1,0:T(8,128)(2,1)S(1)}, bf16[24,3584]{1,0:T(8,128)(2,1)S(1)}, u32[]{:S(2)}, u32[]{:S(2)}) collective-permute-start(bf16[24,3584]{1,0:T(8,128)(2,1)S(1)} %fusion.12), channel_id=1, source_target_pairs={{0,32},{1,225},{2,34},{3,227},{4,36},{5,229},{6,38},{7,231},{8,40}... | collective-permute-start | bytes 516104 | tf_op jit(solution)/shard_map/ppermute | solution.py:28
  95.7 5.4 %collective-permute-start.22 = (bf16[24,3584]{1,0:T(8,128)(2,1)S(1)}, bf16[24,3584]{1,0:T(8,128)(2,1)S(1)}, u32[]{:S(2)}, u32[]{:S(2)}) collective-permute-start(bf16[24,3584]{1,0:T(8,128)(2,1)S(1)} %get-tuple-element.27), channel_id=1, source_target_pairs={{0,224},{1,33},{2,226},{3,35},{4,228},{5,37},{6,230},{7,39},{8,232... | collective-permute-start | bytes 516104 | tf_op jit(solution)/shard_map/ppermute | solution.py:28
  102.1 1.9 %collective-permute-start.30 = (bf16[32,7168]{1,0:T(8,128)(2,1)S(1)}, bf16[32,7168]{1,0:T(8,128)(2,1)S(1)}, u32[]{:S(2)}, u32[]{:S(2)}) collective-permute-start(bf16[32,7168]{1,0:T(8,128)(2,1)S(1)} %slice.373), channel_id=1, source_target_pairs={{0,1},{1,0},{2,3},{3,2},{4,5},{5,4},{6,7},{7,6},{8,9},{9,8},{10,11... | collective-permute-start | bytes 1376264 | tf_op jit(solution)/shard_map/ppermute | solution.py:19
  105.0 14.9 %all-to-all-start.1 = ((bf16[16,2,7168]{2,1,0:T(2,128)(2,1)}), bf16[16,2,7168]{2,1,0:T(2,128)(2,1)S(1)}, u32[]{:S(2)}, u32[]{:S(2)}) async-start(bf16[16,2,7168]{2,1,0:T(2,128)(2,1)} %reshape.16), calls=%async_computation.1 | async-start | bytes 917504 | tf_op jit(solution)/shard_map/all_to_all | solution.py:249
